TPU v7x, 512 devices: a whole 4x8x8 slice. The times are simulated.
512 devices in a mesh: head: 8 (over x, y_lo), ctx: 64 (over y_hi, z, core).
Axes of the slice: x: 4, y: 8 (y_hi: 4, y_lo: 2; y = y_hi * 2 + y_lo), z: 8, core: 2. Of those that a mesh axis runs over, the one named last changes fastest.
Arguments:
- queries: bfloat16 [8192, 1024], P(('head', 'ctx')), may hold values from -30 to 30
- key_vecs: bfloat16 [8192, 128], P(('head', 'ctx')), may hold values from -10 to 10
- value_vecs: bfloat16 [8192, 128], P(('head', 'ctx')), may hold values from -6 to 6
- out_grad: bfloat16 [8192, 1024], P(('head', 'ctx')), may hold values from -6 to 6
- positions: int32 [8192], P(('head', 'ctx')), may hold values from 0 to 8191, as said below
- documents: int32 [8192], P(('head', 'ctx')), may hold values from 0 to 8, as said below
Outputs:
- grad_queries: float32 [8192, 1024], P(('head', 'ctx'))
- grad_keys: float32 [8192, 128], P(('head', 'ctx'))
- grad_values: float32 [8192, 128], P(('head', 'ctx'))
Inputs may be any that keep to these rules, and one draw needn't show every extreme that they name: positions is a permutation of 0 to 8191; each aligned run of 16 rows holds 16 consecutive positions in rising order. `documents`: document ids never fall as positions rise, the token at position 0 has id 0, and every id up to the most occurs.
All inputs are finite; a program needn't handle non-finite values.
Results may differ from a plain program's by a relative error of at most 0.0059.
Values may be sent and summed in bfloat16 or wider, within the bound.
No kernel may reach another device: no remote copies, remote signals or barrier semaphores. Data moves between devices by JAX's collectives and lax.ppermute only.
A program may use at most 64 MiB of HBM per device.

v0:
```python
import math

import jax
import jax.numpy as jnp
from jax import lax
from jax.sharding import PartitionSpec as P

NEG_BIG = -1e30


def from_behind(block, axis, distance):
    devices = range(lax.axis_size(axis))
    route = [((i - distance) % len(devices), i) for i in devices]
    return lax.ppermute(block, axis, route)


def block_visible(pos_query, doc_query, pos_key, doc_key):
    return (pos_key[None, :] <= pos_query[:, None]) & (doc_key[None, :] == doc_query[:, None])


def masked_scores(query_cube, key_rows, visible):
    inv_root = 1.0 / math.sqrt(query_cube.shape[-1])
    raw_scores = (
        jnp.einsum("thd,kd->thk", query_cube, key_rows, preferred_element_type=jnp.float32)
        * inv_root
    )
    return jnp.where(visible[:, None, :], raw_scores, NEG_BIG)


def stats_update(running, query_cube, grad_cube, key_rows, value_rows, visible):
    highest, denoms, cross_sum = running
    scores = masked_scores(query_cube, key_rows, visible)
    dprobs = jnp.einsum("thd,kd->thk", grad_cube, value_rows, preferred_element_type=jnp.float32)
    new_high = jnp.maximum(highest, jnp.max(scores, axis=2))
    weights = jnp.where(visible[:, None, :], jnp.exp(scores - new_high[:, :, None]), 0.0)
    return (new_high, jnp.sum(weights, axis=2), jnp.sum(weights * dprobs, axis=2))


def block_grads(query_cube, grad_cube, log_total, row_dot, key_rows, value_rows, visible):
    scores = masked_scores(query_cube, key_rows, visible)
    weights = jnp.where(visible[:, None, :], jnp.exp(scores - log_total[:, :, None]), 0.0)
    dprobs = jnp.einsum("thd,kd->thk", grad_cube, value_rows, preferred_element_type=jnp.float32)
    dscores = (weights * (dprobs - row_dot[:, :, None])).astype(jnp.bfloat16)
    return (weights.astype(jnp.bfloat16), dscores)


def query_part(dscores, key_rows):
    inv_root = 1.0 / math.sqrt(key_rows.shape[-1])
    return (
        jnp.einsum("thk,kd->thd", dscores, key_rows, preferred_element_type=jnp.float32) * inv_root
    )


def key_part(weights_b, dscores, query_cube, grad_cube):
    inv_root = 1.0 / math.sqrt(query_cube.shape[-1])
    key_grad = (
        jnp.einsum("thk,thd->kd", dscores, query_cube, preferred_element_type=jnp.float32)
        * inv_root
    )
    value_grad = jnp.einsum("thk,thd->kd", weights_b, grad_cube, preferred_element_type=jnp.float32)
    return jnp.concatenate([key_grad, value_grad], axis=1)


def on_device(queries, key_vecs, value_vecs, out_grad, positions, documents):
    head_count = lax.axis_size("head")
    ctx_count = lax.axis_size("ctx")
    ctx_here = lax.axis_index("ctx")
    head_dim = key_vecs.shape[1]
    query_tok, grad_tok = (
        lax.all_to_all(queries, "head", split_axis=1, concat_axis=0, tiled=True),
        lax.all_to_all(out_grad, "head", split_axis=1, concat_axis=0, tiled=True),
    )
    tok_rows = query_tok.shape[0]
    local_heads = query_tok.shape[1] // head_dim
    query_cube = query_tok.reshape(tok_rows, local_heads, head_dim)
    grad_cube = grad_tok.reshape(tok_rows, local_heads, head_dim)
    pos_all, doc_all = (
        lax.all_gather(positions, ("head", "ctx"), axis=0, tiled=True),
        lax.all_gather(documents, ("head", "ctx"), axis=0, tiled=True),
    )
    seq_len = pos_all.shape[0]
    shard_rows = seq_len // (head_count * ctx_count)
    pos_grid = pos_all.reshape(head_count, ctx_count, shard_rows)
    doc_grid = doc_all.reshape(head_count, ctx_count, shard_rows)
    pos_seq = jnp.transpose(pos_grid, (1, 0, 2)).reshape(seq_len)
    doc_seq = jnp.transpose(doc_grid, (1, 0, 2)).reshape(seq_len)

    def ctx_block(table, block_index):
        return lax.dynamic_index_in_dim(table, block_index, 1, keepdims=False).reshape(tok_rows)

    pos_own = ctx_block(pos_grid, ctx_here)
    doc_own = ctx_block(doc_grid, ctx_here)
    stat_zero = jnp.zeros((tok_rows, local_heads), jnp.float32)
    start_stats = (jnp.full((tok_rows, local_heads), NEG_BIG, jnp.float32), stat_zero, stat_zero)
    key_own, value_own = (
        lax.all_gather(key_vecs, "head", axis=0, tiled=True),
        lax.all_gather(value_vecs, "head", axis=0, tiled=True),
    )
    grad_zero = jnp.zeros((tok_rows, local_heads, head_dim), jnp.float32)
    pair_zero = jnp.zeros((tok_rows, 2 * head_dim), jnp.float32)
    key_rows = lax.all_gather(key_own, "ctx", axis=0, tiled=True)
    value_rows = lax.all_gather(value_own, "ctx", axis=0, tiled=True)
    visible = block_visible(pos_own, doc_own, pos_seq, doc_seq)
    highest, denoms, cross_sum = stats_update(
        start_stats, query_cube, grad_cube, key_rows, value_rows, visible
    )
    log_total = highest + jnp.log(denoms)
    row_dot = cross_sum / denoms

    def visit(step_no, state):
        query_blk, grad_blk, log_blk, dot_blk, qgrad_blk, key_grads = state
        block_index = (ctx_here - step_no) % ctx_count
        visible = block_visible(
            ctx_block(pos_grid, block_index), ctx_block(doc_grid, block_index), pos_own, doc_own
        )
        weights_b, dscores = block_grads(
            query_blk, grad_blk, log_blk, dot_blk, key_own, value_own, visible
        )
        qgrad_blk, key_grads = (
            qgrad_blk + query_part(dscores, key_own),
            key_grads + key_part(weights_b, dscores, query_blk, grad_blk),
        )
        return (query_blk, grad_blk, log_blk, dot_blk, qgrad_blk, key_grads)

    def advance(step_no, state):
        query_blk, grad_blk, log_blk, dot_blk, qgrad_blk, key_grads = visit(step_no, state)
        query_blk, grad_blk = from_behind((query_blk, grad_blk), "ctx", 1)
        log_blk, dot_blk, qgrad_blk = from_behind((log_blk, dot_blk, qgrad_blk), "ctx", 1)
        return (query_blk, grad_blk, log_blk, dot_blk, qgrad_blk, key_grads)

    state = (query_cube, grad_cube, log_total, row_dot, grad_zero, pair_zero)
    state = lax.fori_loop(0, ctx_count - 1, advance, state)
    state = visit(ctx_count - 1, state)
    grad_home = from_behind(state[4], "ctx", 1)
    key_grads = state[5]
    summed = lax.psum_scatter(key_grads, "head", scatter_dimension=0, tiled=True)
    grad_queries = lax.all_to_all(
        grad_home.reshape(tok_rows, local_heads * head_dim),
        "head",
        split_axis=0,
        concat_axis=1,
        tiled=True,
    )
    return (grad_queries, summed[:, :head_dim], summed[:, head_dim:])


def solution(mesh):
    placed = (
        P(("head", "ctx"), None),
        P(("head", "ctx"), None),
        P(("head", "ctx"), None),
        P(("head", "ctx"), None),
        P(("head", "ctx")),
        P(("head", "ctx")),
    )
    return jax.shard_map(
        on_device,
        mesh=mesh,
        in_specs=placed,
        out_specs=(P(("head", "ctx"), None), P(("head", "ctx"), None), P(("head", "ctx"), None)),
        check_vma=False,
    )
```

profile of v0, /device:TPU:16, one launch (start us, length us, event | category | flops | bytes accessed | tf_op | source)
XLA Modules:
  0.0 1526.2 jit_solution(12706832629339352924)
XLA Ops:
  10.5 30.1 %all_gather.20 = bf16[128,128]{1,0:T(8,128)(2,1)} all-gather(bf16[16,128]{1,0:T(8,128)(2,1)} %param.9), channel_id=1, replica_groups=mesh['head'=8,'ctx'=64] {'head'}, dimensions={0}, use_global_device_ids=true | all-gather | bytes 36864 | tf_op jit(solution)/shard_map/all_gather | solution.py:96
  40.7 29.6 %all_gather.22 = bf16[128,128]{1,0:T(8,128)(2,1)} all-gather(bf16[16,128]{1,0:T(8,128)(2,1)} %param.10), channel_id=1, replica_groups=mesh['head'=8,'ctx'=64] {'head'}, dimensions={0}, use_global_device_ids=true | all-gather | bytes 36864 | tf_op jit(solution)/shard_map/all_gather | solution.py:97
  71.0 4.9 all-to-all-start
  77.3 205.7 %all-reduce.5.cloned.1.call-done = (s32[8192]{0:T(1024)}, s32[8192]{0:T(1024)}) async-done(((s32[8192]{0:T(1024)}, s32[8192]{0:T(1024)}), (s32[8192]{0:T(1024)}, s32[8192]{0:T(1024)})) %all-reduce.5.cloned.1.call-update) | async-done | bytes 65552
  301.4 1156.3 %while.27 = (s32[]{:T(128)}, bf16[128,1,128]{2,0,1:T(8,128)(2,1)S(1)}, bf16[128,1,128]{2,0,1:T(8,128)(2,1)S(1)}, f32[128,1]{0,1:T(1,128)S(1)}, f32[128,1]{0,1:T(...) while((s32[]{:T(128)}, ...), condition=%wide.wide.region_4.5_spmd.clone, body=%wide.wide.region_3.4_spmd.clone.sunk | while | flops 21299216 | bytes 1848870 | solution.py:132
  366.7 4.7 collective-permute-done.4
  385.8 5.7 collective-permute-done.4
  405.1 5.4 collective-permute-done.4
  424.2 4.5 collective-permute-done.4
  442.4 4.5 collective-permute-done.4
  460.7 5.4 collective-permute-done.4
  479.7 5.2 collective-permute-done.4
  498.6 4.9 collective-permute-done.4
  517.3 4.5 collective-permute-done.4
  535.5 5.3 collective-permute-done.4
  554.5 5.2 collective-permute-done.4
  573.4 4.9 collective-permute-done.4
  592.0 4.5 collective-permute-done.4
  610.2 6.1 collective-permute-done.4
  630.0 5.0 collective-permute-done.4
  685.1 5.0 collective-permute-done.4
  703.8 4.6 collective-permute-done.4
  722.0 5.9 collective-permute-done.4
  741.6 4.8 collective-permute-done.4
  760.2 4.8 collective-permute-done.4
  778.6 4.5 collective-permute-done.4
  796.8 4.6 collective-permute-done.4
  815.2 4.7 collective-permute-done.4
  851.7 4.5 collective-permute-done.4
  870.0 4.5 collective-permute-done.4
  888.2 4.5 collective-permute-done.4
  906.4 4.5 collective-permute-done.4
  924.6 4.5 collective-permute-done.4
  942.9 4.5 collective-permute-done.4
  961.1 4.5 collective-permute-done.4
  979.3 4.5 collective-permute-done.4
  997.5 4.5 collective-permute-done.4
  1015.8 4.5 collective-permute-done.4
  1034.0 4.5 collective-permute-done.4
  1052.2 4.5 collective-permute-done.4
  1070.4 4.5 collective-permute-done.4
  1088.6 4.5 collective-permute-done.4
  1106.9 4.5 collective-permute-done.4
  1125.1 4.5 collective-permute-done.4
  1143.3 4.5 collective-permute-done.4
  1161.5 4.5 collective-permute-done.4
  1179.8 4.5 collective-permute-done.4
  1198.0 4.5 collective-permute-done.4
  1216.2 4.5 collective-permute-done.4
  1234.4 4.5 collective-permute-done.4
  1252.7 4.5 collective-permute-done.4
  1270.9 4.5 collective-permute-done.4
  1289.1 4.5 collective-permute-done.4
  1307.3 4.5 collective-permute-done.4
  1325.6 4.5 collective-permute-done.4
  1343.8 4.5 collective-permute-done.4
  1362.0 4.5 collective-permute-done.4
  1398.5 4.5 collective-permute-done.4
  1416.7 4.5 collective-permute-done.4
  1434.9 4.5 collective-permute-done.4
  1460.5 6.6 collective-permute-done.5
  1467.0 6.6 all-to-all-start.2
  1474.3 5.6 all-to-all-done.2
  1480.6 36.8 %reduce-scatter.2.cloned.1.call-done = f32[16,256]{1,0:T(8,128)} async-done(((f32[128,256]{1,0:T(8,128)}), f32[16,256]{1,0:T(8,128)}) %reduce-scatter.2.cloned.1.call-update) | async-done | bytes 16400 | tf_op jit(solution)/shard_map/reduce_scatter | solution.py:136
  (1459 shorter events, 915.4 us)
Async XLA Ops:
  8.0 275.0 %all-reduce.5.cloned.1.call-start = ((), (), s32[]{:S(2)}) async-start(), calls=%async_computation.7 | async-start | bytes 131072
  10.5 280.2 %all-gather.3.cloned.1.call-start = ((), (), s32[]{:S(2)}) async-start(), calls=%async_computation.4 | async-start | bytes 2129920 | tf_op jit(solution)/shard_map/all_gather | solution.py:101
  40.7 256.2 %all-gather.5.cloned.1.call-start = ((), (), s32[]{:S(2)}) async-start(), calls=%async_computation.5 | async-start | bytes 2129920 | tf_op jit(solution)/shard_map/all_gather | solution.py:102
  71.0 216.1 %all-to-all-start = ((bf16[16,8,128]{2,0,1:T(8,128)(2,1)}), bf16[16,8,128]{2,0,1:T(8,128)(2,1)S(1)}, u32[]{:S(2)}, u32[]{:S(2)}) async-start(bf16[16,8,128]{2,0,1:T(8,128)(2,1)} %copy_bitcast_fusion.2), calls=%async_computation | async-start | bytes 65536 | tf_op jit(solution)/shard_map/all_to_all | solution.py:70
  301.4 14.0 collective-permute-start
  318.7 13.7 collective-permute-start
  336.0 13.7 collective-permute-start
  353.0 13.7 collective-permute-start
  371.4 14.4 collective-permute-start
  391.4 13.7 collective-permute-start
  410.5 13.7 collective-permute-start
  428.7 13.7 collective-permute-start
  447.0 13.7 collective-permute-start
  466.0 13.7 collective-permute-start
  485.0 13.7 collective-permute-start
  503.6 13.7 collective-permute-start
  521.8 13.7 collective-permute-start
  540.8 13.7 collective-permute-start
  559.7 13.7 collective-permute-start
  578.3 13.7 collective-permute-start
  596.5 13.7 collective-permute-start
  616.3 13.7 collective-permute-start
  635.0 13.7 collective-permute-start
  653.2 13.7 collective-permute-start
  671.4 13.7 collective-permute-start
  690.1 13.7 collective-permute-start
  708.4 13.7 collective-permute-start
  728.0 13.7 collective-permute-start
  746.5 13.7 collective-permute-start
  764.9 13.7 collective-permute-start
  783.2 13.7 collective-permute-start
  801.5 13.7 collective-permute-start
  819.8 13.7 collective-permute-start
  838.0 13.7 collective-permute-start
  856.3 13.7 collective-permute-start
  874.5 13.7 collective-permute-start
  892.7 13.7 collective-permute-start
  910.9 13.7 collective-permute-start
  929.2 13.7 collective-permute-start
  947.4 13.7 collective-permute-start
  965.6 13.7 collective-permute-start
  983.8 13.7 collective-permute-start
  1002.1 13.7 collective-permute-start
  1020.3 13.7 collective-permute-start
  1038.5 13.7 collective-permute-start
  1056.7 13.7 collective-permute-start
  1075.0 13.7 collective-permute-start
  1093.2 13.7 collective-permute-start
  1111.4 13.7 collective-permute-start
  1129.6 13.7 collective-permute-start
  1166.1 13.7 collective-permute-start
  1184.3 13.7 collective-permute-start
  1202.5 13.7 collective-permute-start
  1220.8 13.7 collective-permute-start
  1239.0 13.7 collective-permute-start
  1275.4 13.7 collective-permute-start
  1293.7 13.7 collective-permute-start
  1311.9 13.7 collective-permute-start
  1330.1 13.7 collective-permute-start
  1348.3 13.7 collective-permute-start
  1403.0 13.7 collective-permute-start
  1421.2 13.7 collective-permute-start
  1439.5 13.7 collective-permute-start
  1473.6 43.8 %reduce-scatter.2.cloned.1.call-start = ((), (), s32[]{:S(2)}) async-start(), calls=%async_computation.6 | async-start | bytes 147456 | tf_op jit(solution)/shard_map/reduce_scatter | solution.py:136
  (267 other events, 2477.1 us)
Sparse Core Ops, SparseCore 0:
  14.1 268.8 all-reduce.4
  1477.4 39.9 reduce-scatter.1
Sparse Core Ops, SparseCore 1:
  40.8 87.4 all-gather.2
  131.4 80.4 all-gather.4
where the time goes:
time: 1540 us; the launch traced here: 1530 us
  starting transfers between devices  702 us (46%)
  waiting for transfers between devices  650 us (42%)
  matrix products  60.7 us (4%)
  blocking collectives  59.8 us (4%)
  local copies, waits for them, and re-layouts  24.1 us (2%)
  between operations  15.7 us (1%)
    ppermute x316, starting transfers between devices, from_behind(): return lax.ppermute(block, axis, route)  687 us
    ppermute x316, waiting for transfers between devices, from_behind(): return lax.ppermute(block, axis, route)  402 us
    unnamed x5, waiting for transfers between devices  206 us
    reduce_scatter x1, waiting for transfers between devices, on_device(): lax.psum_scatter(key_grads, 'head', scatter_dimension=0, tiled=True)  36.8 us
  transfers between devices with their start and end apart: 323, of which 133 were waited for; matrix products, arithmetic and copies ran while one was open for 5% of the time, Pallas kernels for 0%

commit v1 on v0

v1 whole, which is shorter than its diff:
```python
import functools
import math

import jax
import jax.numpy as jnp
from jax import lax
from jax.experimental import pallas as pl
from jax.experimental.pallas import tpu as pltpu
from jax.sharding import PartitionSpec as P

LOW = -1e30
FLOOR = -1e29
DOC_STEP = 8192.0
META = 8


def dot_rows(a, b):
    return lax.dot_general(a, b, (((1,), (1,)), ((), ())), preferred_element_type=jnp.float32)


def dot_plain(a, b):
    return lax.dot_general(a, b, (((1,), (0,)), ((), ())), preferred_element_type=jnp.float32)


def dot_cols(a, b):
    return lax.dot_general(a, b, (((0,), (0,)), ((), ())), preferred_element_type=jnp.float32)


def pack_kernel(pos_ref, doc_ref, q_ref, g_ref, k_ref, v_ref, qp_ref, kp_ref):
    run, hd = k_ref.shape
    heads = q_ref.shape[1] // hd
    n_q, n_k = qp_ref.shape[0], kp_ref.shape[0]
    rows = run * heads
    first = pos_ref[0] // run
    high, low = first // 16, first % 16
    row = lax.broadcasted_iota(jnp.int32, (META, hd), 0)
    lane = lax.broadcasted_iota(jnp.int32, (META, hd), 1)
    tok = lane % run
    docs = jnp.zeros((META, hd), jnp.int32)
    for t in range(run):
        docs = jnp.where(tok == t, doc_ref[t], docs)
    q_meta = jnp.where(row == 0, docs, jnp.where(row == 1, high, jnp.where(row == 2, low, 0)))
    half = hd // 2
    tok_here = jnp.where(lane >= half, row + META, row)
    docs = jnp.zeros((META, hd), jnp.int32)
    for t in range(run):
        docs = jnp.where(tok_here == t, doc_ref[t], docs)
    item = lane % half
    k_meta = jnp.where(item == 0, docs, jnp.where(item == 1, high, jnp.where(item == 2, low, 0)))
    q_meta = q_meta.astype(jnp.float32).astype(jnp.bfloat16)
    k_meta = k_meta.astype(jnp.float32).astype(jnp.bfloat16)
    for h in range(heads):
        q_h = q_ref[:, h * hd : (h + 1) * hd]
        g_h = g_ref[:, h * hd : (h + 1) * hd]
        for d in range(n_q):
            qp_ref[d, h * run : (h + 1) * run, :] = q_h
            qp_ref[d, rows + h * run : rows + (h + 1) * run, :] = g_h
    for d in range(n_q):
        qp_ref[d, 2 * rows : 2 * rows + META, :] = q_meta
    k, v = k_ref[...], v_ref[...]
    for d in range(n_k):
        kp_ref[d, 0:run, :] = k
        kp_ref[d, run : 2 * run, :] = v
        kp_ref[d, 2 * run : 2 * run + META, :] = k_meta


def key_codes(kp_ref, run):
    n_k, _, hd = kp_ref.shape
    meta = kp_ref[:, 2 * run : 2 * run + META, :].astype(jnp.float32).reshape(n_k * META, hd)
    src = lax.broadcasted_iota(jnp.int32, (hd, 2 * hd), 0)
    dst = lax.broadcasted_iota(jnp.int32, (hd, 2 * hd), 1)
    half = hd // 2
    item = src % half
    weight = jnp.where(
        item == 0, DOC_STEP, jnp.where(item == 1, run * 16.0, jnp.where(item == 2, run * 1.0, 0.0))
    )
    weight = jnp.where((src >= half) == (dst >= hd), weight, 0.0)
    codes = dot_plain(meta.astype(jnp.bfloat16), weight.astype(jnp.bfloat16))
    tok = lax.broadcasted_iota(jnp.int32, (n_k, META, hd), 1).astype(jnp.float32)
    lower = codes[:, :hd].reshape(n_k, META, hd) + tok
    upper = codes[:, hd:].reshape(n_k, META, hd) + (tok + META)
    return jnp.concatenate([lower, upper], axis=1).reshape(n_k * run, hd)


def query_codes(qp_ref, d, run):
    rows = (qp_ref.shape[1] - META) // 2
    meta = qp_ref[d, 2 * rows : 2 * rows + META, :].astype(jnp.float32)
    tok = (lax.broadcasted_iota(jnp.int32, (1, rows), 1) % run).astype(jnp.float32)
    base = meta[0:1] * DOC_STEP
    return base, base + meta[1:2] * (run * 16.0) + meta[2:3] * float(run) + tok


def stats_kernel(qp_ref, kp_ref, out_ref, code_ref, *, chunk):
    n_q, block, hd = qp_ref.shape
    n_k = kp_ref.shape[0]
    rows = (block - META) // 2
    run = (kp_ref.shape[1] - META) // 2
    scale = 1.0 / math.sqrt(hd)
    code_ref[...] = key_codes(kp_ref, run)
    per = chunk // run
    for d in range(0, n_q, 2):
        q = qp_ref[d : d + 2, 0:rows, :].reshape(2 * rows, hd)
        g = qp_ref[d : d + 2, rows : 2 * rows, :].reshape(2 * rows, hd)
        pairs = [query_codes(qp_ref, d + i, run) for i in range(2)]
        base = jnp.concatenate([p[0] for p in pairs], axis=1)
        top = jnp.concatenate([p[1] for p in pairs], axis=1)
        high = jnp.full((1, 2 * rows), FLOOR, jnp.float32)
        total = jnp.zeros((1, 2 * rows), jnp.float32)
        cross = jnp.zeros((1, 2 * rows), jnp.float32)
        for c in range(n_k // per):
            k = kp_ref[c * per : (c + 1) * per, 0:run, :].reshape(chunk, hd)
            v = kp_ref[c * per : (c + 1) * per, run : 2 * run, :].reshape(chunk, hd)
            code = code_ref[c * chunk : (c + 1) * chunk, :]
            code = jnp.concatenate([code] * (2 * rows // hd), axis=1)
            seen = (code <= top) & (code >= base)
            s = jnp.where(seen, dot_rows(k, q) * scale, LOW)
            dp = dot_rows(v, g)
            new = jnp.maximum(high, jnp.max(s, axis=0, keepdims=True))
            w = jnp.exp(s - new)
            keep = jnp.exp(high - new)
            total = total * keep + jnp.sum(w, axis=0, keepdims=True)
            cross = cross * keep + jnp.sum(w * dp, axis=0, keepdims=True)
            high = new
        some = total > 0.0
        safe = jnp.where(some, total, 1.0)
        log_total = jnp.where(some, high + jnp.log(safe), LOW)
        row_dot = jnp.where(some, cross / safe, 0.0)
        for i in range(2):
            for to in range(n_q):
                lo, hi = i * rows, (i + 1) * rows
                out_ref[to, d + i : d + i + 1, :] = log_total[:, lo:hi]
                out_ref[to, n_q + d + i : n_q + d + i + 1, :] = row_dot[:, lo:hi]


def grads_kernel(qp_ref, kp_ref, st_ref, gq_ref, gkv_ref, code_ref, log_ref, dot_ref, acc_ref, *, chunk):
    n_q, block, hd = qp_ref.shape
    n_k = kp_ref.shape[0]
    rows = (block - META) // 2
    run = (kp_ref.shape[1] - META) // 2
    scale = 1.0 / math.sqrt(hd)
    code_ref[...] = key_codes(kp_ref, run)
    logs = st_ref[:, 0:n_q, :]
    high = jnp.max(logs, axis=0)
    log_total = high + jnp.log(jnp.sum(jnp.exp(logs - high[None]), axis=0))
    log_ref[...] = log_total
    dot_ref[...] = jnp.sum(jnp.exp(logs - log_total[None]) * st_ref[:, n_q:, :], axis=0)
    per = chunk // run
    for d in range(0, n_q, 2):
        q = qp_ref[d : d + 2, 0:rows, :].reshape(2 * rows, hd)
        g = qp_ref[d : d + 2, rows : 2 * rows, :].reshape(2 * rows, hd)
        pairs = [query_codes(qp_ref, d + i, run) for i in range(2)]
        base = jnp.concatenate([p[0] for p in pairs], axis=1)
        top = jnp.concatenate([p[1] for p in pairs], axis=1)
        log_row = jnp.concatenate([log_ref[d + i : d + i + 1, :] for i in range(2)], axis=1)
        dot_row = jnp.concatenate([dot_ref[d + i : d + i + 1, :] for i in range(2)], axis=1)
        gq = jnp.zeros((2 * rows, hd), jnp.float32)
        for c in range(n_k // per):
            k = kp_ref[c * per : (c + 1) * per, 0:run, :].reshape(chunk, hd)
            v = kp_ref[c * per : (c + 1) * per, run : 2 * run, :].reshape(chunk, hd)
            code = code_ref[c * chunk : (c + 1) * chunk, :]
            code = jnp.concatenate([code] * (2 * rows // hd), axis=1)
            seen = (code <= top) & (code >= base)
            w = jnp.exp(jnp.where(seen, dot_rows(k, q) * scale, LOW) - log_row)
            ds = (w * (dot_rows(v, g) - dot_row)).astype(jnp.bfloat16)
            gq = gq + dot_cols(ds, k)
            gk = dot_plain(ds, q)
            gv = dot_plain(w.astype(jnp.bfloat16), g)
            at = pl.ds(c * chunk, chunk)
            if d == 0:
                acc_ref[0, at, :] = gk
                acc_ref[1, at, :] = gv
            else:
                acc_ref[0, at, :] += gk
                acc_ref[1, at, :] += gv
        gq_ref[d : d + 2] = (gq * scale).reshape(2, rows, hd).astype(gq_ref.dtype)
    gkv_ref[:, 0:run, :] = (acc_ref[0] * scale).reshape(n_k, run, hd).astype(gkv_ref.dtype)
    gkv_ref[:, run:, :] = acc_ref[1].reshape(n_k, run, hd).astype(gkv_ref.dtype)


def finish_kernel(gq_ref, gkv_ref, oq_ref, ok_ref, ov_ref):
    run, hd = ok_ref.shape
    gq = jnp.sum(gq_ref[...].astype(jnp.float32), axis=0)
    for h in range(oq_ref.shape[1] // hd):
        oq_ref[:, h * hd : (h + 1) * hd] = gq[h * run : (h + 1) * run, :]
    gkv = jnp.sum(gkv_ref[...].astype(jnp.float32), axis=0)
    ok_ref[...] = gkv[:run]
    ov_ref[...] = gkv[run:]


VMEM = pl.BlockSpec(memory_space=pltpu.VMEM)
SMEM = pl.BlockSpec(memory_space=pltpu.SMEM)


def call(kernel, in_specs, outs, scratch=()):
    return pl.pallas_call(
        kernel,
        in_specs=in_specs,
        out_specs=[VMEM] * len(outs),
        out_shape=outs,
        scratch_shapes=list(scratch),
        compiler_params=pltpu.CompilerParams(vmem_limit_bytes=48 * 1024 * 1024),
    )


def on_device(queries, key_vecs, value_vecs, out_grad, positions, documents):
    n_q, n_k = lax.axis_size("head"), lax.axis_size("ctx")
    run, hd = key_vecs.shape
    heads = queries.shape[1] // hd
    rows = run * heads
    bf, f32 = jnp.bfloat16, jnp.float32
    keys = n_k * run
    chunk = min(256, keys)
    struct = jax.ShapeDtypeStruct

    def swap(x, axis):
        return lax.all_to_all(x, axis, split_axis=0, concat_axis=0, tiled=True)

    qp, kp = call(
        pack_kernel,
        [SMEM, SMEM] + [VMEM] * 4,
        [struct((n_q, 2 * rows + META, hd), bf), struct((n_k, 2 * run + META, hd), bf)],
    )(positions, documents, queries, out_grad, key_vecs, value_vecs)
    kp = swap(kp, "ctx")
    qp = swap(qp, "head")
    (st,) = call(
        functools.partial(stats_kernel, chunk=chunk),
        [VMEM] * 2,
        [struct((n_q, 2 * n_q, rows), f32)],
        [pltpu.VMEM((keys, hd), f32)],
    )(qp, kp)
    st = swap(st, "head")
    gq, gkv = call(
        functools.partial(grads_kernel, chunk=chunk),
        [VMEM] * 3,
        [struct((n_q, rows, hd), f32), struct((n_k, 2 * run, hd), bf)],
        [
            pltpu.VMEM((keys, hd), f32),
            pltpu.VMEM((n_q, rows), f32),
            pltpu.VMEM((n_q, rows), f32),
            pltpu.VMEM((2, keys, hd), f32),
        ],
    )(qp, kp, st)
    gkv = swap(gkv, "ctx")
    gq = swap(gq, "head")
    return tuple(
        call(
            finish_kernel,
            [VMEM] * 2,
            [struct((run, heads * hd), f32), struct((run, hd), f32), struct((run, hd), f32)],
        )(gq, gkv)
    )


def solution(mesh):
    tok = P(("head", "ctx"))
    two = P(("head", "ctx"), None)
    return jax.shard_map(
        on_device,
        mesh=mesh,
        in_specs=(two, two, two, two, tok, tok),
        out_specs=(two, two, two),
        check_vma=False,
    )
```

time: 1540 us -> 116 us (0.08)
  starting transfers between devices: 702 us -> 0 us
  waiting for transfers between devices: 650 us -> 0 us
  matrix products: 60.7 us -> 0 us
  blocking collectives: 59.8 us -> 101 us
  local copies, waits for them, and re-layouts: 24.1 us -> 4.19 us
    ppermute x316 -> x0, starting transfers between devices: 687 us -> none  [from_behind(): return lax.ppermute(block, axis, route)]
    ppermute x316 -> x0, waiting for transfers between devices: 402 us -> none  [from_behind(): return lax.ppermute(block, axis, route)]
    unnamed x5 -> x0, waiting for transfers between devices: 206 us -> none
    all_to_all x0 -> x5, blocking collectives: none -> 101 us  [swap(): return lax.all_to_all(x, axis, split_axis=0, concat_axis=0, tiled=True)]
    dot_general x322 -> x0, matrix products: 60.7 us -> none  [the longest x65 14 us: masked_scores(): jnp.einsum('thd,kd->thk', query_cube, key_rows, preferred_element_type=jn...]
    all_gather x2 -> x0, blocking collectives: 59.8 us -> none  [the longest x1 30.1 us: on_device(): lax.all_gather(key_vecs, 'head', axis=0, tiled=True)]
    reduce_scatter x1 -> x0, waiting for transfers between devices: 36.8 us -> none  [on_device(): lax.psum_scatter(key_grads, 'head', scatter_dimension=0, tiled=True)]
  transfers between devices with their start and end apart: 323 -> 0, of which waited for: 133 -> 0; matrix products, arithmetic and copies ran while one was open for 5% -> 0% of each run, Pallas kernels for 0% -> 0%
where the time goes in v1:
time: 116 us; the launch traced here: 115 us
  blocking collectives  101 us (87%)
  Pallas kernels  9.37 us (8%)
  local copies, waits for them, and re-layouts  4.19 us (4%)
    all_to_all x5, blocking collectives, swap(): return lax.all_to_all(x, axis, split_axis=0, concat_axis=0, tiled=True)  101 us
    pallas_call x1, Pallas kernels, on_device(): call(functools.partial(grads_kernel, chunk=chunk), [VMEM] * 3, [struct((n...  5.68 us
    unnamed x12, local copies, waits for them, and re-layouts  4.19 us

profile of v1, /device:TPU:16, one launch (start us, length us, event | category | flops | bytes accessed | tf_op | source)
XLA Modules:
  0.0 114.9 jit_solution(4304845164577853333)
XLA Ops:
  0.6 0.0 copy-start
  0.6 0.7 copy-done
  1.4 0.0 copy-start.1
  1.4 0.8 copy-done.1
  2.1 0.0 copy-start.2
  2.2 0.7 copy-done.2
  2.8 0.0 copy-start.3
  2.8 0.7 copy-done.3
  3.5 0.0 copy-start.4
  3.5 0.7 copy-done.4
  4.2 0.0 copy-start.5
  4.2 0.7 copy-done.5
  4.8 0.7 shard_map.85
  5.5 15.6 %all_to_all.25.qp_ref = bf16[8,264,128]{2,1,0:T(8,128)(2,1)S(1)} all-to-all(bf16[8,264,128]{2,1,0:T(8,128)(2,1)S(1)} %get-tuple-element.7), channel_id=1, replica_groups=mesh['head'=8,'ctx'=64] {'head'}, dimensions={0} | all-to-all | bytes 1081344 | tf_op jit(solution)/shard_map/all_to_all | solution.py:216
  21.2 37.9 %all_to_all.26.kp_ref = bf16[64,40,128]{2,1,0:T(8,128)(2,1)S(1)} all-to-all(bf16[64,40,128]{2,1,0:T(8,128)(2,1)S(1)} %get-tuple-element.8), channel_id=1, replica_groups=mesh['head'=8,'ctx'=64] {'ctx'}, dimensions={0} | all-to-all | bytes 1310720 | tf_op jit(solution)/shard_map/all_to_all | solution.py:216
  59.0 2.3 %shard_map.86 = f32[8,16,128]{2,1,0:T(8,128)S(1)} custom-call(bf16[8,264,128]{2,1,0:T(8,128)(2,1)S(1)} %all_to_all.25.qp_ref, bf16[64,40,128]{2,1,0:T(8,128)(2,1)S(1)} %all_to_all.26.kp_ref), custom_call_target="tpu_custom_call" | custom-call | tf_op jit(solution)/shard_map/pallas_call | solution.py:225
  61.3 8.7 %all_to_all.27.st_ref = f32[8,16,128]{2,1,0:T(8,128)S(1)} all-to-all(f32[8,16,128]{2,1,0:T(8,128)S(1)} %shard_map.86), channel_id=1, replica_groups=mesh['head'=8,'ctx'=64] {'head'}, dimensions={0} | all-to-all | bytes 131072 | tf_op jit(solution)/shard_map/all_to_all | solution.py:216
  70.1 5.7 %shard_map.87 = (f32[8,128,128]{2,1,0:T(8,128)S(1)}, bf16[64,32,128]{2,1,0:T(8,128)(2,1)S(1)}) custom-call(bf16[8,264,128]{2,1,0:T(8,128)(2,1)S(1)} %all_to_all.25.qp_ref, bf16[64,40,128]{2,1,0:T(8,128)(2,1)S(1)} %all_to_all.26.kp_ref, f32[8,16,128]{2,1,0:T(8,128)S(1)} %all_to_all.27.st_ref), custom_call_target="tpu_custom_call" | custom-call | tf_op jit(solution)/shard_map/pallas_call | solution.py:232
  75.7 12.4 %all_to_all.28.gq_ref = f32[8,128,128]{2,1,0:T(8,128)S(1)} all-to-all(f32[8,128,128]{2,1,0:T(8,128)S(1)} %get-tuple-element.9), channel_id=1, replica_groups=mesh['head'=8,'ctx'=64] {'head'}, dimensions={0} | all-to-all | bytes 1048576 | tf_op jit(solution)/shard_map/all_to_all | solution.py:216
  88.2 26.0 %all_to_all.29.gkv_ref = bf16[64,32,128]{2,1,0:T(8,128)(2,1)S(1)} all-to-all(bf16[64,32,128]{2,1,0:T(8,128)(2,1)S(1)} %get-tuple-element.10), channel_id=1, replica_groups=mesh['head'=8,'ctx'=64] {'ctx'}, dimensions={0} | all-to-all | bytes 1048576 | tf_op jit(solution)/shard_map/all_to_all | solution.py:216
  114.1 0.7 shard_map.88
Async XLA Ops:
  0.6 0.8 copy-start
  1.4 0.8 copy-start.1
  2.1 0.7 copy-start.2
  2.8 0.7 copy-start.3
  3.5 0.7 copy-start.4
  4.2 0.7 copy-start.5

commit v2 on v1

--- a/solution.py
+++ b/solution.py
@@ -6,8 +6,10 @@
 from jax import lax
 from jax.experimental import pallas as pl
 from jax.experimental.pallas import tpu as pltpu
+from jax.sharding import Mesh
 from jax.sharding import PartitionSpec as P
 
+GRANT = 60 * 1024 * 1024
 LOW = -1e30
 FLOOR = -1e29
 DOC_STEP = 8192.0
@@ -26,7 +28,15 @@
     return lax.dot_general(a, b, (((0,), (0,)), ((), ())), preferred_element_type=jnp.float32)
 
 
-def pack_kernel(pos_ref, doc_ref, q_ref, g_ref, k_ref, v_ref, qp_ref, kp_ref):
+def pack_kernel(pos_any, doc_any, q_any, g_any, k_any, v_any, qp_ref, kp_ref, *scratch):
+    bufs, sems = scratch[:6], scratch[6]
+    hbm = (pos_any, doc_any, q_any, g_any, k_any, v_any)
+    copies = [pltpu.make_async_copy(src, dst, sems.at[i]) for i, (src, dst) in enumerate(zip(hbm, bufs))]
+    for copy in copies:
+        copy.start()
+    for copy in copies:
+        copy.wait()
+    pos_ref, doc_ref, q_ref, g_ref, k_ref, v_ref = bufs
     run, hd = k_ref.shape
     heads = q_ref.shape[1] // hd
     n_q, n_k = qp_ref.shape[0], kp_ref.shape[0]
@@ -90,18 +100,21 @@
     return base, base + meta[1:2] * (run * 16.0) + meta[2:3] * float(run) + tok
 
 
-def stats_kernel(qp_ref, kp_ref, out_ref, code_ref, *, chunk):
-    n_q, block, hd = qp_ref.shape
+def stats_kernel(side_ref, qa_ref, qb_ref, kp_ref, out_ref, code_ref, *, chunk):
+    n_q, block, hd = qa_ref.shape
     n_k = kp_ref.shape[0]
     rows = (block - META) // 2
     run = (kp_ref.shape[1] - META) // 2
     scale = 1.0 / math.sqrt(hd)
+    side = side_ref[0]
     code_ref[...] = key_codes(kp_ref, run)
     per = chunk // run
-    for d in range(0, n_q, 2):
-        q = qp_ref[d : d + 2, 0:rows, :].reshape(2 * rows, hd)
-        g = qp_ref[d : d + 2, rows : 2 * rows, :].reshape(2 * rows, hd)
-        pairs = [query_codes(qp_ref, d + i, run) for i in range(2)]
+    for d in range(0, 2 * n_q, 2):
+        qp_ref, at = (qa_ref, d) if d < n_q else (qb_ref, d - n_q)
+        home = (side if d < n_q else 1 - side) * n_q + at
+        q = qp_ref[at : at + 2, 0:rows, :].reshape(2 * rows, hd)
+        g = qp_ref[at : at + 2, rows : 2 * rows, :].reshape(2 * rows, hd)
+        pairs = [query_codes(qp_ref, at + i, run) for i in range(2)]
         base = jnp.concatenate([p[0] for p in pairs], axis=1)
         top = jnp.concatenate([p[1] for p in pairs], axis=1)
         high = jnp.full((1, 2 * rows), FLOOR, jnp.float32)
@@ -126,33 +139,38 @@
         log_total = jnp.where(some, high + jnp.log(safe), LOW)
         row_dot = jnp.where(some, cross / safe, 0.0)
         for i in range(2):
-            for to in range(n_q):
+            for to in range(out_ref.shape[0]):
                 lo, hi = i * rows, (i + 1) * rows
-                out_ref[to, d + i : d + i + 1, :] = log_total[:, lo:hi]
-                out_ref[to, n_q + d + i : n_q + d + i + 1, :] = row_dot[:, lo:hi]
-
-
-def grads_kernel(qp_ref, kp_ref, st_ref, gq_ref, gkv_ref, code_ref, log_ref, dot_ref, acc_ref, *, chunk):
-    n_q, block, hd = qp_ref.shape
+                out_ref[to, pl.ds(home + i, 1), :] = log_total[:, lo:hi]
+                out_ref[to, pl.ds(2 * n_q + home + i, 1), :] = row_dot[:, lo:hi]
+
+
+def grads_kernel(
+    side_ref, qa_ref, qb_ref, kp_ref, st_ref, own_ref, oth_ref, gkv_ref, code_ref, log_ref, dot_ref, acc_ref, *, chunk
+):
+    n_q, block, hd = qa_ref.shape
     n_k = kp_ref.shape[0]
     rows = (block - META) // 2
     run = (kp_ref.shape[1] - META) // 2
     scale = 1.0 / math.sqrt(hd)
+    side = side_ref[0]
     code_ref[...] = key_codes(kp_ref, run)
-    logs = st_ref[:, 0:n_q, :]
+    logs = st_ref[:, 0 : 2 * n_q, :]
     high = jnp.max(logs, axis=0)
     log_total = high + jnp.log(jnp.sum(jnp.exp(logs - high[None]), axis=0))
     log_ref[...] = log_total
-    dot_ref[...] = jnp.sum(jnp.exp(logs - log_total[None]) * st_ref[:, n_q:, :], axis=0)
+    dot_ref[...] = jnp.sum(jnp.exp(logs - log_total[None]) * st_ref[:, 2 * n_q :, :], axis=0)
     per = chunk // run
-    for d in range(0, n_q, 2):
-        q = qp_ref[d : d + 2, 0:rows, :].reshape(2 * rows, hd)
-        g = qp_ref[d : d + 2, rows : 2 * rows, :].reshape(2 * rows, hd)
-        pairs = [query_codes(qp_ref, d + i, run) for i in range(2)]
+    for d in range(0, 2 * n_q, 2):
+        qp_ref, at, gq_ref = (qa_ref, d, own_ref) if d < n_q else (qb_ref, d - n_q, oth_ref)
+        home = (side if d < n_q else 1 - side) * n_q + at
+        q = qp_ref[at : at + 2, 0:rows, :].reshape(2 * rows, hd)
+        g = qp_ref[at : at + 2, rows : 2 * rows, :].reshape(2 * rows, hd)
+        pairs = [query_codes(qp_ref, at + i, run) for i in range(2)]
         base = jnp.concatenate([p[0] for p in pairs], axis=1)
         top = jnp.concatenate([p[1] for p in pairs], axis=1)
-        log_row = jnp.concatenate([log_ref[d + i : d + i + 1, :] for i in range(2)], axis=1)
-        dot_row = jnp.concatenate([dot_ref[d + i : d + i + 1, :] for i in range(2)], axis=1)
+        log_row = jnp.concatenate([log_ref[pl.ds(home + i, 1), :] for i in range(2)], axis=1)
+        dot_row = jnp.concatenate([dot_ref[pl.ds(home + i, 1), :] for i in range(2)], axis=1)
         gq = jnp.zeros((2 * rows, hd), jnp.float32)
         for c in range(n_k // per):
             k = kp_ref[c * per : (c + 1) * per, 0:run, :].reshape(chunk, hd)
@@ -165,14 +183,14 @@
             gq = gq + dot_cols(ds, k)
             gk = dot_plain(ds, q)
             gv = dot_plain(w.astype(jnp.bfloat16), g)
-            at = pl.ds(c * chunk, chunk)
+            where = pl.ds(c * chunk, chunk)
             if d == 0:
-                acc_ref[0, at, :] = gk
-                acc_ref[1, at, :] = gv
+                acc_ref[0, where, :] = gk
+                acc_ref[1, where, :] = gv
             else:
-                acc_ref[0, at, :] += gk
-                acc_ref[1, at, :] += gv
-        gq_ref[d : d + 2] = (gq * scale).reshape(2, rows, hd).astype(gq_ref.dtype)
+                acc_ref[0, where, :] += gk
+                acc_ref[1, where, :] += gv
+        gq_ref[at : at + 2] = (gq * scale).reshape(2, rows, hd).astype(gq_ref.dtype)
     gkv_ref[:, 0:run, :] = (acc_ref[0] * scale).reshape(n_k, run, hd).astype(gkv_ref.dtype)
     gkv_ref[:, run:, :] = acc_ref[1].reshape(n_k, run, hd).astype(gkv_ref.dtype)
 
@@ -189,21 +207,22 @@
 
 VMEM = pl.BlockSpec(memory_space=pltpu.VMEM)
 SMEM = pl.BlockSpec(memory_space=pltpu.SMEM)
-
-
-def call(kernel, in_specs, outs, scratch=()):
+HBM = pl.BlockSpec(memory_space=pltpu.HBM)
+
+
+def call(kernel, in_specs, outs, scratch=(), grant=48 * 1024 * 1024):
     return pl.pallas_call(
         kernel,
         in_specs=in_specs,
         out_specs=[VMEM] * len(outs),
         out_shape=outs,
         scratch_shapes=list(scratch),
-        compiler_params=pltpu.CompilerParams(vmem_limit_bytes=48 * 1024 * 1024),
+        compiler_params=pltpu.CompilerParams(vmem_limit_bytes=grant),
     )
 
 
 def on_device(queries, key_vecs, value_vecs, out_grad, positions, documents):
-    n_q, n_k = lax.axis_size("head"), lax.axis_size("ctx")
+    n_q, n_k, sides = lax.axis_size("head"), lax.axis_size("far"), lax.axis_size("core")
     run, hd = key_vecs.shape
     heads = queries.shape[1] // hd
     rows = run * heads
@@ -215,32 +234,43 @@
     def swap(x, axis):
         return lax.all_to_all(x, axis, split_axis=0, concat_axis=0, tiled=True)
 
+    def other(x):
+        return lax.ppermute(x, "core", [(0, 1), (1, 0)])
+
+    side = lax.axis_index("core").astype(jnp.int32).reshape(1)
+    args = (positions, documents, queries, out_grad, key_vecs, value_vecs)
     qp, kp = call(
         pack_kernel,
-        [SMEM, SMEM] + [VMEM] * 4,
+        [HBM] * 6,
         [struct((n_q, 2 * rows + META, hd), bf), struct((n_k, 2 * run + META, hd), bf)],
-    )(positions, documents, queries, out_grad, key_vecs, value_vecs)
-    kp = swap(kp, "ctx")
-    qp = swap(qp, "head")
+        [(pltpu.SMEM if a.ndim == 1 else pltpu.VMEM)(a.shape, a.dtype) for a in args]
+        + [pltpu.SemaphoreType.DMA((6,))],
+        grant=GRANT,
+    )(*args)
+    qa = swap(qp, "head")
+    qb = other(qa)
+    kp = swap(kp, "far")
     (st,) = call(
         functools.partial(stats_kernel, chunk=chunk),
-        [VMEM] * 2,
-        [struct((n_q, 2 * n_q, rows), f32)],
+        [SMEM] + [VMEM] * 3,
+        [struct((sides * n_q, 2 * sides * n_q, rows), f32)],
         [pltpu.VMEM((keys, hd), f32)],
-    )(qp, kp)
-    st = swap(st, "head")
-    gq, gkv = call(
+    )(side, qa, qb, kp)
+    st = swap(st, ("head", "core"))
+    own, oth, gkv = call(
         functools.partial(grads_kernel, chunk=chunk),
-        [VMEM] * 3,
-        [struct((n_q, rows, hd), f32), struct((n_k, 2 * run, hd), bf)],
+        [SMEM] + [VMEM] * 4,
+        [struct((n_q, rows, hd), f32), struct((n_q, rows, hd), bf), struct((n_k, 2 * run, hd), bf)],
         [
             pltpu.VMEM((keys, hd), f32),
-            pltpu.VMEM((n_q, rows), f32),
-            pltpu.VMEM((n_q, rows), f32),
+            pltpu.VMEM((sides * n_q, rows), f32),
+            pltpu.VMEM((sides * n_q, rows), f32),
             pltpu.VMEM((2, keys, hd), f32),
         ],
-    )(qp, kp, st)
-    gkv = swap(gkv, "ctx")
+    )(side, qa, qb, kp, st)
+    oth = other(oth)
+    gkv = swap(gkv, "far")
+    gq = (own + oth.astype(f32)).astype(bf)
     gq = swap(gq, "head")
     return tuple(
         call(
@@ -252,11 +282,13 @@
 
 
 def solution(mesh):
-    tok = P(("head", "ctx"))
-    two = P(("head", "ctx"), None)
+    n_head, n_ctx = mesh.devices.shape
+    fine = Mesh(mesh.devices.reshape(n_head, n_ctx // 2, 2), ("head", "far", "core"))
+    tok = P(("head", "far", "core"))
+    two = P(("head", "far", "core"), None)
     return jax.shard_map(
         on_device,
-        mesh=mesh,
+        mesh=fine,
         in_specs=(two, two, two, two, tok, tok),
         out_specs=(two, two, two),
         check_vma=False,

time: 116 us -> 98.8 us (0.85)
  blocking collectives: 101 us -> 37.3 us
  waiting for transfers between devices: 0 us -> 25.2 us
  starting transfers between devices: 0 us -> 24.1 us
  local copies, waits for them, and re-layouts: 4.19 us -> 0 us
  Pallas kernels: 9.37 us -> 11 us
    all_to_all x5 -> x3, blocking collectives: 101 us -> 37.3 us  [swap(): return lax.all_to_all(x, axis, split_axis=0, concat_axis=0, tiled=True)]
    all_to_all x0 -> x2, waiting for transfers between devices: none -> 25.2 us  [swap(): return lax.all_to_all(x, axis, split_axis=0, concat_axis=0, tiled=True)]
    all_to_all x0 -> x2, starting transfers between devices: none -> 20.3 us  [swap(): return lax.all_to_all(x, axis, split_axis=0, concat_axis=0, tiled=True)]
    unnamed x12 -> x0, local copies, waits for them, and re-layouts: 4.19 us -> none
    ppermute x0 -> x2, starting transfers between devices: none -> 3.83 us  [other(): return lax.ppermute(x, 'core', [(0, 1), (1, 0)])]
    pallas_call x3, Pallas kernels: 8.64 us -> 10.3 us  [the longest x1 5.95 us: on_device(): call(functools.partial(grads_kernel, chunk=chunk), [SMEM] + [VMEM] * 4, [...]
  transfers between devices with their start and end apart: 0 -> 4, of which waited for: 0 -> 2; matrix products, arithmetic and copies ran while one was open for 0% -> 0% of each run, Pallas kernels for 0% -> 0%
where the time goes in v2:
time: 98.8 us; the launch traced here: 98.3 us
  blocking collectives  37.3 us (38%)
  waiting for transfers between devices  25.2 us (26%)
  starting transfers between devices  24.1 us (24%)
  Pallas kernels  11 us (11%)
    all_to_all x3, blocking collectives, swap(): return lax.all_to_all(x, axis, split_axis=0, concat_axis=0, tiled=True)  37.3 us
    all_to_all x2, waiting for transfers between devices, swap(): return lax.all_to_all(x, axis, split_axis=0, concat_axis=0, tiled=True)  25.2 us
    all_to_all x2, starting transfers between devices, swap(): return lax.all_to_all(x, axis, split_axis=0, concat_axis=0, tiled=True)  20.3 us
    pallas_call x1, Pallas kernels, on_device(): call(functools.partial(grads_kernel, chunk=chunk), [SMEM] + [VMEM] * 4, [...  5.95 us
    ppermute x2, starting transfers between devices, other(): return lax.ppermute(x, 'core', [(0, 1), (1, 0)])  3.83 us
    pallas_call x1, Pallas kernels, on_device(): call(functools.partial(stats_kernel, chunk=chunk), [SMEM] + [VMEM] * 3, [...  2.5 us
  transfers between devices with their start and end apart: 4, of which 2 were waited for; matrix products, arithmetic and copies ran while one was open for 0% of the time, Pallas kernels for 0%

profile of v2, /device:TPU:16, one launch (start us, length us, event | category | flops | bytes accessed | tf_op | source)
XLA Modules:
  0.0 98.3 jit_solution(9129278466210859518)
XLA Ops:
  0.6 1.8 %shard_map.85 = (bf16[8,264,128]{2,1,0:T(8,128)(2,1)}, bf16[32,40,128]{2,1,0:T(8,128)(2,1)}) custom-call(s32[16]{0:T(128)} %pos_any.1, s32[16]{0:T(128)} %doc_any.1, bf16[16,1024]{1,0:T(8,128)(2,1)} %q_any.1, bf16[16,1024]{1,0:T(8,128)(2,1)} %g_any.1, bf16[16,128]{1,0:T(8,128)(2,1)} %k_any.1, bf16[16,128]{1,0:T(8,128)(2,1)} %v_any.1), custom_call_target="tpu_custom_call" | custom-call | tf_op jit(solution)/shard_map/pallas_call | solution.py:242
  2.5 15.8 %all_to_all.25.qa_ref = bf16[8,264,128]{2,1,0:T(8,128)(2,1)S(1)} all-to-all(bf16[8,264,128]{2,1,0:T(8,128)(2,1)} %get-tuple-element.8), channel_id=1, replica_groups=mesh['head'=8,'far'=32,'core'=2] {'head'}, dimensions={0} | all-to-all | bytes 1081344 | tf_op jit(solution)/shard_map/all_to_all | solution.py:235
  18.3 15.2 %all-to-all-start.1 = ((bf16[32,40,128]{2,1,0:T(8,128)(2,1)}), bf16[32,40,128]{2,1,0:T(8,128)(2,1)S(1)}, u32[]{:S(2)}, u32[]{:S(2)}) async-start(bf16[32,40,128]{2,1,0:T(8,128)(2,1)} %get-tuple-element.9), calls=%async_computation.1 | async-start | bytes 655360 | tf_op jit(solution)/shard_map/all_to_all | solution.py:235
  33.5 1.9 %collective-permute-start = (bf16[8,264,128]{2,1,0:T(8,128)(2,1)S(1)}, bf16[8,264,128]{2,1,0:T(8,128)(2,1)S(1)}, u32[]{:S(2)}, u32[]{:S(2)}) collective-permute-start(bf16[8,264,128]{2,1,0:T(8,128)(2,1)S(1)} %all_to_all.25.qa_ref), channel_id=1, source_target_pairs={{0,1},{1,0},{2,3},{3,2},{4,5},{5,4},{6,7},{7,6},{8,9},{9,8},{10,11... | collective-permute-start | bytes 1622024 | tf_op jit(solution)/shard_map/ppermute | solution.py:238
  35.4 10.7 %all-to-all-done.1.kp_ref = bf16[32,40,128]{2,1,0:T(8,128)(2,1)S(1)} async-done(((bf16[32,40,128]{2,1,0:T(8,128)(2,1)}), bf16[32,40,128]{2,1,0:T(8,128)(2,1)S(1)}, u32[]{:S(2)}, u32[]{:S(2)}) %all-to-all-start.1) | async-done | bytes 327712 | tf_op jit(solution)/shard_map/all_to_all | solution.py:235
  46.1 0.0 collective-permute-done.qb_ref
  46.1 2.5 %shard_map.86 = f32[16,32,128]{2,1,0:T(8,128)S(1)} custom-call(s32[1]{0:T(128)} %bitcast.side_ref, bf16[8,264,128]{2,1,0:T(8,128)(2,1)S(1)} %all_to_all.25.qa_ref, bf16[8,264,128]{2,1,0:T(8,128)(2,1)S(1)} %collective-permute-done.qb_ref, bf16[32,40,128]{2,1,0:T(8,128)(2,1)S(1)} %all-to-all-done.1.kp_ref), custom_call_target="tpu_custom_call" | custom-call | tf_op jit(solution)/shard_map/pallas_call | solution.py:253
  48.6 11.8 %all_to_all.26.st_ref = f32[16,32,128]{2,1,0:T(8,128)S(1)} all-to-all(f32[16,32,128]{2,1,0:T(8,128)S(1)} %shard_map.86), channel_id=1, replica_groups=mesh['head'=8,'far'=32,'core'=2] {'head','core'}, dimensions={0} | all-to-all | bytes 524288 | tf_op jit(solution)/shard_map/all_to_all | solution.py:235
  60.4 5.9 %shard_map.87 = (f32[8,128,128]{2,1,0:T(8,128)S(1)}, bf16[8,128,128]{2,1,0:T(8,128)(2,1)S(1)}, bf16[32,32,128]{2,1,0:T(8,128)(2,1)}) custom-call(s32[1]{0:T(128)} %bitcast.side_ref, bf16[8,264,128]{2,1,0:T(8,128)(2,1)S(1)} %all_to_all.25.qa_ref, bf16[8,264,128]{2,1,0:T(8,128)(2,1)S(1)} %collective-permute-done.qb_ref, ...), custom_call_target="tpu_custom_call" | custom-call | tf_op jit(solution)/shard_map/pallas_call | solution.py:260
  66.3 1.9 %collective-permute-start.1 = (bf16[8,128,128]{2,1,0:T(8,128)(2,1)S(1)}, bf16[8,128,128]{2,1,0:T(8,128)(2,1)S(1)}, u32[]{:S(2)}, u32[]{:S(2)}) collective-permute-start(bf16[8,128,128]{2,1,0:T(8,128)(2,1)S(1)} %get-tuple-element.11), channel_id=1, source_target_pairs={{0,1},{1,0},{2,3},{3,2},{4,5},{5,4},{6,7},{7,6},{8,9},{9,8},{10,11... | collective-permute-start | bytes 786440 | tf_op jit(solution)/shard_map/ppermute | solution.py:238
  68.2 5.1 %all-to-all-start.4 = ((bf16[32,32,128]{2,1,0:T(8,128)(2,1)}), bf16[32,32,128]{2,1,0:T(8,128)(2,1)S(1)}, u32[]{:S(2)}, u32[]{:S(2)}) async-start(bf16[32,32,128]{2,1,0:T(8,128)(2,1)} %get-tuple-element.12), calls=%async_computation.4 | async-start | bytes 524288 | tf_op jit(solution)/shard_map/all_to_all | solution.py:235
  73.3 0.0 collective-permute-done.1
  73.3 0.1 add_convert_fusion
  73.4 14.5 %all-to-all-done.4.gkv_ref = bf16[32,32,128]{2,1,0:T(8,128)(2,1)S(1)} async-done(((bf16[32,32,128]{2,1,0:T(8,128)(2,1)}), bf16[32,32,128]{2,1,0:T(8,128)(2,1)S(1)}, u32[]{:S(2)}, u32[]{:S(2)}) %all-to-all-start.4) | async-done | bytes 262176 | tf_op jit(solution)/shard_map/all_to_all | solution.py:235
  87.9 9.7 %all_to_all.27.gq_ref = bf16[8,128,128]{2,1,0:T(8,128)(2,1)S(1)} all-to-all(bf16[8,128,128]{2,1,0:T(8,128)(2,1)S(1)} %add_convert_fusion), channel_id=1, replica_groups=mesh['head'=8,'far'=32,'core'=2] {'head'}, dimensions={0} | all-to-all | bytes 524288 | tf_op jit(solution)/shard_map/all_to_all | solution.py:235
  97.6 0.7 shard_map.88
Async XLA Ops:
  18.3 27.8 %all-to-all-start.1 = ((bf16[32,40,128]{2,1,0:T(8,128)(2,1)}), bf16[32,40,128]{2,1,0:T(8,128)(2,1)S(1)}, u32[]{:S(2)}, u32[]{:S(2)}) async-start(bf16[32,40,128]{2,1,0:T(8,128)(2,1)} %get-tuple-element.9), calls=%async_computation.1 | async-start | bytes 655360 | tf_op jit(solution)/shard_map/all_to_all | solution.py:235
  33.5 12.6 %collective-permute-start = (bf16[8,264,128]{2,1,0:T(8,128)(2,1)S(1)}, bf16[8,264,128]{2,1,0:T(8,128)(2,1)S(1)}, u32[]{:S(2)}, u32[]{:S(2)}) collective-permute-start(bf16[8,264,128]{2,1,0:T(8,128)(2,1)S(1)} %all_to_all.25.qa_ref), channel_id=1, source_target_pairs={{0,1},{1,0},{2,3},{3,2},{4,5},{5,4},{6,7},{7,6},{8,9},{9,8},{10,11... | collective-permute-start | bytes 1622024 | tf_op jit(solution)/shard_map/ppermute | solution.py:238
  66.3 7.0 %collective-permute-start.1 = (bf16[8,128,128]{2,1,0:T(8,128)(2,1)S(1)}, bf16[8,128,128]{2,1,0:T(8,128)(2,1)S(1)}, u32[]{:S(2)}, u32[]{:S(2)}) collective-permute-start(bf16[8,128,128]{2,1,0:T(8,128)(2,1)S(1)} %get-tuple-element.11), channel_id=1, source_target_pairs={{0,1},{1,0},{2,3},{3,2},{4,5},{5,4},{6,7},{7,6},{8,9},{9,8},{10,11... | collective-permute-start | bytes 786440 | tf_op jit(solution)/shard_map/ppermute | solution.py:238
  68.2 19.7 %all-to-all-start.4 = ((bf16[32,32,128]{2,1,0:T(8,128)(2,1)}), bf16[32,32,128]{2,1,0:T(8,128)(2,1)S(1)}, u32[]{:S(2)}, u32[]{:S(2)}) async-start(bf16[32,32,128]{2,1,0:T(8,128)(2,1)} %get-tuple-element.12), calls=%async_computation.4 | async-start | bytes 524288 | tf_op jit(solution)/shard_map/all_to_all | solution.py:235

commit v3 on v2

--- a/solution.py
+++ b/solution.py
@@ -39,7 +39,7 @@
     pos_ref, doc_ref, q_ref, g_ref, k_ref, v_ref = bufs
     run, hd = k_ref.shape
     heads = q_ref.shape[1] // hd
-    n_q, n_k = qp_ref.shape[0], kp_ref.shape[0]
+    n_k = kp_ref.shape[0]
     rows = run * heads
     first = pos_ref[0] // run
     high, low = first // 16, first % 16
@@ -62,11 +62,9 @@
     for h in range(heads):
         q_h = q_ref[:, h * hd : (h + 1) * hd]
         g_h = g_ref[:, h * hd : (h + 1) * hd]
-        for d in range(n_q):
-            qp_ref[d, h * run : (h + 1) * run, :] = q_h
-            qp_ref[d, rows + h * run : rows + (h + 1) * run, :] = g_h
-    for d in range(n_q):
-        qp_ref[d, 2 * rows : 2 * rows + META, :] = q_meta
+        qp_ref[0, h * run : (h + 1) * run, :] = q_h
+        qp_ref[0, rows + h * run : rows + (h + 1) * run, :] = g_h
+    qp_ref[0, 2 * rows : 2 * rows + META, :] = q_meta
     k, v = k_ref[...], v_ref[...]
     for d in range(n_k):
         kp_ref[d, 0:run, :] = k
@@ -100,18 +98,33 @@
     return base, base + meta[1:2] * (run * 16.0) + meta[2:3] * float(run) + tok
 
 
-def stats_kernel(side_ref, qa_ref, qb_ref, kp_ref, out_ref, code_ref, *, chunk):
-    n_q, block, hd = qa_ref.shape
+def home_of(place_ref, part, at, n_x):
+    place = place_ref[0]
+    side, y, x = place % 2, (place // 2) % 2, place // 4
+    far_y, far_side = part % 2, part // 2
+    y = 1 - y if far_y else y
+    side = 1 - side if far_side else side
+    return (lax.rem(x + n_x - at, n_x) * 2 + y) * 2 + side
+
+
+def tiles(place_ref, parts, log_ref=None):
+    n_x = parts[0].shape[0]
+    for p, ref in enumerate(parts):
+        for at in range(0, n_x, 2):
+            yield p, ref, at, [home_of(place_ref, p, at + i, n_x) for i in range(2)]
+
+
+def stats_kernel(place_ref, *refs, chunk):
+    parts, kp_ref, out_ref, code_ref = refs[:4], refs[4], refs[5], refs[6]
+    n_x, block, hd = parts[0].shape
+    n_dev = out_ref.shape[0]
     n_k = kp_ref.shape[0]
     rows = (block - META) // 2
     run = (kp_ref.shape[1] - META) // 2
     scale = 1.0 / math.sqrt(hd)
-    side = side_ref[0]
     code_ref[...] = key_codes(kp_ref, run)
     per = chunk // run
-    for d in range(0, 2 * n_q, 2):
-        qp_ref, at = (qa_ref, d) if d < n_q else (qb_ref, d - n_q)
-        home = (side if d < n_q else 1 - side) * n_q + at
+    for _, qp_ref, at, homes in tiles(place_ref, parts):
         q = qp_ref[at : at + 2, 0:rows, :].reshape(2 * rows, hd)
         g = qp_ref[at : at + 2, rows : 2 * rows, :].reshape(2 * rows, hd)
         pairs = [query_codes(qp_ref, at + i, run) for i in range(2)]
@@ -138,39 +151,40 @@
         safe = jnp.where(some, total, 1.0)
         log_total = jnp.where(some, high + jnp.log(safe), LOW)
         row_dot = jnp.where(some, cross / safe, 0.0)
-        for i in range(2):
-            for to in range(out_ref.shape[0]):
-                lo, hi = i * rows, (i + 1) * rows
-                out_ref[to, pl.ds(home + i, 1), :] = log_total[:, lo:hi]
-                out_ref[to, pl.ds(2 * n_q + home + i, 1), :] = row_dot[:, lo:hi]
-
-
-def grads_kernel(
-    side_ref, qa_ref, qb_ref, kp_ref, st_ref, own_ref, oth_ref, gkv_ref, code_ref, log_ref, dot_ref, acc_ref, *, chunk
-):
-    n_q, block, hd = qa_ref.shape
+        for i, home in enumerate(homes):
+            lo, hi = i * rows, (i + 1) * rows
+            for to in range(n_dev):
+                out_ref[to, pl.ds(home, 1), :] = log_total[:, lo:hi]
+                out_ref[to, pl.ds(n_dev + home, 1), :] = row_dot[:, lo:hi]
+
+
+def grads_kernel(place_ref, *refs, chunk):
+    parts, kp_ref, st_ref = refs[:4], refs[4], refs[5]
+    own_ref, near_ref, far_ref, gkv_ref = refs[6:10]
+    code_ref, log_ref, dot_ref, acc_ref = refs[10:]
+    n_x, block, hd = parts[0].shape
+    n_dev = st_ref.shape[0]
     n_k = kp_ref.shape[0]
     rows = (block - META) // 2
     run = (kp_ref.shape[1] - META) // 2
     scale = 1.0 / math.sqrt(hd)
-    side = side_ref[0]
     code_ref[...] = key_codes(kp_ref, run)
-    logs = st_ref[:, 0 : 2 * n_q, :]
+    logs = st_ref[:, 0:n_dev, :]
     high = jnp.max(logs, axis=0)
     log_total = high + jnp.log(jnp.sum(jnp.exp(logs - high[None]), axis=0))
     log_ref[...] = log_total
-    dot_ref[...] = jnp.sum(jnp.exp(logs - log_total[None]) * st_ref[:, 2 * n_q :, :], axis=0)
+    dot_ref[...] = jnp.sum(jnp.exp(logs - log_total[None]) * st_ref[:, n_dev:, :], axis=0)
     per = chunk // run
-    for d in range(0, 2 * n_q, 2):
-        qp_ref, at, gq_ref = (qa_ref, d, own_ref) if d < n_q else (qb_ref, d - n_q, oth_ref)
-        home = (side if d < n_q else 1 - side) * n_q + at
+    first = True
+    for p, qp_ref, at, homes in tiles(place_ref, parts):
+        gq_ref, to = ((own_ref, at), (near_ref, at), (far_ref, at), (far_ref, n_x + at))[p]
         q = qp_ref[at : at + 2, 0:rows, :].reshape(2 * rows, hd)
         g = qp_ref[at : at + 2, rows : 2 * rows, :].reshape(2 * rows, hd)
         pairs = [query_codes(qp_ref, at + i, run) for i in range(2)]
         base = jnp.concatenate([p[0] for p in pairs], axis=1)
         top = jnp.concatenate([p[1] for p in pairs], axis=1)
-        log_row = jnp.concatenate([log_ref[pl.ds(home + i, 1), :] for i in range(2)], axis=1)
-        dot_row = jnp.concatenate([dot_ref[pl.ds(home + i, 1), :] for i in range(2)], axis=1)
+        log_row = jnp.concatenate([log_ref[pl.ds(home, 1), :] for home in homes], axis=1)
+        dot_row = jnp.concatenate([dot_ref[pl.ds(home, 1), :] for home in homes], axis=1)
         gq = jnp.zeros((2 * rows, hd), jnp.float32)
         for c in range(n_k // per):
             k = kp_ref[c * per : (c + 1) * per, 0:run, :].reshape(chunk, hd)
@@ -184,20 +198,24 @@
             gk = dot_plain(ds, q)
             gv = dot_plain(w.astype(jnp.bfloat16), g)
             where = pl.ds(c * chunk, chunk)
-            if d == 0:
+            if first:
                 acc_ref[0, where, :] = gk
                 acc_ref[1, where, :] = gv
             else:
                 acc_ref[0, where, :] += gk
                 acc_ref[1, where, :] += gv
-        gq_ref[at : at + 2] = (gq * scale).reshape(2, rows, hd).astype(gq_ref.dtype)
+        first = False
+        gq_ref[to : to + 2] = (gq * scale).reshape(2, rows, hd).astype(gq_ref.dtype)
     gkv_ref[:, 0:run, :] = (acc_ref[0] * scale).reshape(n_k, run, hd).astype(gkv_ref.dtype)
     gkv_ref[:, run:, :] = acc_ref[1].reshape(n_k, run, hd).astype(gkv_ref.dtype)
 
 
-def finish_kernel(gq_ref, gkv_ref, oq_ref, ok_ref, ov_ref):
+def finish_kernel(*refs):
+    pieces, gkv_ref, (oq_ref, ok_ref, ov_ref) = refs[:-4], refs[-4], refs[-3:]
     run, hd = ok_ref.shape
-    gq = jnp.sum(gq_ref[...].astype(jnp.float32), axis=0)
+    gq = pieces[0][...]
+    for piece in pieces[1:]:
+        gq = gq + piece[...].astype(jnp.float32)
     for h in range(oq_ref.shape[1] // hd):
         oq_ref[:, h * hd : (h + 1) * hd] = gq[h * run : (h + 1) * run, :]
     gkv = jnp.sum(gkv_ref[...].astype(jnp.float32), axis=0)
@@ -222,7 +240,8 @@
 
 
 def on_device(queries, key_vecs, value_vecs, out_grad, positions, documents):
-    n_q, n_k, sides = lax.axis_size("head"), lax.axis_size("far"), lax.axis_size("core")
+    n_x, n_k = lax.axis_size("x"), lax.axis_size("far")
+    n_dev = 4 * n_x
     run, hd = key_vecs.shape
     heads = queries.shape[1] // hd
     rows = run * heads
@@ -234,58 +253,66 @@
     def swap(x, axis):
         return lax.all_to_all(x, axis, split_axis=0, concat_axis=0, tiled=True)
 
-    def other(x):
-        return lax.ppermute(x, "core", [(0, 1), (1, 0)])
-
-    side = lax.axis_index("core").astype(jnp.int32).reshape(1)
+    def shift(x, axis, by):
+        n = lax.axis_size(axis)
+        return lax.ppermute(x, axis, [(i, (i + by) % n) for i in range(n)])
+
+    place = lax.axis_index(("x", "near", "core")).astype(jnp.int32).reshape(1)
     args = (positions, documents, queries, out_grad, key_vecs, value_vecs)
     qp, kp = call(
         pack_kernel,
         [HBM] * 6,
-        [struct((n_q, 2 * rows + META, hd), bf), struct((n_k, 2 * run + META, hd), bf)],
+        [struct((1, 2 * rows + META, hd), bf), struct((n_k, 2 * run + META, hd), bf)],
         [(pltpu.SMEM if a.ndim == 1 else pltpu.VMEM)(a.shape, a.dtype) for a in args]
         + [pltpu.SemaphoreType.DMA((6,))],
         grant=GRANT,
     )(*args)
-    qa = swap(qp, "head")
-    qb = other(qa)
     kp = swap(kp, "far")
+    q_here = jnp.concatenate([qp] + [shift(qp, "x", d) for d in range(1, n_x)], axis=0)
+    q_near = shift(q_here, "near", 1)
+    parts = (q_here, q_near, shift(q_here, "core", 1), shift(q_near, "core", 1))
     (st,) = call(
         functools.partial(stats_kernel, chunk=chunk),
-        [SMEM] + [VMEM] * 3,
-        [struct((sides * n_q, 2 * sides * n_q, rows), f32)],
+        [SMEM] + [VMEM] * 5,
+        [struct((n_dev, 2 * n_dev, rows), f32)],
         [pltpu.VMEM((keys, hd), f32)],
-    )(side, qa, qb, kp)
-    st = swap(st, ("head", "core"))
-    own, oth, gkv = call(
+    )(place, *parts, kp)
+    st = swap(st, ("x", "near", "core"))
+    own, near, far, gkv = call(
         functools.partial(grads_kernel, chunk=chunk),
-        [SMEM] + [VMEM] * 4,
-        [struct((n_q, rows, hd), f32), struct((n_q, rows, hd), bf), struct((n_k, 2 * run, hd), bf)],
+        [SMEM] + [VMEM] * 6,
+        [
+            struct((n_x, rows, hd), f32),
+            struct((n_x, rows, hd), f32),
+            struct((2 * n_x, rows, hd), bf),
+            struct((n_k, 2 * run, hd), bf),
+        ],
         [
             pltpu.VMEM((keys, hd), f32),
-            pltpu.VMEM((sides * n_q, rows), f32),
-            pltpu.VMEM((sides * n_q, rows), f32),
+            pltpu.VMEM((n_dev, rows), f32),
+            pltpu.VMEM((n_dev, rows), f32),
             pltpu.VMEM((2, keys, hd), f32),
         ],
-    )(side, qa, qb, kp, st)
-    oth = other(oth)
+    )(place, *parts, kp, st)
     gkv = swap(gkv, "far")
-    gq = (own + oth.astype(f32)).astype(bf)
-    gq = swap(gq, "head")
+    far = shift(far, "core", 1).astype(f32)
+    near = shift((near + far[n_x:]).astype(bf), "near", 1).astype(f32)
+    own = own + far[:n_x] + near
+    pieces = [own[0]] + [shift(own[d].astype(bf), "x", -d) for d in range(1, n_x)]
     return tuple(
         call(
             finish_kernel,
-            [VMEM] * 2,
+            [VMEM] * (n_x + 1),
             [struct((run, heads * hd), f32), struct((run, hd), f32), struct((run, hd), f32)],
-        )(gq, gkv)
+        )(*pieces, gkv)
     )
 
 
 def solution(mesh):
     n_head, n_ctx = mesh.devices.shape
-    fine = Mesh(mesh.devices.reshape(n_head, n_ctx // 2, 2), ("head", "far", "core"))
-    tok = P(("head", "far", "core"))
-    two = P(("head", "far", "core"), None)
+    fine = Mesh(mesh.devices.reshape(n_head // 2, 2, n_ctx // 2, 2), ("x", "near", "far", "core"))
+    every = ("x", "near", "far", "core")
+    tok, two = P(every), P(every, None)
     return jax.shard_map(
         on_device,
         mesh=fine,

time: 98.8 us -> 98.9 us (level)
  the two profiles are of different devices: /device:TPU:16 before, /device:TPU:8 now
where the time goes in v3:
time: 98.9 us; the launch traced here: 98.2 us
  starting transfers between devices  58 us (59%)
  waiting for transfers between devices  16.7 us (17%)
  blocking collectives  11.7 us (12%)
  Pallas kernels  10.8 us (11%)
    ppermute x11, starting transfers between devices, shift(): return lax.ppermute(x, axis, [(i, (i + by) % n) for i in range(n)])  31.7 us
    all_to_all x2, starting transfers between devices, swap(): return lax.all_to_all(x, axis, split_axis=0, concat_axis=0, tiled=True)  26.2 us
    ppermute x11, waiting for transfers between devices, shift(): return lax.ppermute(x, axis, [(i, (i + by) % n) for i in range(n)])  14.2 us
    all_to_all x1, blocking collectives, swap(): return lax.all_to_all(x, axis, split_axis=0, concat_axis=0, tiled=True)  11.7 us
    pallas_call x1, Pallas kernels, on_device(): call(functools.partial(grads_kernel, chunk=chunk), [SMEM] + [VMEM] * 6, [...  5.97 us
    pallas_call x1, Pallas kernels, on_device(): call(functools.partial(stats_kernel, chunk=chunk), [SMEM] + [VMEM] * 5, [...  2.53 us
    all_to_all x2, waiting for transfers between devices, swap(): return lax.all_to_all(x, axis, split_axis=0, concat_axis=0, tiled=True)  2.43 us
  transfers between devices with their start and end apart: 13, of which 5 were waited for; matrix products, arithmetic and copies ran while one was open for 0% of the time, Pallas kernels for 0%

profile of v3, /device:TPU:8, one launch (start us, length us, event | category | flops | bytes accessed | tf_op | source)
XLA Modules:
  0.0 98.2 jit_solution(8431510965202491634)
XLA Ops:
  0.6 1.6 %shard_map.85 = (bf16[1,264,128]{2,1,0:T(8,128)(2,1)}, bf16[32,40,128]{2,1,0:T(8,128)(2,1)}) custom-call(s32[16]{0:T(128)} %pos_any.1, s32[16]{0:T(128)} %doc_any.1, bf16[16,1024]{1,0:T(8,128)(2,1)} %q_any.1, bf16[16,1024]{1,0:T(8,128)(2,1)} %g_any.1, bf16[16,128]{1,0:T(8,128)(2,1)} %k_any.1, bf16[16,128]{1,0:T(8,128)(2,1)} %v_any.1), custom_call_target="tpu_custom_call" | custom-call | tf_op jit(solution)/shard_map/pallas_call | solution.py:262
  2.3 4.7 %collective-permute-start.2 = (bf16[1,264,128]{2,1,0:T(8,128)(2,1)}, bf16[1,264,128]{2,1,0:T(8,128)(2,1)S(1)}, u32[]{:S(2)}, u32[]{:S(2)}) collective-permute-start(bf16[1,264,128]{2,1,0:T(8,128)(2,1)} %get-tuple-element.9), channel_id=1, source_target_pairs={{0,384},{128,0},{256,128},{384,256},{1,385},{129,1},{257,129},{385... | collective-permute-start | bytes 202760 | tf_op jit(solution)/shard_map/ppermute | solution.py:258
  6.9 2.7 %collective-permute-start.1 = (bf16[1,264,128]{2,1,0:T(8,128)(2,1)}, bf16[1,264,128]{2,1,0:T(8,128)(2,1)S(1)}, u32[]{:S(2)}, u32[]{:S(2)}) collective-permute-start(bf16[1,264,128]{2,1,0:T(8,128)(2,1)} %get-tuple-element.9), channel_id=1, source_target_pairs={{0,256},{128,384},{256,0},{384,128},{1,257},{129,385},{257,1},{385... | collective-permute-start | bytes 202760 | tf_op jit(solution)/shard_map/ppermute | solution.py:258
  9.7 2.8 %collective-permute-start = (bf16[1,264,128]{2,1,0:T(8,128)(2,1)}, bf16[1,264,128]{2,1,0:T(8,128)(2,1)S(1)}, u32[]{:S(2)}, u32[]{:S(2)}) collective-permute-start(bf16[1,264,128]{2,1,0:T(8,128)(2,1)} %get-tuple-element.9), channel_id=1, source_target_pairs={{0,128},{128,256},{256,384},{384,0},{1,129},{129,257},{257,385},{3... | collective-permute-start | bytes 202760 | tf_op jit(solution)/shard_map/ppermute | solution.py:258
  12.5 0.0 copy-start
  12.5 15.2 %all-to-all-start = ((bf16[32,40,128]{2,1,0:T(8,128)(2,1)}), bf16[32,40,128]{2,1,0:T(8,128)(2,1)S(1)}, u32[]{:S(2)}, u32[]{:S(2)}) async-start(bf16[32,40,128]{2,1,0:T(8,128)(2,1)} %get-tuple-element.10), calls=%async_computation | async-start | bytes 655360 | tf_op jit(solution)/shard_map/all_to_all | solution.py:254
  27.7 0.0 copy-done
  27.7 0.0 collective-permute-done
  27.7 0.0 collective-permute-done.1
  27.8 0.0 collective-permute-done.2
  27.8 3.3 %collective-permute-start.3 = (bf16[4,264,128]{2,1,0:T(8,128)(2,1)S(1)}, bf16[4,264,128]{2,1,0:T(8,128)(2,1)S(1)}, u32[]{:S(2)}, u32[]{:S(2)}) collective-permute-start(bf16[4,264,128]{2,1,0:T(8,128)(2,1)S(1)} %constant_dynamic-update-slice_fusion.refs_0_), channel_id=1, source_target_pairs={{0,64},{64,0},{1,65},{65,1},{2,66},{66,2},{3,67},{67,3},{4,68},{68... | collective-permute-start | bytes 811016 | tf_op jit(solution)/shard_map/ppermute | solution.py:258
  31.1 1.9 %collective-permute-start.4 = (bf16[4,264,128]{2,1,0:T(8,128)(2,1)S(1)}, bf16[4,264,128]{2,1,0:T(8,128)(2,1)S(1)}, u32[]{:S(2)}, u32[]{:S(2)}) collective-permute-start(bf16[4,264,128]{2,1,0:T(8,128)(2,1)S(1)} %constant_dynamic-update-slice_fusion.refs_0_), channel_id=1, source_target_pairs={{0,1},{1,0},{2,3},{3,2},{4,5},{5,4},{6,7},{7,6},{8,9},{9,8},{10,11... | collective-permute-start | bytes 811016 | tf_op jit(solution)/shard_map/ppermute | solution.py:258
  33.0 8.6 %collective-permute-done.3.refs_1_ = bf16[4,264,128]{2,1,0:T(8,128)(2,1)S(1)} collective-permute-done((bf16[4,264,128]{2,1,0:T(8,128)(2,1)S(1)}, bf16[4,264,128]{2,1,0:T(8,128)(2,1)S(1)}, u32[]{:S(2)}, u32[]{:S(2)}) %collective-permute-start.3) | collective-permute-done | bytes 270368 | tf_op jit(solution)/shard_map/ppermute | solution.py:258
  41.6 1.9 %collective-permute-start.5 = (bf16[4,264,128]{2,1,0:T(8,128)(2,1)S(1)}, bf16[4,264,128]{2,1,0:T(8,128)(2,1)S(1)}, u32[]{:S(2)}, u32[]{:S(2)}) collective-permute-start(bf16[4,264,128]{2,1,0:T(8,128)(2,1)S(1)} %collective-permute-done.3.refs_1_), channel_id=1, source_target_pairs={{0,1},{1,0},{2,3},{3,2},{4,5},{5,4},{6,7},{7,6},{8,9},{9,8},{10,11... | collective-permute-start | bytes 811016 | tf_op jit(solution)/shard_map/ppermute | solution.py:258
  43.5 0.0 collective-permute-done.4.refs_2_
  43.5 1.5 %collective-permute-done.5.refs_3_ = bf16[4,264,128]{2,1,0:T(8,128)(2,1)S(1)} collective-permute-done((bf16[4,264,128]{2,1,0:T(8,128)(2,1)S(1)}, bf16[4,264,128]{2,1,0:T(8,128)(2,1)S(1)}, u32[]{:S(2)}, u32[]{:S(2)}) %collective-permute-start.5) | collective-permute-done | bytes 270368 | tf_op jit(solution)/shard_map/ppermute | solution.py:258
  45.0 0.0 all-to-all-done.refs_4_
  45.0 2.5 %shard_map.86 = f32[16,32,128]{2,1,0:T(8,128)S(1)} custom-call(s32[1]{0:T(128)} %bitcast.place_ref, bf16[4,264,128]{2,1,0:T(8,128)(2,1)S(1)} %constant_dynamic-update-slice_fusion.refs_0_, bf16[4,264,128]{2,1,0:T(8,128)(2,1)S(1)} %collective-permute-done.3.refs_1_, bf16[4,264,128]{2,1,0:T(8,128)(2,1)S(1)} %collective-permute-done.4.refs_2_, ...), custom_call_target="tpu_custom_call" | custom-call | tf_op jit(solution)/shard_map/pallas_call | solution.py:274
  47.6 11.7 %all_to_all.15.refs_5_ = f32[16,32,128]{2,1,0:T(8,128)S(1)} all-to-all(f32[16,32,128]{2,1,0:T(8,128)S(1)} %shard_map.86), channel_id=1, replica_groups=mesh['x'=4,'near'=2,'far'=32,'core'=2] {'x','near','core'}, dimensions={0} | all-to-all | bytes 524288 | tf_op jit(solution)/shard_map/all_to_all | solution.py:254
  59.3 6.0 %shard_map.87 = (f32[4,128,128]{2,1,0:T(8,128)S(1)}, f32[4,128,128]{2,1,0:T(8,128)S(1)}, bf16[8,128,128]{2,1,0:T(8,128)(2,1)S(1)}, bf16[32,32,128]{2,1,0:T(8,128)(2,1)}) custom-call(s32[1]{0:T(128)} %bitcast.place_ref, bf16[4,264,128]{2,1,0:T(8,128)(2,1)S(1)} %constant_dynamic-update-slice_fusion.refs_0_, ...), custom_call_target="tpu_custom_call" | custom-call | tf_op jit(solution)/shard_map/pallas_call | solution.py:281
  65.2 2.0 %collective-permute-start.6 = (bf16[8,128,128]{2,1,0:T(8,128)(2,1)S(1)}, bf16[8,128,128]{2,1,0:T(8,128)(2,1)S(1)}, u32[]{:S(2)}, u32[]{:S(2)}) collective-permute-start(bf16[8,128,128]{2,1,0:T(8,128)(2,1)S(1)} %get-tuple-element.12), channel_id=1, source_target_pairs={{0,1},{1,0},{2,3},{3,2},{4,5},{5,4},{6,7},{7,6},{8,9},{9,8},{10,11... | collective-permute-start | bytes 786440 | tf_op jit(solution)/shard_map/ppermute | solution.py:258
  67.3 1.4 %collective-permute-done.6 = bf16[8,128,128]{2,1,0:T(8,128)(2,1)S(1)} collective-permute-done((bf16[8,128,128]{2,1,0:T(8,128)(2,1)S(1)}, bf16[8,128,128]{2,1,0:T(8,128)(2,1)S(1)}, u32[]{:S(2)}, u32[]{:S(2)}) %collective-permute-start.6) | collective-permute-done | bytes 262176 | tf_op jit(solution)/shard_map/ppermute | solution.py:258
  68.7 3.3 %collective-permute-start.7 = (bf16[4,128,128]{2,1,0:T(8,128)(2,1)S(1)}, bf16[4,128,128]{2,1,0:T(8,128)(2,1)S(1)}, u32[]{:S(2)}, u32[]{:S(2)}) collective-permute-start(bf16[4,128,128]{2,1,0:T(8,128)(2,1)S(1)} %fusion), channel_id=1, source_target_pairs={{0,64},{64,0},{1,65},{65,1},{2,66},{66,2},{3,67},{67,3},{4,68},{68... | collective-permute-start | bytes 393224 | tf_op jit(solution)/shard_map/ppermute | solution.py:258
  72.0 11.0 %all-to-all-start.2 = ((bf16[32,32,128]{2,1,0:T(8,128)(2,1)}), bf16[32,32,128]{2,1,0:T(8,128)(2,1)S(1)}, u32[]{:S(2)}, u32[]{:S(2)}) async-start(bf16[32,32,128]{2,1,0:T(8,128)(2,1)} %get-tuple-element.14), calls=%async_computation.2 | async-start | bytes 524288 | tf_op jit(solution)/shard_map/all_to_all | solution.py:254
  83.0 0.0 collective-permute-done.7
  83.1 1.9 %collective-permute-start.10 = (bf16[128,128]{1,0:T(8,128)(2,1)S(1)}, bf16[128,128]{1,0:T(8,128)(2,1)S(1)}, u32[]{:S(2)}, u32[]{:S(2)}) collective-permute-start(bf16[128,128]{1,0:T(8,128)(2,1)S(1)} %get-tuple-element.17), channel_id=1, source_target_pairs={{0,128},{128,256},{256,384},{384,0},{1,129},{129,257},{257,385},{3... | collective-permute-start | bytes 98312 | tf_op jit(solution)/shard_map/ppermute | solution.py:258
  85.1 4.2 %collective-permute-start.9 = (bf16[128,128]{1,0:T(8,128)(2,1)S(1)}, bf16[128,128]{1,0:T(8,128)(2,1)S(1)}, u32[]{:S(2)}, u32[]{:S(2)}) collective-permute-start(bf16[128,128]{1,0:T(8,128)(2,1)S(1)} %get-tuple-element.18), channel_id=1, source_target_pairs={{0,256},{128,384},{256,0},{384,128},{1,257},{129,385},{257,1},{385... | collective-permute-start | bytes 98312 | tf_op jit(solution)/shard_map/ppermute | solution.py:258
  89.3 3.1 %collective-permute-start.8 = (bf16[128,128]{1,0:T(8,128)(2,1)S(1)}, bf16[128,128]{1,0:T(8,128)(2,1)S(1)}, u32[]{:S(2)}, u32[]{:S(2)}) collective-permute-start(bf16[128,128]{1,0:T(8,128)(2,1)S(1)} %get-tuple-element.19), channel_id=1, source_target_pairs={{0,384},{128,0},{256,128},{384,256},{1,385},{129,1},{257,129},{385... | collective-permute-start | bytes 98312 | tf_op jit(solution)/shard_map/ppermute | solution.py:258
  92.4 0.0 collective-permute-done.10.refs_3_
  92.4 0.0 collective-permute-done.9.refs_2_
  92.4 2.7 %collective-permute-done.8.refs_1_ = bf16[128,128]{1,0:T(8,128)(2,1)S(1)} collective-permute-done((bf16[128,128]{1,0:T(8,128)(2,1)S(1)}, bf16[128,128]{1,0:T(8,128)(2,1)S(1)}, u32[]{:S(2)}, u32[]{:S(2)}) %collective-permute-start.8) | collective-permute-done | bytes 32800 | tf_op jit(solution)/shard_map/ppermute | solution.py:258
  95.1 2.4 %all-to-all-done.2.refs_4_ = bf16[32,32,128]{2,1,0:T(8,128)(2,1)S(1)} async-done(((bf16[32,32,128]{2,1,0:T(8,128)(2,1)}), bf16[32,32,128]{2,1,0:T(8,128)(2,1)S(1)}, u32[]{:S(2)}, u32[]{:S(2)}) %all-to-all-start.2) | async-done | bytes 262176 | tf_op jit(solution)/shard_map/all_to_all | solution.py:254
  97.5 0.7 shard_map.88
  (9 shorter events, 0.2 us)
Async XLA Ops:
  2.3 25.5 %collective-permute-start.2 = (bf16[1,264,128]{2,1,0:T(8,128)(2,1)}, bf16[1,264,128]{2,1,0:T(8,128)(2,1)S(1)}, u32[]{:S(2)}, u32[]{:S(2)}) collective-permute-start(bf16[1,264,128]{2,1,0:T(8,128)(2,1)} %get-tuple-element.9), channel_id=1, source_target_pairs={{0,384},{128,0},{256,128},{384,256},{1,385},{129,1},{257,129},{385... | collective-permute-start | bytes 202760 | tf_op jit(solution)/shard_map/ppermute | solution.py:258
  6.9 20.8 %collective-permute-start.1 = (bf16[1,264,128]{2,1,0:T(8,128)(2,1)}, bf16[1,264,128]{2,1,0:T(8,128)(2,1)S(1)}, u32[]{:S(2)}, u32[]{:S(2)}) collective-permute-start(bf16[1,264,128]{2,1,0:T(8,128)(2,1)} %get-tuple-element.9), channel_id=1, source_target_pairs={{0,256},{128,384},{256,0},{384,128},{1,257},{129,385},{257,1},{385... | collective-permute-start | bytes 202760 | tf_op jit(solution)/shard_map/ppermute | solution.py:258
  9.7 18.1 %collective-permute-start = (bf16[1,264,128]{2,1,0:T(8,128)(2,1)}, bf16[1,264,128]{2,1,0:T(8,128)(2,1)S(1)}, u32[]{:S(2)}, u32[]{:S(2)}) collective-permute-start(bf16[1,264,128]{2,1,0:T(8,128)(2,1)} %get-tuple-element.9), channel_id=1, source_target_pairs={{0,128},{128,256},{256,384},{384,0},{1,129},{129,257},{257,385},{3... | collective-permute-start | bytes 202760 | tf_op jit(solution)/shard_map/ppermute | solution.py:258
  12.5 15.2 %copy-start = (bf16[1,264,128]{2,1,0:T(8,128)(2,1)S(1)}, bf16[1,264,128]{2,1,0:T(8,128)(2,1)}, u32[]{:S(2)}) copy-start(bf16[1,264,128]{2,1,0:T(8,128)(2,1)} %get-tuple-element.9) | copy-start | bytes 202756
  12.5 32.6 %all-to-all-start = ((bf16[32,40,128]{2,1,0:T(8,128)(2,1)}), bf16[32,40,128]{2,1,0:T(8,128)(2,1)S(1)}, u32[]{:S(2)}, u32[]{:S(2)}) async-start(bf16[32,40,128]{2,1,0:T(8,128)(2,1)} %get-tuple-element.10), calls=%async_computation | async-start | bytes 655360 | tf_op jit(solution)/shard_map/all_to_all | solution.py:254
  27.8 13.8 %collective-permute-start.3 = (bf16[4,264,128]{2,1,0:T(8,128)(2,1)S(1)}, bf16[4,264,128]{2,1,0:T(8,128)(2,1)S(1)}, u32[]{:S(2)}, u32[]{:S(2)}) collective-permute-start(bf16[4,264,128]{2,1,0:T(8,128)(2,1)S(1)} %constant_dynamic-update-slice_fusion.refs_0_), channel_id=1, source_target_pairs={{0,64},{64,0},{1,65},{65,1},{2,66},{66,2},{3,67},{67,3},{4,68},{68... | collective-permute-start | bytes 811016 | tf_op jit(solution)/shard_map/ppermute | solution.py:258
  31.1 12.5 %collective-permute-start.4 = (bf16[4,264,128]{2,1,0:T(8,128)(2,1)S(1)}, bf16[4,264,128]{2,1,0:T(8,128)(2,1)S(1)}, u32[]{:S(2)}, u32[]{:S(2)}) collective-permute-start(bf16[4,264,128]{2,1,0:T(8,128)(2,1)S(1)} %constant_dynamic-update-slice_fusion.refs_0_), channel_id=1, source_target_pairs={{0,1},{1,0},{2,3},{3,2},{4,5},{5,4},{6,7},{7,6},{8,9},{9,8},{10,11... | collective-permute-start | bytes 811016 | tf_op jit(solution)/shard_map/ppermute | solution.py:258
  41.6 3.4 %collective-permute-start.5 = (bf16[4,264,128]{2,1,0:T(8,128)(2,1)S(1)}, bf16[4,264,128]{2,1,0:T(8,128)(2,1)S(1)}, u32[]{:S(2)}, u32[]{:S(2)}) collective-permute-start(bf16[4,264,128]{2,1,0:T(8,128)(2,1)S(1)} %collective-permute-done.3.refs_1_), channel_id=1, source_target_pairs={{0,1},{1,0},{2,3},{3,2},{4,5},{5,4},{6,7},{7,6},{8,9},{9,8},{10,11... | collective-permute-start | bytes 811016 | tf_op jit(solution)/shard_map/ppermute | solution.py:258
  65.2 3.4 %collective-permute-start.6 = (bf16[8,128,128]{2,1,0:T(8,128)(2,1)S(1)}, bf16[8,128,128]{2,1,0:T(8,128)(2,1)S(1)}, u32[]{:S(2)}, u32[]{:S(2)}) collective-permute-start(bf16[8,128,128]{2,1,0:T(8,128)(2,1)S(1)} %get-tuple-element.12), channel_id=1, source_target_pairs={{0,1},{1,0},{2,3},{3,2},{4,5},{5,4},{6,7},{7,6},{8,9},{9,8},{10,11... | collective-permute-start | bytes 786440 | tf_op jit(solution)/shard_map/ppermute | solution.py:258
  68.7 14.3 %collective-permute-start.7 = (bf16[4,128,128]{2,1,0:T(8,128)(2,1)S(1)}, bf16[4,128,128]{2,1,0:T(8,128)(2,1)S(1)}, u32[]{:S(2)}, u32[]{:S(2)}) collective-permute-start(bf16[4,128,128]{2,1,0:T(8,128)(2,1)S(1)} %fusion), channel_id=1, source_target_pairs={{0,64},{64,0},{1,65},{65,1},{2,66},{66,2},{3,67},{67,3},{4,68},{68... | collective-permute-start | bytes 393224 | tf_op jit(solution)/shard_map/ppermute | solution.py:258
  72.0 25.5 %all-to-all-start.2 = ((bf16[32,32,128]{2,1,0:T(8,128)(2,1)}), bf16[32,32,128]{2,1,0:T(8,128)(2,1)S(1)}, u32[]{:S(2)}, u32[]{:S(2)}) async-start(bf16[32,32,128]{2,1,0:T(8,128)(2,1)} %get-tuple-element.14), calls=%async_computation.2 | async-start | bytes 524288 | tf_op jit(solution)/shard_map/all_to_all | solution.py:254
  83.1 9.2 %collective-permute-start.10 = (bf16[128,128]{1,0:T(8,128)(2,1)S(1)}, bf16[128,128]{1,0:T(8,128)(2,1)S(1)}, u32[]{:S(2)}, u32[]{:S(2)}) collective-permute-start(bf16[128,128]{1,0:T(8,128)(2,1)S(1)} %get-tuple-element.17), channel_id=1, source_target_pairs={{0,128},{128,256},{256,384},{384,0},{1,129},{129,257},{257,385},{3... | collective-permute-start | bytes 98312 | tf_op jit(solution)/shard_map/ppermute | solution.py:258
  85.1 7.3 %collective-permute-start.9 = (bf16[128,128]{1,0:T(8,128)(2,1)S(1)}, bf16[128,128]{1,0:T(8,128)(2,1)S(1)}, u32[]{:S(2)}, u32[]{:S(2)}) collective-permute-start(bf16[128,128]{1,0:T(8,128)(2,1)S(1)} %get-tuple-element.18), channel_id=1, source_target_pairs={{0,256},{128,384},{256,0},{384,128},{1,257},{129,385},{257,1},{385... | collective-permute-start | bytes 98312 | tf_op jit(solution)/shard_map/ppermute | solution.py:258
  89.3 5.8 %collective-permute-start.8 = (bf16[128,128]{1,0:T(8,128)(2,1)S(1)}, bf16[128,128]{1,0:T(8,128)(2,1)S(1)}, u32[]{:S(2)}, u32[]{:S(2)}) collective-permute-start(bf16[128,128]{1,0:T(8,128)(2,1)S(1)} %get-tuple-element.19), channel_id=1, source_target_pairs={{0,384},{128,0},{256,128},{384,256},{1,385},{129,1},{257,129},{385... | collective-permute-start | bytes 98312 | tf_op jit(solution)/shard_map/ppermute | solution.py:258

commit v4 on v2

--- a/solution.py
+++ b/solution.py
@@ -1,4 +1,3 @@
-import functools
 import math
 
 import jax
@@ -100,99 +99,91 @@
     return base, base + meta[1:2] * (run * 16.0) + meta[2:3] * float(run) + tok
 
 
-def stats_kernel(side_ref, qa_ref, qb_ref, kp_ref, out_ref, code_ref, *, chunk):
+def blocks(qa_ref, qb_ref, side):
+    n_q = qa_ref.shape[0]
+    for d in range(0, 2 * n_q, 2):
+        ref, at = (qa_ref, d) if d < n_q else (qb_ref, d - n_q)
+        yield ref, at, d, (side if d < n_q else 1 - side) * n_q + at
+
+
+def stats_kernel(side_ref, qa_ref, qb_ref, kp_ref, out_ref, e_ref, dp_ref, top_ref, code_ref):
     n_q, block, hd = qa_ref.shape
     n_k = kp_ref.shape[0]
     rows = (block - META) // 2
     run = (kp_ref.shape[1] - META) // 2
     scale = 1.0 / math.sqrt(hd)
-    side = side_ref[0]
     code_ref[...] = key_codes(kp_ref, run)
-    per = chunk // run
-    for d in range(0, 2 * n_q, 2):
-        qp_ref, at = (qa_ref, d) if d < n_q else (qb_ref, d - n_q)
-        home = (side if d < n_q else 1 - side) * n_q + at
+    k = kp_ref[:, 0:run, :].reshape(n_k * run, hd)
+    v = kp_ref[:, run : 2 * run, :].reshape(n_k * run, hd)
+    for qp_ref, at, d, home in blocks(qa_ref, qb_ref, side_ref[0]):
         q = qp_ref[at : at + 2, 0:rows, :].reshape(2 * rows, hd)
         g = qp_ref[at : at + 2, rows : 2 * rows, :].reshape(2 * rows, hd)
         pairs = [query_codes(qp_ref, at + i, run) for i in range(2)]
         base = jnp.concatenate([p[0] for p in pairs], axis=1)
         top = jnp.concatenate([p[1] for p in pairs], axis=1)
-        high = jnp.full((1, 2 * rows), FLOOR, jnp.float32)
-        total = jnp.zeros((1, 2 * rows), jnp.float32)
-        cross = jnp.zeros((1, 2 * rows), jnp.float32)
-        for c in range(n_k // per):
-            k = kp_ref[c * per : (c + 1) * per, 0:run, :].reshape(chunk, hd)
-            v = kp_ref[c * per : (c + 1) * per, run : 2 * run, :].reshape(chunk, hd)
-            code = code_ref[c * chunk : (c + 1) * chunk, :]
-            code = jnp.concatenate([code] * (2 * rows // hd), axis=1)
-            seen = (code <= top) & (code >= base)
-            s = jnp.where(seen, dot_rows(k, q) * scale, LOW)
-            dp = dot_rows(v, g)
-            new = jnp.maximum(high, jnp.max(s, axis=0, keepdims=True))
-            w = jnp.exp(s - new)
-            keep = jnp.exp(high - new)
-            total = total * keep + jnp.sum(w, axis=0, keepdims=True)
-            cross = cross * keep + jnp.sum(w * dp, axis=0, keepdims=True)
-            high = new
+        code = jnp.concatenate([code_ref[...]] * (2 * rows // hd), axis=1)
+        seen = (code <= top) & (code >= base)
+        s = jnp.where(seen, dot_rows(k, q) * scale, LOW)
+        dp = dot_rows(v, g)
+        high = jnp.maximum(jnp.max(s, axis=0, keepdims=True), FLOOR)
+        e = jnp.exp(s - high)
+        cols = slice(d * rows, (d + 2) * rows)
+        e_ref[:, cols] = e
+        dp_ref[:, cols] = dp
+        total = jnp.sum(e, axis=0, keepdims=True)
+        cross = jnp.sum(e * dp, axis=0, keepdims=True)
         some = total > 0.0
         safe = jnp.where(some, total, 1.0)
         log_total = jnp.where(some, high + jnp.log(safe), LOW)
         row_dot = jnp.where(some, cross / safe, 0.0)
         for i in range(2):
+            lo, hi = i * rows, (i + 1) * rows
+            top_ref[d + i : d + i + 1, :] = high[:, lo:hi]
             for to in range(out_ref.shape[0]):
-                lo, hi = i * rows, (i + 1) * rows
                 out_ref[to, pl.ds(home + i, 1), :] = log_total[:, lo:hi]
                 out_ref[to, pl.ds(2 * n_q + home + i, 1), :] = row_dot[:, lo:hi]
 
 
-def grads_kernel(
-    side_ref, qa_ref, qb_ref, kp_ref, st_ref, own_ref, oth_ref, gkv_ref, code_ref, log_ref, dot_ref, acc_ref, *, chunk
-):
+def keys_kernel(side_ref, qa_ref, qb_ref, st_ref, e_ref, dp_ref, top_ref, gkv_ref, ds_ref, log_ref, dot_ref):
     n_q, block, hd = qa_ref.shape
-    n_k = kp_ref.shape[0]
+    n_k, twice, _ = gkv_ref.shape
+    run = twice // 2
     rows = (block - META) // 2
-    run = (kp_ref.shape[1] - META) // 2
     scale = 1.0 / math.sqrt(hd)
-    side = side_ref[0]
-    code_ref[...] = key_codes(kp_ref, run)
     logs = st_ref[:, 0 : 2 * n_q, :]
     high = jnp.max(logs, axis=0)
     log_total = high + jnp.log(jnp.sum(jnp.exp(logs - high[None]), axis=0))
     log_ref[...] = log_total
     dot_ref[...] = jnp.sum(jnp.exp(logs - log_total[None]) * st_ref[:, 2 * n_q :, :], axis=0)
-    per = chunk // run
-    for d in range(0, 2 * n_q, 2):
-        qp_ref, at, gq_ref = (qa_ref, d, own_ref) if d < n_q else (qb_ref, d - n_q, oth_ref)
-        home = (side if d < n_q else 1 - side) * n_q + at
+    gk = jnp.zeros((n_k * run, hd), jnp.float32)
+    gv = jnp.zeros((n_k * run, hd), jnp.float32)
+    for qp_ref, at, d, home in blocks(qa_ref, qb_ref, side_ref[0]):
         q = qp_ref[at : at + 2, 0:rows, :].reshape(2 * rows, hd)
         g = qp_ref[at : at + 2, rows : 2 * rows, :].reshape(2 * rows, hd)
-        pairs = [query_codes(qp_ref, at + i, run) for i in range(2)]
-        base = jnp.concatenate([p[0] for p in pairs], axis=1)
-        top = jnp.concatenate([p[1] for p in pairs], axis=1)
-        log_row = jnp.concatenate([log_ref[pl.ds(home + i, 1), :] for i in range(2)], axis=1)
+        factor = jnp.concatenate(
+            [jnp.exp(top_ref[d + i : d + i + 1, :] - log_ref[pl.ds(home + i, 1), :]) for i in range(2)], axis=1
+        )
         dot_row = jnp.concatenate([dot_ref[pl.ds(home + i, 1), :] for i in range(2)], axis=1)
-        gq = jnp.zeros((2 * rows, hd), jnp.float32)
-        for c in range(n_k // per):
-            k = kp_ref[c * per : (c + 1) * per, 0:run, :].reshape(chunk, hd)
-            v = kp_ref[c * per : (c + 1) * per, run : 2 * run, :].reshape(chunk, hd)
-            code = code_ref[c * chunk : (c + 1) * chunk, :]
-            code = jnp.concatenate([code] * (2 * rows // hd), axis=1)
-            seen = (code <= top) & (code >= base)
-            w = jnp.exp(jnp.where(seen, dot_rows(k, q) * scale, LOW) - log_row)
-            ds = (w * (dot_rows(v, g) - dot_row)).astype(jnp.bfloat16)
-            gq = gq + dot_cols(ds, k)
-            gk = dot_plain(ds, q)
-            gv = dot_plain(w.astype(jnp.bfloat16), g)
-            where = pl.ds(c * chunk, chunk)
-            if d == 0:
-                acc_ref[0, where, :] = gk
-                acc_ref[1, where, :] = gv
-            else:
-                acc_ref[0, where, :] += gk
-                acc_ref[1, where, :] += gv
-        gq_ref[at : at + 2] = (gq * scale).reshape(2, rows, hd).astype(gq_ref.dtype)
-    gkv_ref[:, 0:run, :] = (acc_ref[0] * scale).reshape(n_k, run, hd).astype(gkv_ref.dtype)
-    gkv_ref[:, run:, :] = acc_ref[1].reshape(n_k, run, hd).astype(gkv_ref.dtype)
+        cols = slice(d * rows, (d + 2) * rows)
+        w = e_ref[:, cols] * factor
+        ds = (w * (dp_ref[:, cols] - dot_row)).astype(jnp.bfloat16)
+        ds_ref[:, cols] = ds
+        gk = gk + dot_plain(ds, q)
+        gv = gv + dot_plain(w.astype(jnp.bfloat16), g)
+    gkv_ref[:, 0:run, :] = (gk * scale).reshape(n_k, run, hd).astype(gkv_ref.dtype)
+    gkv_ref[:, run:, :] = gv.reshape(n_k, run, hd).astype(gkv_ref.dtype)
+
+
+def queries_kernel(kp_ref, ds_ref, own_ref, oth_ref):
+    n_q, rows, hd = own_ref.shape
+    n_k = kp_ref.shape[0]
+    run = (kp_ref.shape[1] - META) // 2
+    scale = 1.0 / math.sqrt(hd)
+    k = kp_ref[:, 0:run, :].reshape(n_k * run, hd)
+    for d in list(range(n_q, 2 * n_q, 2)) + list(range(0, n_q, 2)):
+        ref, at = (own_ref, d) if d < n_q else (oth_ref, d - n_q)
+        gq = dot_cols(ds_ref[:, d * rows : (d + 2) * rows], k) * scale
+        ref[at : at + 2] = gq.reshape(2, rows, hd).astype(ref.dtype)
 
 
 def finish_kernel(gq_ref, gkv_ref, oq_ref, ok_ref, ov_ref):
@@ -210,13 +201,14 @@
 HBM = pl.BlockSpec(memory_space=pltpu.HBM)
 
 
-def call(kernel, in_specs, outs, scratch=(), grant=48 * 1024 * 1024):
+def call(kernel, in_specs, outs, scratch=(), grant=16 * 1024 * 1024, cost=0):
     return pl.pallas_call(
         kernel,
         in_specs=in_specs,
         out_specs=[VMEM] * len(outs),
         out_shape=outs,
         scratch_shapes=list(scratch),
+        cost_estimate=pl.CostEstimate(flops=cost, bytes_accessed=0, transcendentals=0) if cost else None,
         compiler_params=pltpu.CompilerParams(vmem_limit_bytes=grant),
     )
 
@@ -228,7 +220,6 @@
     rows = run * heads
     bf, f32 = jnp.bfloat16, jnp.float32
     keys = n_k * run
-    chunk = min(256, keys)
     struct = jax.ShapeDtypeStruct
 
     def swap(x, axis):
@@ -250,24 +241,27 @@
     qa = swap(qp, "head")
     qb = other(qa)
     kp = swap(kp, "far")
-    (st,) = call(
-        functools.partial(stats_kernel, chunk=chunk),
+    full = struct((keys, sides * n_q * rows), f32)
+    line = struct((sides * n_q, rows), f32)
+    st, e, dp, top = call(
+        stats_kernel,
         [SMEM] + [VMEM] * 3,
-        [struct((sides * n_q, 2 * sides * n_q, rows), f32)],
+        [struct((sides * n_q, 2 * sides * n_q, rows), f32), full, full, line],
         [pltpu.VMEM((keys, hd), f32)],
     )(side, qa, qb, kp)
     st = swap(st, ("head", "core"))
-    own, oth, gkv = call(
-        functools.partial(grads_kernel, chunk=chunk),
-        [SMEM] + [VMEM] * 4,
-        [struct((n_q, rows, hd), f32), struct((n_q, rows, hd), bf), struct((n_k, 2 * run, hd), bf)],
-        [
-            pltpu.VMEM((keys, hd), f32),
-            pltpu.VMEM((sides * n_q, rows), f32),
-            pltpu.VMEM((sides * n_q, rows), f32),
-            pltpu.VMEM((2, keys, hd), f32),
-        ],
-    )(side, qa, qb, kp, st)
+    gkv, ds = call(
+        keys_kernel,
+        [SMEM] + [VMEM] * 6,
+        [struct((n_k, 2 * run, hd), bf), struct(full.shape, bf)],
+        [pltpu.VMEM(line.shape, f32), pltpu.VMEM(line.shape, f32)],
+    )(side, qa, qb, st, e, dp, top)
+    own, oth = call(
+        queries_kernel,
+        [VMEM] * 2,
+        [struct((n_q, rows, hd), f32), struct((n_q, rows, hd), bf)],
+        cost=2 * keys * sides * n_q * rows * hd,
+    )(kp, ds)
     oth = other(oth)
     gkv = swap(gkv, "far")
     gq = (own + oth.astype(f32)).astype(bf)

time: 98.8 us -> 96.1 us (0.973)
  Pallas kernels: 11 us -> 8.24 us
    pallas_call x2 -> x3, Pallas kernels: 8.45 us -> 5.67 us  [the longest x1 2.8 us: on_device(): call(stats_kernel, [SMEM] + [VMEM] * 3, [struct((sides * n_q, 2 * sides *...]
where the time goes in v4:
time: 96.1 us; the launch traced here: 95.6 us
  blocking collectives  37.3 us (39%)
  waiting for transfers between devices  25.2 us (26%)
  starting transfers between devices  24.1 us (25%)
  Pallas kernels  8.24 us (9%)
    all_to_all x3, blocking collectives, swap(): return lax.all_to_all(x, axis, split_axis=0, concat_axis=0, tiled=True)  37.3 us
    all_to_all x2, waiting for transfers between devices, swap(): return lax.all_to_all(x, axis, split_axis=0, concat_axis=0, tiled=True)  25.2 us
    all_to_all x2, starting transfers between devices, swap(): return lax.all_to_all(x, axis, split_axis=0, concat_axis=0, tiled=True)  20.2 us
    ppermute x2, starting transfers between devices, other(): return lax.ppermute(x, 'core', [(0, 1), (1, 0)])  3.84 us
    pallas_call x1, Pallas kernels, on_device(): call(stats_kernel, [SMEM] + [VMEM] * 3, [struct((sides * n_q, 2 * sides *...  2.8 us
    pallas_call x1, Pallas kernels, on_device(): call(keys_kernel, [SMEM] + [VMEM] * 6, [struct((n_k, 2 * run, hd), bf), s...  2.05 us
  transfers between devices with their start and end apart: 4, of which 2 were waited for; matrix products, arithmetic and copies ran while one was open for 0% of the time, Pallas kernels for 0%

profile of v4, /device:TPU:16, one launch (start us, length us, event | category | flops | bytes accessed | tf_op | source)
XLA Modules:
  0.0 95.6 jit_solution(711926578293641177)
XLA Ops:
  0.6 1.9 %shard_map.85 = (bf16[8,264,128]{2,1,0:T(8,128)(2,1)}, bf16[32,40,128]{2,1,0:T(8,128)(2,1)}) custom-call(s32[16]{0:T(128)} %pos_any.1, s32[16]{0:T(128)} %doc_any.1, bf16[16,1024]{1,0:T(8,128)(2,1)} %q_any.1, bf16[16,1024]{1,0:T(8,128)(2,1)} %g_any.1, bf16[16,128]{1,0:T(8,128)(2,1)} %k_any.1, bf16[16,128]{1,0:T(8,128)(2,1)} %v_any.1), custom_call_target="tpu_custom_call" | custom-call | tf_op jit(solution)/shard_map/pallas_call | solution.py:233
  2.5 15.8 %all_to_all.25.qa_ref = bf16[8,264,128]{2,1,0:T(8,128)(2,1)S(1)} all-to-all(bf16[8,264,128]{2,1,0:T(8,128)(2,1)} %get-tuple-element.14), channel_id=1, replica_groups=mesh['head'=8,'far'=32,'core'=2] {'head'}, dimensions={0} | all-to-all | bytes 1081344 | tf_op jit(solution)/shard_map/all_to_all | solution.py:226
  18.3 15.2 %all-to-all-start = ((bf16[32,40,128]{2,1,0:T(8,128)(2,1)}), bf16[32,40,128]{2,1,0:T(8,128)(2,1)S(1)}, u32[]{:S(2)}, u32[]{:S(2)}) async-start(bf16[32,40,128]{2,1,0:T(8,128)(2,1)} %get-tuple-element.13), calls=%async_computation | async-start | bytes 655360 | tf_op jit(solution)/shard_map/all_to_all | solution.py:226
  33.5 1.9 %collective-permute-start = (bf16[8,264,128]{2,1,0:T(8,128)(2,1)S(1)}, bf16[8,264,128]{2,1,0:T(8,128)(2,1)S(1)}, u32[]{:S(2)}, u32[]{:S(2)}) collective-permute-start(bf16[8,264,128]{2,1,0:T(8,128)(2,1)S(1)} %all_to_all.25.qa_ref), channel_id=1, source_target_pairs={{0,1},{1,0},{2,3},{3,2},{4,5},{5,4},{6,7},{7,6},{8,9},{9,8},{10,11... | collective-permute-start | bytes 1622024 | tf_op jit(solution)/shard_map/ppermute | solution.py:229
  35.4 10.7 %all-to-all-done.kp_ref = bf16[32,40,128]{2,1,0:T(8,128)(2,1)S(1)} async-done(((bf16[32,40,128]{2,1,0:T(8,128)(2,1)}), bf16[32,40,128]{2,1,0:T(8,128)(2,1)S(1)}, u32[]{:S(2)}, u32[]{:S(2)}) %all-to-all-start) | async-done | bytes 327712 | tf_op jit(solution)/shard_map/all_to_all | solution.py:226
  46.1 0.0 collective-permute-done.qb_ref
  46.1 2.8 %shard_map.86 = (f32[16,32,128]{2,1,0:T(8,128)S(1)}, f32[512,2048]{1,0:T(8,128)S(1)}, f32[512,2048]{1,0:T(8,128)S(1)}, f32[16,128]{1,0:T(8,128)S(1)}) custom-call(s32[1]{0:T(128)} %bitcast.side_ref, bf16[8,264,128]{2,1,0:T(8,128)(2,1)S(1)} %all_to_all.25.qa_ref, bf16[8,264,128]{2,1,0:T(8,128)(2,1)S(1)} %collective-permute-done.qb_ref, ...), custom_call_target="tpu_custom_call" | custom-call | tf_op jit(solution)/shard_map/pallas_call | solution.py:246
  48.9 11.8 %all_to_all.26.st_ref = f32[16,32,128]{2,1,0:T(8,128)S(1)} all-to-all(f32[16,32,128]{2,1,0:T(8,128)S(1)} %get-tuple-element.15), channel_id=1, replica_groups=mesh['head'=8,'far'=32,'core'=2] {'head','core'}, dimensions={0} | all-to-all | bytes 524288 | tf_op jit(solution)/shard_map/all_to_all | solution.py:226
  60.7 2.1 %shard_map.87 = (bf16[32,32,128]{2,1,0:T(8,128)(2,1)}, bf16[512,2048]{1,0:T(8,128)(2,1)S(1)}) custom-call(s32[1]{0:T(128)} %bitcast.side_ref, bf16[8,264,128]{2,1,0:T(8,128)(2,1)S(1)} %all_to_all.25.qa_ref, bf16[8,264,128]{2,1,0:T(8,128)(2,1)S(1)} %collective-permute-done.qb_ref, f32[16,32,128]{2,1,0:T(8,128)S(1)} %all_to_all.26.st_ref, ...), custom_call_target="tpu_custom_call" | custom-call | tf_op jit(solution)/shard_map/pallas_call | solution.py:253
  62.8 0.8 shard_map.88
  63.6 1.9 %collective-permute-start.1 = (bf16[8,128,128]{2,1,0:T(8,128)(2,1)S(1)}, bf16[8,128,128]{2,1,0:T(8,128)(2,1)S(1)}, u32[]{:S(2)}, u32[]{:S(2)}) collective-permute-start(bf16[8,128,128]{2,1,0:T(8,128)(2,1)S(1)} %get-tuple-element.21), channel_id=1, source_target_pairs={{0,1},{1,0},{2,3},{3,2},{4,5},{5,4},{6,7},{7,6},{8,9},{9,8},{10,11... | collective-permute-start | bytes 786440 | tf_op jit(solution)/shard_map/ppermute | solution.py:229
  65.5 5.1 %all-to-all-start.4 = ((bf16[32,32,128]{2,1,0:T(8,128)(2,1)}), bf16[32,32,128]{2,1,0:T(8,128)(2,1)S(1)}, u32[]{:S(2)}, u32[]{:S(2)}) async-start(bf16[32,32,128]{2,1,0:T(8,128)(2,1)} %get-tuple-element.22), calls=%async_computation.4 | async-start | bytes 524288 | tf_op jit(solution)/shard_map/all_to_all | solution.py:226
  70.6 0.0 collective-permute-done.1
  70.6 0.1 add_convert_fusion
  70.7 14.6 %all-to-all-done.4.gkv_ref = bf16[32,32,128]{2,1,0:T(8,128)(2,1)S(1)} async-done(((bf16[32,32,128]{2,1,0:T(8,128)(2,1)}), bf16[32,32,128]{2,1,0:T(8,128)(2,1)S(1)}, u32[]{:S(2)}, u32[]{:S(2)}) %all-to-all-start.4) | async-done | bytes 262176 | tf_op jit(solution)/shard_map/all_to_all | solution.py:226
  85.2 9.7 %all_to_all.27.gq_ref = bf16[8,128,128]{2,1,0:T(8,128)(2,1)S(1)} all-to-all(bf16[8,128,128]{2,1,0:T(8,128)(2,1)S(1)} %add_convert_fusion), channel_id=1, replica_groups=mesh['head'=8,'far'=32,'core'=2] {'head'}, dimensions={0} | all-to-all | bytes 524288 | tf_op jit(solution)/shard_map/all_to_all | solution.py:226
  94.9 0.7 shard_map.89
Async XLA Ops:
  18.3 27.8 %all-to-all-start = ((bf16[32,40,128]{2,1,0:T(8,128)(2,1)}), bf16[32,40,128]{2,1,0:T(8,128)(2,1)S(1)}, u32[]{:S(2)}, u32[]{:S(2)}) async-start(bf16[32,40,128]{2,1,0:T(8,128)(2,1)} %get-tuple-element.13), calls=%async_computation | async-start | bytes 655360 | tf_op jit(solution)/shard_map/all_to_all | solution.py:226
  33.5 12.6 %collective-permute-start = (bf16[8,264,128]{2,1,0:T(8,128)(2,1)S(1)}, bf16[8,264,128]{2,1,0:T(8,128)(2,1)S(1)}, u32[]{:S(2)}, u32[]{:S(2)}) collective-permute-start(bf16[8,264,128]{2,1,0:T(8,128)(2,1)S(1)} %all_to_all.25.qa_ref), channel_id=1, source_target_pairs={{0,1},{1,0},{2,3},{3,2},{4,5},{5,4},{6,7},{7,6},{8,9},{9,8},{10,11... | collective-permute-start | bytes 1622024 | tf_op jit(solution)/shard_map/ppermute | solution.py:229
  63.6 7.0 %collective-permute-start.1 = (bf16[8,128,128]{2,1,0:T(8,128)(2,1)S(1)}, bf16[8,128,128]{2,1,0:T(8,128)(2,1)S(1)}, u32[]{:S(2)}, u32[]{:S(2)}) collective-permute-start(bf16[8,128,128]{2,1,0:T(8,128)(2,1)S(1)} %get-tuple-element.21), channel_id=1, source_target_pairs={{0,1},{1,0},{2,3},{3,2},{4,5},{5,4},{6,7},{7,6},{8,9},{9,8},{10,11... | collective-permute-start | bytes 786440 | tf_op jit(solution)/shard_map/ppermute | solution.py:229
  65.5 19.7 %all-to-all-start.4 = ((bf16[32,32,128]{2,1,0:T(8,128)(2,1)}), bf16[32,32,128]{2,1,0:T(8,128)(2,1)S(1)}, u32[]{:S(2)}, u32[]{:S(2)}) async-start(bf16[32,32,128]{2,1,0:T(8,128)(2,1)} %get-tuple-element.22), calls=%async_computation.4 | async-start | bytes 524288 | tf_op jit(solution)/shard_map/all_to_all | solution.py:226

commit v5 on v4

--- a/solution.py
+++ b/solution.py
@@ -262,9 +262,11 @@
         [struct((n_q, rows, hd), f32), struct((n_q, rows, hd), bf)],
         cost=2 * keys * sides * n_q * rows * hd,
     )(kp, ds)
-    oth = other(oth)
     gkv = swap(gkv, "far")
+    both = lax.all_gather(oth, "core", axis=0, tiled=False)
+    oth = jnp.where(side == 0, both[1], both[0])
     gq = (own + oth.astype(f32)).astype(bf)
+    gq, gkv = lax.optimization_barrier((gq, gkv))
     gq = swap(gq, "head")
     return tuple(
         call(

time: 96.1 us -> 92.3 us (0.960)
  waiting for transfers between devices: 25.2 us -> 19 us
  blocking collectives: 37.3 us -> 41.6 us
  starting transfers between devices: 24.1 us -> 22.1 us
    all_to_all x2, waiting for transfers between devices: 25.2 us -> 19 us  [swap(): return lax.all_to_all(x, axis, split_axis=0, concat_axis=0, tiled=True)]
    all_gather x0 -> x1, blocking collectives: none -> 2.18 us  [on_device(): both = lax.all_gather(oth, 'core', axis=0, tiled=False)]
    all_to_all x3, blocking collectives: 37.3 us -> 39.4 us  [swap(): return lax.all_to_all(x, axis, split_axis=0, concat_axis=0, tiled=True)]
    ppermute x2 -> x1, starting transfers between devices: 3.84 us -> 1.92 us  [other(): return lax.ppermute(x, 'core', [(0, 1), (1, 0)])]
  transfers between devices with their start and end apart: 4 -> 3, of which waited for: 2 -> 2; matrix products, arithmetic and copies ran while one was open for 0% -> 0% of each run, Pallas kernels for 0% -> 1%
where the time goes in v5:
time: 92.3 us; the launch traced here: 91.8 us
  blocking collectives  41.6 us (45%)
  starting transfers between devices  22.1 us (24%)
  waiting for transfers between devices  19 us (21%)
  Pallas kernels  7.51 us (8%)
    all_to_all x3, blocking collectives, swap(): return lax.all_to_all(x, axis, split_axis=0, concat_axis=0, tiled=True)  39.4 us
    all_to_all x2, starting transfers between devices, swap(): return lax.all_to_all(x, axis, split_axis=0, concat_axis=0, tiled=True)  20.2 us
    all_to_all x2, waiting for transfers between devices, swap(): return lax.all_to_all(x, axis, split_axis=0, concat_axis=0, tiled=True)  19 us
    pallas_call x1, Pallas kernels, on_device(): call(stats_kernel, [SMEM] + [VMEM] * 3, [struct((sides * n_q, 2 * sides *...  2.79 us
    all_gather x1, blocking collectives, on_device(): both = lax.all_gather(oth, 'core', axis=0, tiled=False)  2.18 us
    ppermute x1, starting transfers between devices, other(): return lax.ppermute(x, 'core', [(0, 1), (1, 0)])  1.92 us
    pallas_call x1, Pallas kernels, on_device(): call(pack_kernel, [HBM] * 6, [struct((n_q, 2 * rows + META, hd), bf), str...  1.87 us
  transfers between devices with their start and end apart: 3, of which 2 were waited for; matrix products, arithmetic and copies ran while one was open for 0% of the time, Pallas kernels for 1%

profile of v5, /device:TPU:16, one launch (start us, length us, event | category | flops | bytes accessed | tf_op | source)
XLA Modules:
  0.0 91.8 jit_solution(11030795481964563983)
XLA Ops:
  0.6 1.9 %shard_map.85 = (bf16[8,264,128]{2,1,0:T(8,128)(2,1)}, bf16[32,40,128]{2,1,0:T(8,128)(2,1)}) custom-call(s32[16]{0:T(128)} %pos_any.1, s32[16]{0:T(128)} %doc_any.1, bf16[16,1024]{1,0:T(8,128)(2,1)} %q_any.1, bf16[16,1024]{1,0:T(8,128)(2,1)} %g_any.1, bf16[16,128]{1,0:T(8,128)(2,1)} %k_any.1, bf16[16,128]{1,0:T(8,128)(2,1)} %v_any.1), custom_call_target="tpu_custom_call" | custom-call | tf_op jit(solution)/shard_map/pallas_call | solution.py:233
  2.5 15.8 %all_to_all.25.qa_ref = bf16[8,264,128]{2,1,0:T(8,128)(2,1)S(1)} all-to-all(bf16[8,264,128]{2,1,0:T(8,128)(2,1)} %get-tuple-element.16), channel_id=1, replica_groups=mesh['head'=8,'far'=32,'core'=2] {'head'}, dimensions={0} | all-to-all | bytes 1081344 | tf_op jit(solution)/shard_map/all_to_all | solution.py:226
  18.3 15.2 %all-to-all-start = ((bf16[32,40,128]{2,1,0:T(8,128)(2,1)}), bf16[32,40,128]{2,1,0:T(8,128)(2,1)S(1)}, u32[]{:S(2)}, u32[]{:S(2)}) async-start(bf16[32,40,128]{2,1,0:T(8,128)(2,1)} %get-tuple-element.15), calls=%async_computation | async-start | bytes 655360 | tf_op jit(solution)/shard_map/all_to_all | solution.py:226
  33.5 1.9 %collective-permute-start = (bf16[8,264,128]{2,1,0:T(8,128)(2,1)S(1)}, bf16[8,264,128]{2,1,0:T(8,128)(2,1)S(1)}, u32[]{:S(2)}, u32[]{:S(2)}) collective-permute-start(bf16[8,264,128]{2,1,0:T(8,128)(2,1)S(1)} %all_to_all.25.qa_ref), channel_id=1, source_target_pairs={{0,1},{1,0},{2,3},{3,2},{4,5},{5,4},{6,7},{7,6},{8,9},{9,8},{10,11... | collective-permute-start | bytes 1622024 | tf_op jit(solution)/shard_map/ppermute | solution.py:229
  35.4 10.7 %all-to-all-done.kp_ref = bf16[32,40,128]{2,1,0:T(8,128)(2,1)S(1)} async-done(((bf16[32,40,128]{2,1,0:T(8,128)(2,1)}), bf16[32,40,128]{2,1,0:T(8,128)(2,1)S(1)}, u32[]{:S(2)}, u32[]{:S(2)}) %all-to-all-start) | async-done | bytes 327712 | tf_op jit(solution)/shard_map/all_to_all | solution.py:226
  46.1 0.0 collective-permute-done.qb_ref
  46.1 2.8 %shard_map.86 = (f32[16,32,128]{2,1,0:T(8,128)S(1)}, f32[512,2048]{1,0:T(8,128)S(1)}, f32[512,2048]{1,0:T(8,128)S(1)}, f32[16,128]{1,0:T(8,128)S(1)}) custom-call(s32[1]{0:T(128)} %bitcast.side_ref, bf16[8,264,128]{2,1,0:T(8,128)(2,1)S(1)} %all_to_all.25.qa_ref, bf16[8,264,128]{2,1,0:T(8,128)(2,1)S(1)} %collective-permute-done.qb_ref, ...), custom_call_target="tpu_custom_call" | custom-call | tf_op jit(solution)/shard_map/pallas_call | solution.py:246
  48.9 11.8 %all_to_all.26.st_ref = f32[16,32,128]{2,1,0:T(8,128)S(1)} all-to-all(f32[16,32,128]{2,1,0:T(8,128)S(1)} %get-tuple-element.17), channel_id=1, replica_groups=mesh['head'=8,'far'=32,'core'=2] {'head','core'}, dimensions={0} | all-to-all | bytes 524288 | tf_op jit(solution)/shard_map/all_to_all | solution.py:226
  60.7 1.3 %shard_map.87 = (bf16[32,32,128]{2,1,0:T(8,128)(2,1)S(1)}, bf16[512,2048]{1,0:T(8,128)(2,1)S(1)}) custom-call(s32[1]{0:T(128)} %bitcast.side_ref, bf16[8,264,128]{2,1,0:T(8,128)(2,1)S(1)} %all_to_all.25.qa_ref, bf16[8,264,128]{2,1,0:T(8,128)(2,1)S(1)} %collective-permute-done.qb_ref, f32[16,32,128]{2,1,0:T(8,128)S(1)} %all_to_all.26.st_ref, ...), custom_call_target="tpu_custom_call" | custom-call | tf_op jit(solution)/shard_map/pallas_call | solution.py:253
  62.0 0.0 copy-start
  62.1 0.7 copy-done
  62.7 5.1 %all-to-all-start.3 = ((bf16[32,32,128]{2,1,0:T(8,128)(2,1)}), bf16[32,32,128]{2,1,0:T(8,128)(2,1)S(1)}, u32[]{:S(2)}, u32[]{:S(2)}) async-start(bf16[32,32,128]{2,1,0:T(8,128)(2,1)} %copy-done), calls=%async_computation.3 | async-start | bytes 524288 | tf_op jit(solution)/shard_map/all_to_all | solution.py:226
  67.8 0.8 shard_map.88
  68.6 2.2 %all-gather = bf16[16,128,128]{2,1,0:T(8,128)(2,1)S(1)} all-gather(bf16[8,128,128]{2,1,0:T(8,128)(2,1)S(1)} %get-tuple-element.23), channel_id=2, replica_groups=mesh['head'=8,'far'=32,'core'=2] {'core'}, dimensions={0}, use_global_device_ids=true | all-gather | bytes 786432 | tf_op jit(solution)/shard_map/all_gather | solution.py:266
  70.8 0.1 fusion
  70.9 8.4 %all-to-all-done.3.gkv_ref = bf16[32,32,128]{2,1,0:T(8,128)(2,1)S(1)} async-done(((bf16[32,32,128]{2,1,0:T(8,128)(2,1)}), bf16[32,32,128]{2,1,0:T(8,128)(2,1)S(1)}, u32[]{:S(2)}, u32[]{:S(2)}) %all-to-all-start.3) | async-done | bytes 262176 | tf_op jit(solution)/shard_map/all_to_all | solution.py:226
  79.3 11.8 %all_to_all.27.gq_ref = bf16[8,128,128]{2,1,0:T(8,128)(2,1)S(1)} all-to-all(bf16[8,128,128]{2,1,0:T(8,128)(2,1)S(1)} %fusion), channel_id=1, replica_groups=mesh['head'=8,'far'=32,'core'=2] {'head'}, dimensions={0} | all-to-all | bytes 524288 | tf_op jit(solution)/shard_map/all_to_all | solution.py:226
  91.1 0.7 shard_map.89
Async XLA Ops:
  18.3 27.8 %all-to-all-start = ((bf16[32,40,128]{2,1,0:T(8,128)(2,1)}), bf16[32,40,128]{2,1,0:T(8,128)(2,1)S(1)}, u32[]{:S(2)}, u32[]{:S(2)}) async-start(bf16[32,40,128]{2,1,0:T(8,128)(2,1)} %get-tuple-element.15), calls=%async_computation | async-start | bytes 655360 | tf_op jit(solution)/shard_map/all_to_all | solution.py:226
  33.5 12.6 %collective-permute-start = (bf16[8,264,128]{2,1,0:T(8,128)(2,1)S(1)}, bf16[8,264,128]{2,1,0:T(8,128)(2,1)S(1)}, u32[]{:S(2)}, u32[]{:S(2)}) collective-permute-start(bf16[8,264,128]{2,1,0:T(8,128)(2,1)S(1)} %all_to_all.25.qa_ref), channel_id=1, source_target_pairs={{0,1},{1,0},{2,3},{3,2},{4,5},{5,4},{6,7},{7,6},{8,9},{9,8},{10,11... | collective-permute-start | bytes 1622024 | tf_op jit(solution)/shard_map/ppermute | solution.py:229
  62.0 0.7 copy-start
  62.7 16.5 %all-to-all-start.3 = ((bf16[32,32,128]{2,1,0:T(8,128)(2,1)}), bf16[32,32,128]{2,1,0:T(8,128)(2,1)S(1)}, u32[]{:S(2)}, u32[]{:S(2)}) async-start(bf16[32,32,128]{2,1,0:T(8,128)(2,1)} %copy-done), calls=%async_computation.3 | async-start | bytes 524288 | tf_op jit(solution)/shard_map/all_to_all | solution.py:226

commit v6 on v5

--- a/solution.py
+++ b/solution.py
@@ -246,10 +246,10 @@
     st, e, dp, top = call(
         stats_kernel,
         [SMEM] + [VMEM] * 3,
-        [struct((sides * n_q, 2 * sides * n_q, rows), f32), full, full, line],
+        [struct((n_q, 2 * sides * n_q, rows), f32), full, full, line],
         [pltpu.VMEM((keys, hd), f32)],
     )(side, qa, qb, kp)
-    st = swap(st, ("head", "core"))
+    st = lax.all_gather(swap(st, "head"), "core", axis=0, tiled=True)
     gkv, ds = call(
         keys_kernel,
         [SMEM] + [VMEM] * 6,

time: 92.3 us -> 93.3 us (1.011)
  waiting for transfers between devices: 19 us -> 21.8 us
  blocking collectives: 41.6 us -> 40 us
    all_to_all x3, blocking collectives: 39.4 us -> 35.8 us  [swap(): return lax.all_to_all(x, axis, split_axis=0, concat_axis=0, tiled=True)]
    all_to_all x2, waiting for transfers between devices: 19 us -> 21.8 us  [swap(): return lax.all_to_all(x, axis, split_axis=0, concat_axis=0, tiled=True)]
    all_gather x0 -> x1, blocking collectives: none -> 1.98 us  [on_device(): st = lax.all_gather(swap(st, 'head'), 'core', axis=0, tiled=True)]
where the time goes in v6:
time: 93.3 us; the launch traced here: 92.7 us
  blocking collectives  40 us (43%)
  starting transfers between devices  22.1 us (24%)
  waiting for transfers between devices  21.8 us (23%)
  Pallas kernels  7.33 us (8%)
    all_to_all x3, blocking collectives, swap(): return lax.all_to_all(x, axis, split_axis=0, concat_axis=0, tiled=True)  35.8 us
    all_to_all x2, waiting for transfers between devices, swap(): return lax.all_to_all(x, axis, split_axis=0, concat_axis=0, tiled=True)  21.8 us
    all_to_all x2, starting transfers between devices, swap(): return lax.all_to_all(x, axis, split_axis=0, concat_axis=0, tiled=True)  20.1 us
    pallas_call x1, Pallas kernels, on_device(): call(stats_kernel, [SMEM] + [VMEM] * 3, [struct((n_q, 2 * sides * n_q, ro...  2.62 us
    all_gather x1, blocking collectives, on_device(): both = lax.all_gather(oth, 'core', axis=0, tiled=False)  2.18 us
    all_gather x1, blocking collectives, on_device(): st = lax.all_gather(swap(st, 'head'), 'core', axis=0, tiled=True)  1.98 us
    ppermute x1, starting transfers between devices, other(): return lax.ppermute(x, 'core', [(0, 1), (1, 0)])  1.92 us
    pallas_call x1, Pallas kernels, on_device(): call(pack_kernel, [HBM] * 6, [struct((n_q, 2 * rows + META, hd), bf), str...  1.87 us
  transfers between devices with their start and end apart: 3, of which 2 were waited for; matrix products, arithmetic and copies ran while one was open for 0% of the time, Pallas kernels for 1%

profile of v6, /device:TPU:16, one launch (start us, length us, event | category | flops | bytes accessed | tf_op | source)
XLA Modules:
  0.0 92.7 jit_solution(12753505049927008186)
XLA Ops:
  0.6 1.9 %shard_map.85 = (bf16[8,264,128]{2,1,0:T(8,128)(2,1)}, bf16[32,40,128]{2,1,0:T(8,128)(2,1)}) custom-call(s32[16]{0:T(128)} %pos_any.1, s32[16]{0:T(128)} %doc_any.1, bf16[16,1024]{1,0:T(8,128)(2,1)} %q_any.1, bf16[16,1024]{1,0:T(8,128)(2,1)} %g_any.1, bf16[16,128]{1,0:T(8,128)(2,1)} %k_any.1, bf16[16,128]{1,0:T(8,128)(2,1)} %v_any.1), custom_call_target="tpu_custom_call" | custom-call | tf_op jit(solution)/shard_map/pallas_call | solution.py:233
  2.5 15.8 %all_to_all.25.qa_ref = bf16[8,264,128]{2,1,0:T(8,128)(2,1)S(1)} all-to-all(bf16[8,264,128]{2,1,0:T(8,128)(2,1)} %get-tuple-element.16), channel_id=1, replica_groups=mesh['head'=8,'far'=32,'core'=2] {'head'}, dimensions={0} | all-to-all | bytes 1081344 | tf_op jit(solution)/shard_map/all_to_all | solution.py:226
  18.3 15.2 %all-to-all-start = ((bf16[32,40,128]{2,1,0:T(8,128)(2,1)}), bf16[32,40,128]{2,1,0:T(8,128)(2,1)S(1)}, u32[]{:S(2)}, u32[]{:S(2)}) async-start(bf16[32,40,128]{2,1,0:T(8,128)(2,1)} %get-tuple-element.15), calls=%async_computation | async-start | bytes 655360 | tf_op jit(solution)/shard_map/all_to_all | solution.py:226
  33.5 1.9 %collective-permute-start = (bf16[8,264,128]{2,1,0:T(8,128)(2,1)S(1)}, bf16[8,264,128]{2,1,0:T(8,128)(2,1)S(1)}, u32[]{:S(2)}, u32[]{:S(2)}) collective-permute-start(bf16[8,264,128]{2,1,0:T(8,128)(2,1)S(1)} %all_to_all.25.qa_ref), channel_id=1, source_target_pairs={{0,1},{1,0},{2,3},{3,2},{4,5},{5,4},{6,7},{7,6},{8,9},{9,8},{10,11... | collective-permute-start | bytes 1622024 | tf_op jit(solution)/shard_map/ppermute | solution.py:229
  35.4 10.7 %all-to-all-done.kp_ref = bf16[32,40,128]{2,1,0:T(8,128)(2,1)S(1)} async-done(((bf16[32,40,128]{2,1,0:T(8,128)(2,1)}), bf16[32,40,128]{2,1,0:T(8,128)(2,1)S(1)}, u32[]{:S(2)}, u32[]{:S(2)}) %all-to-all-start) | async-done | bytes 327712 | tf_op jit(solution)/shard_map/all_to_all | solution.py:226
  46.1 0.0 collective-permute-done.qb_ref
  46.1 2.6 %shard_map.86 = (f32[8,32,128]{2,1,0:T(8,128)S(1)}, f32[512,2048]{1,0:T(8,128)S(1)}, f32[512,2048]{1,0:T(8,128)S(1)}, f32[16,128]{1,0:T(8,128)S(1)}) custom-call(s32[1]{0:T(128)} %bitcast.side_ref, bf16[8,264,128]{2,1,0:T(8,128)(2,1)S(1)} %all_to_all.25.qa_ref, bf16[8,264,128]{2,1,0:T(8,128)(2,1)S(1)} %collective-permute-done.qb_ref, ...), custom_call_target="tpu_custom_call" | custom-call | tf_op jit(solution)/shard_map/pallas_call | solution.py:246
  48.7 10.3 %all_to_all.26 = f32[8,32,128]{2,1,0:T(8,128)S(1)} all-to-all(f32[8,32,128]{2,1,0:T(8,128)S(1)} %get-tuple-element.17), channel_id=1, replica_groups=mesh['head'=8,'far'=32,'core'=2] {'head'}, dimensions={0} | all-to-all | bytes 262144 | tf_op jit(solution)/shard_map/all_to_all | solution.py:226
  59.1 2.0 %all_gather.9.st_ref = f32[16,32,128]{2,1,0:T(8,128)S(1)} all-gather(f32[8,32,128]{2,1,0:T(8,128)S(1)} %all_to_all.26), channel_id=1, replica_groups=mesh['head'=8,'far'=32,'core'=2] {'core'}, dimensions={0}, use_global_device_ids=true | all-gather | bytes 393216 | tf_op jit(solution)/shard_map/all_gather | solution.py:252
  61.0 1.3 %shard_map.87 = (bf16[32,32,128]{2,1,0:T(8,128)(2,1)S(1)}, bf16[512,2048]{1,0:T(8,128)(2,1)S(1)}) custom-call(s32[1]{0:T(128)} %bitcast.side_ref, bf16[8,264,128]{2,1,0:T(8,128)(2,1)S(1)} %all_to_all.25.qa_ref, bf16[8,264,128]{2,1,0:T(8,128)(2,1)S(1)} %collective-permute-done.qb_ref, f32[16,32,128]{2,1,0:T(8,128)S(1)} %all_gather.9.st_ref, ...), custom_call_target="tpu_custom_call" | custom-call | tf_op jit(solution)/shard_map/pallas_call | solution.py:253
  62.4 0.0 copy-start
  62.4 0.7 copy-done
  63.1 5.0 %all-to-all-start.3 = ((bf16[32,32,128]{2,1,0:T(8,128)(2,1)}), bf16[32,32,128]{2,1,0:T(8,128)(2,1)S(1)}, u32[]{:S(2)}, u32[]{:S(2)}) async-start(bf16[32,32,128]{2,1,0:T(8,128)(2,1)} %copy-done), calls=%async_computation.3 | async-start | bytes 524288 | tf_op jit(solution)/shard_map/all_to_all | solution.py:226
  68.1 0.8 shard_map.88
  68.9 2.2 %all-gather = bf16[16,128,128]{2,1,0:T(8,128)(2,1)S(1)} all-gather(bf16[8,128,128]{2,1,0:T(8,128)(2,1)S(1)} %get-tuple-element.23), channel_id=2, replica_groups=mesh['head'=8,'far'=32,'core'=2] {'core'}, dimensions={0}, use_global_device_ids=true | all-gather | bytes 786432 | tf_op jit(solution)/shard_map/all_gather | solution.py:266
  71.1 0.1 fusion
  71.2 11.2 %all-to-all-done.3.gkv_ref = bf16[32,32,128]{2,1,0:T(8,128)(2,1)S(1)} async-done(((bf16[32,32,128]{2,1,0:T(8,128)(2,1)}), bf16[32,32,128]{2,1,0:T(8,128)(2,1)S(1)}, u32[]{:S(2)}, u32[]{:S(2)}) %all-to-all-start.3) | async-done | bytes 262176 | tf_op jit(solution)/shard_map/all_to_all | solution.py:226
  82.4 9.7 %all_to_all.27.gq_ref = bf16[8,128,128]{2,1,0:T(8,128)(2,1)S(1)} all-to-all(bf16[8,128,128]{2,1,0:T(8,128)(2,1)S(1)} %fusion), channel_id=1, replica_groups=mesh['head'=8,'far'=32,'core'=2] {'head'}, dimensions={0} | all-to-all | bytes 524288 | tf_op jit(solution)/shard_map/all_to_all | solution.py:226
  92.0 0.7 shard_map.89
Async XLA Ops:
  18.3 27.8 %all-to-all-start = ((bf16[32,40,128]{2,1,0:T(8,128)(2,1)}), bf16[32,40,128]{2,1,0:T(8,128)(2,1)S(1)}, u32[]{:S(2)}, u32[]{:S(2)}) async-start(bf16[32,40,128]{2,1,0:T(8,128)(2,1)} %get-tuple-element.15), calls=%async_computation | async-start | bytes 655360 | tf_op jit(solution)/shard_map/all_to_all | solution.py:226
  33.5 12.6 %collective-permute-start = (bf16[8,264,128]{2,1,0:T(8,128)(2,1)S(1)}, bf16[8,264,128]{2,1,0:T(8,128)(2,1)S(1)}, u32[]{:S(2)}, u32[]{:S(2)}) collective-permute-start(bf16[8,264,128]{2,1,0:T(8,128)(2,1)S(1)} %all_to_all.25.qa_ref), channel_id=1, source_target_pairs={{0,1},{1,0},{2,3},{3,2},{4,5},{5,4},{6,7},{7,6},{8,9},{9,8},{10,11... | collective-permute-start | bytes 1622024 | tf_op jit(solution)/shard_map/ppermute | solution.py:229
  62.4 0.7 copy-start
  63.1 19.3 %all-to-all-start.3 = ((bf16[32,32,128]{2,1,0:T(8,128)(2,1)}), bf16[32,32,128]{2,1,0:T(8,128)(2,1)S(1)}, u32[]{:S(2)}, u32[]{:S(2)}) async-start(bf16[32,32,128]{2,1,0:T(8,128)(2,1)} %copy-done), calls=%async_computation.3 | async-start | bytes 524288 | tf_op jit(solution)/shard_map/all_to_all | solution.py:226

commit v7 on v5

--- a/solution.py
+++ b/solution.py
@@ -1,3 +1,4 @@
+import functools
 import math
 
 import jax
@@ -8,11 +9,11 @@
 from jax.sharding import Mesh
 from jax.sharding import PartitionSpec as P
 
-GRANT = 60 * 1024 * 1024
 LOW = -1e30
 FLOOR = -1e29
 DOC_STEP = 8192.0
 META = 8
+CHUNK = 256
 
 
 def dot_rows(a, b):
@@ -27,13 +28,13 @@
     return lax.dot_general(a, b, (((0,), (0,)), ((), ())), preferred_element_type=jnp.float32)
 
 
-def pack_kernel(pos_any, doc_any, q_any, g_any, k_any, v_any, qp_ref, kp_ref, *scratch):
-    bufs, sems = scratch[:6], scratch[6]
+def pack_kernel(pos_any, doc_any, q_any, g_any, k_any, v_any, qp_ref, kp_hbm, *scratch):
+    bufs, sems, kp_ref, out_sem = scratch[:6], scratch[6], scratch[7], scratch[8]
     hbm = (pos_any, doc_any, q_any, g_any, k_any, v_any)
     copies = [pltpu.make_async_copy(src, dst, sems.at[i]) for i, (src, dst) in enumerate(zip(hbm, bufs))]
     for copy in copies:
         copy.start()
-    for copy in copies:
+    for copy in copies[:2] + copies[4:]:
         copy.wait()
     pos_ref, doc_ref, q_ref, g_ref, k_ref, v_ref = bufs
     run, hd = k_ref.shape
@@ -58,6 +59,15 @@
     k_meta = jnp.where(item == 0, docs, jnp.where(item == 1, high, jnp.where(item == 2, low, 0)))
     q_meta = q_meta.astype(jnp.float32).astype(jnp.bfloat16)
     k_meta = k_meta.astype(jnp.float32).astype(jnp.bfloat16)
+    k, v = k_ref[...], v_ref[...]
+    for d in range(n_k):
+        kp_ref[d, 0:run, :] = k
+        kp_ref[d, run : 2 * run, :] = v
+        kp_ref[d, 2 * run : 2 * run + META, :] = k_meta
+    out = pltpu.make_async_copy(kp_ref, kp_hbm, out_sem.at[0])
+    out.start()
+    for copy in copies[2:4]:
+        copy.wait()
     for h in range(heads):
         q_h = q_ref[:, h * hd : (h + 1) * hd]
         g_h = g_ref[:, h * hd : (h + 1) * hd]
@@ -66,11 +76,7 @@
             qp_ref[d, rows + h * run : rows + (h + 1) * run, :] = g_h
     for d in range(n_q):
         qp_ref[d, 2 * rows : 2 * rows + META, :] = q_meta
-    k, v = k_ref[...], v_ref[...]
-    for d in range(n_k):
-        kp_ref[d, 0:run, :] = k
-        kp_ref[d, run : 2 * run, :] = v
-        kp_ref[d, 2 * run : 2 * run + META, :] = k_meta
+    out.wait()
 
 
 def key_codes(kp_ref, run):
@@ -113,38 +119,46 @@
     run = (kp_ref.shape[1] - META) // 2
     scale = 1.0 / math.sqrt(hd)
     code_ref[...] = key_codes(kp_ref, run)
-    k = kp_ref[:, 0:run, :].reshape(n_k * run, hd)
-    v = kp_ref[:, run : 2 * run, :].reshape(n_k * run, hd)
+    per = CHUNK // run
+    n_c = n_k // per
     for qp_ref, at, d, home in blocks(qa_ref, qb_ref, side_ref[0]):
         q = qp_ref[at : at + 2, 0:rows, :].reshape(2 * rows, hd)
         g = qp_ref[at : at + 2, rows : 2 * rows, :].reshape(2 * rows, hd)
         pairs = [query_codes(qp_ref, at + i, run) for i in range(2)]
         base = jnp.concatenate([p[0] for p in pairs], axis=1)
         top = jnp.concatenate([p[1] for p in pairs], axis=1)
-        code = jnp.concatenate([code_ref[...]] * (2 * rows // hd), axis=1)
-        seen = (code <= top) & (code >= base)
-        s = jnp.where(seen, dot_rows(k, q) * scale, LOW)
-        dp = dot_rows(v, g)
-        high = jnp.maximum(jnp.max(s, axis=0, keepdims=True), FLOOR)
-        e = jnp.exp(s - high)
         cols = slice(d * rows, (d + 2) * rows)
-        e_ref[:, cols] = e
-        dp_ref[:, cols] = dp
-        total = jnp.sum(e, axis=0, keepdims=True)
-        cross = jnp.sum(e * dp, axis=0, keepdims=True)
+        sums = []
+        for c in range(n_c):
+            at_k, at_c = slice(c * per, (c + 1) * per), slice(c * CHUNK, (c + 1) * CHUNK)
+            k = kp_ref[at_k, 0:run, :].reshape(CHUNK, hd)
+            v = kp_ref[at_k, run : 2 * run, :].reshape(CHUNK, hd)
+            code = jnp.concatenate([code_ref[at_c, :]] * (2 * rows // hd), axis=1)
+            seen = (code <= top) & (code >= base)
+            s = jnp.where(seen, dot_rows(k, q) * scale, LOW)
+            high = jnp.maximum(jnp.max(s, axis=0, keepdims=True), FLOOR)
+            e = jnp.exp(s - high)
+            e_ref[at_c, cols] = e
+            dp = dot_rows(v, g)
+            dp_ref[at_c, cols] = dp
+            top_ref[c : c + 1, cols] = high
+            sums.append((high, jnp.sum(e, axis=0, keepdims=True), jnp.sum(e * dp, axis=0, keepdims=True)))
+        high = functools.reduce(jnp.maximum, [x[0] for x in sums])
+        share = [jnp.exp(x[0] - high) for x in sums]
+        total = sum(f * x[1] for f, x in zip(share, sums))
+        cross = sum(f * x[2] for f, x in zip(share, sums))
         some = total > 0.0
         safe = jnp.where(some, total, 1.0)
         log_total = jnp.where(some, high + jnp.log(safe), LOW)
         row_dot = jnp.where(some, cross / safe, 0.0)
         for i in range(2):
             lo, hi = i * rows, (i + 1) * rows
-            top_ref[d + i : d + i + 1, :] = high[:, lo:hi]
             for to in range(out_ref.shape[0]):
                 out_ref[to, pl.ds(home + i, 1), :] = log_total[:, lo:hi]
                 out_ref[to, pl.ds(2 * n_q + home + i, 1), :] = row_dot[:, lo:hi]
 
 
-def keys_kernel(side_ref, qa_ref, qb_ref, st_ref, e_ref, dp_ref, top_ref, gkv_ref, ds_ref, log_ref, dot_ref):
+def keys_kernel(side_ref, qa_ref, qb_ref, st_ref, e_ref, dp_ref, top_ref, gkv_hbm, ds_ref, log_ref, dot_ref, gkv_ref, sems):
     n_q, block, hd = qa_ref.shape
     n_k, twice, _ = gkv_ref.shape
     run = twice // 2
@@ -155,23 +169,35 @@
     log_total = high + jnp.log(jnp.sum(jnp.exp(logs - high[None]), axis=0))
     log_ref[...] = log_total
     dot_ref[...] = jnp.sum(jnp.exp(logs - log_total[None]) * st_ref[:, 2 * n_q :, :], axis=0)
-    gk = jnp.zeros((n_k * run, hd), jnp.float32)
+
+    def send(rows_at, i):
+        copy = pltpu.make_async_copy(gkv_ref.at[:, rows_at, :], gkv_hbm.at[:, rows_at, :], sems.at[i])
+        copy.start()
+        return copy
+
     gv = jnp.zeros((n_k * run, hd), jnp.float32)
     for qp_ref, at, d, home in blocks(qa_ref, qb_ref, side_ref[0]):
-        q = qp_ref[at : at + 2, 0:rows, :].reshape(2 * rows, hd)
         g = qp_ref[at : at + 2, rows : 2 * rows, :].reshape(2 * rows, hd)
-        factor = jnp.concatenate(
-            [jnp.exp(top_ref[d + i : d + i + 1, :] - log_ref[pl.ds(home + i, 1), :]) for i in range(2)], axis=1
-        )
+        log_row = jnp.concatenate([log_ref[pl.ds(home + i, 1), :] for i in range(2)], axis=1)
         dot_row = jnp.concatenate([dot_ref[pl.ds(home + i, 1), :] for i in range(2)], axis=1)
         cols = slice(d * rows, (d + 2) * rows)
-        w = e_ref[:, cols] * factor
-        ds = (w * (dp_ref[:, cols] - dot_row)).astype(jnp.bfloat16)
-        ds_ref[:, cols] = ds
-        gk = gk + dot_plain(ds, q)
-        gv = gv + dot_plain(w.astype(jnp.bfloat16), g)
+        parts = []
+        for c in range(n_k * run // CHUNK):
+            at_c = slice(c * CHUNK, (c + 1) * CHUNK)
+            w = e_ref[at_c, cols] * jnp.exp(top_ref[c : c + 1, cols] - log_row)
+            ds_ref[at_c, cols] = (w * (dp_ref[at_c, cols] - dot_row)).astype(jnp.bfloat16)
+            parts.append(w.astype(jnp.bfloat16))
+        gv = gv + dot_plain(jnp.concatenate(parts, axis=0), g)
+    gkv_ref[:, run:, :] = gv.reshape(n_k, run, hd).astype(gkv_ref.dtype)
+    values = send(slice(run, 2 * run), 0)
+    gk = jnp.zeros((n_k * run, hd), jnp.float32)
+    for qp_ref, at, d, home in blocks(qa_ref, qb_ref, side_ref[0]):
+        q = qp_ref[at : at + 2, 0:rows, :].reshape(2 * rows, hd)
+        gk = gk + dot_plain(ds_ref[:, d * rows : (d + 2) * rows], q)
     gkv_ref[:, 0:run, :] = (gk * scale).reshape(n_k, run, hd).astype(gkv_ref.dtype)
-    gkv_ref[:, run:, :] = gv.reshape(n_k, run, hd).astype(gkv_ref.dtype)
+    keys = send(slice(0, run), 1)
+    values.wait()
+    keys.wait()
 
 
 def queries_kernel(kp_ref, ds_ref, own_ref, oth_ref):
@@ -201,11 +227,11 @@
 HBM = pl.BlockSpec(memory_space=pltpu.HBM)
 
 
-def call(kernel, in_specs, outs, scratch=(), grant=16 * 1024 * 1024, cost=0):
+def call(kernel, in_specs, outs, scratch=(), grant=16 * 1024 * 1024, cost=0, out_specs=None):
     return pl.pallas_call(
         kernel,
         in_specs=in_specs,
-        out_specs=[VMEM] * len(outs),
+        out_specs=out_specs or [VMEM] * len(outs),
         out_shape=outs,
         scratch_shapes=list(scratch),
         cost_estimate=pl.CostEstimate(flops=cost, bytes_accessed=0, transcendentals=0) if cost else None,
@@ -233,28 +259,39 @@
     qp, kp = call(
         pack_kernel,
         [HBM] * 6,
-        [struct((n_q, 2 * rows + META, hd), bf), struct((n_k, 2 * run + META, hd), bf)],
+        [struct((n_q, 2 * rows + META, hd), bf), pltpu.HBM((n_k, 2 * run + META, hd), bf)],
         [(pltpu.SMEM if a.ndim == 1 else pltpu.VMEM)(a.shape, a.dtype) for a in args]
-        + [pltpu.SemaphoreType.DMA((6,))],
-        grant=GRANT,
-    )(*args)
+        + [
+            pltpu.SemaphoreType.DMA((6,)),
+            pltpu.VMEM((n_k, 2 * run + META, hd), bf),
+            pltpu.SemaphoreType.DMA((1,)),
+        ],
+        out_specs=[VMEM, HBM],
+    )(*(pltpu.with_memory_space_constraint(a, pltpu.HBM) for a in args))
     qa = swap(qp, "head")
     qb = other(qa)
     kp = swap(kp, "far")
     full = struct((keys, sides * n_q * rows), f32)
     line = struct((sides * n_q, rows), f32)
+    tops = struct((keys // CHUNK, full.shape[1]), f32)
     st, e, dp, top = call(
         stats_kernel,
         [SMEM] + [VMEM] * 3,
-        [struct((sides * n_q, 2 * sides * n_q, rows), f32), full, full, line],
+        [struct((sides * n_q, 2 * sides * n_q, rows), f32), full, full, tops],
         [pltpu.VMEM((keys, hd), f32)],
     )(side, qa, qb, kp)
     st = swap(st, ("head", "core"))
     gkv, ds = call(
         keys_kernel,
         [SMEM] + [VMEM] * 6,
-        [struct((n_k, 2 * run, hd), bf), struct(full.shape, bf)],
-        [pltpu.VMEM(line.shape, f32), pltpu.VMEM(line.shape, f32)],
+        [pltpu.HBM((n_k, 2 * run, hd), bf), struct(full.shape, bf)],
+        [
+            pltpu.VMEM(line.shape, f32),
+            pltpu.VMEM(line.shape, f32),
+            pltpu.VMEM((n_k, 2 * run, hd), bf),
+            pltpu.SemaphoreType.DMA((2,)),
+        ],
+        out_specs=[HBM, VMEM],
     )(side, qa, qb, st, e, dp, top)
     own, oth = call(
         queries_kernel,

time: 92.3 us -> 91.5 us (level)
  no operation moved by 1% of the time
where the time goes in v7:
time: 91.5 us; the launch traced here: 91 us
  blocking collectives  41.4 us (45%)
  starting transfers between devices  22.2 us (24%)
  waiting for transfers between devices  19 us (21%)
  Pallas kernels  7.69 us (8%)
    all_to_all x3, blocking collectives, swap(): return lax.all_to_all(x, axis, split_axis=0, concat_axis=0, tiled=True)  39.2 us
    all_to_all x2, starting transfers between devices, swap(): return lax.all_to_all(x, axis, split_axis=0, concat_axis=0, tiled=True)  20.2 us
    all_to_all x2, waiting for transfers between devices, swap(): return lax.all_to_all(x, axis, split_axis=0, concat_axis=0, tiled=True)  19 us
    pallas_call x1, Pallas kernels, on_device(): call(stats_kernel, [SMEM] + [VMEM] * 3, [struct((sides * n_q, 2 * sides *...  2.57 us
    all_gather x1, blocking collectives, on_device(): both = lax.all_gather(oth, 'core', axis=0, tiled=False)  2.18 us
    pallas_call x1, Pallas kernels, on_device(): call(keys_kernel, [SMEM] + [VMEM] * 6, [pltpu.HBM((n_k, 2 * run, hd), bf)...  2.06 us
    ppermute x1, starting transfers between devices, other(): return lax.ppermute(x, 'core', [(0, 1), (1, 0)])  1.92 us
  transfers between devices with their start and end apart: 3, of which 2 were waited for; matrix products, arithmetic and copies ran while one was open for 0% of the time, Pallas kernels for 1%

profile of v7, /device:TPU:16, one launch (start us, length us, event | category | flops | bytes accessed | tf_op | source)
XLA Modules:
  0.0 91.0 jit_solution(2139015773476505155)
XLA Ops:
  0.6 1.6 %shard_map.85 = (bf16[8,264,128]{2,1,0:T(8,128)(2,1)S(1)}, bf16[32,40,128]{2,1,0:T(8,128)(2,1)}) custom-call(s32[16]{0:T(128)} %pos_any.1, s32[16]{0:T(128)} %doc_any.1, bf16[16,1024]{1,0:T(8,128)(2,1)} %q_any.1, bf16[16,1024]{1,0:T(8,128)(2,1)} %g_any.1, bf16[16,128]{1,0:T(8,128)(2,1)} %k_any.1, bf16[16,128]{1,0:T(8,128)(2,1)} %v_any.1), custom_call_target="tpu_custom_call" | custom-call | tf_op jit(solution)/shard_map/pallas_call | solution.py:259
  2.2 15.6 %all_to_all.25.qa_ref = bf16[8,264,128]{2,1,0:T(8,128)(2,1)S(1)} all-to-all(bf16[8,264,128]{2,1,0:T(8,128)(2,1)S(1)} %get-tuple-element.16), channel_id=1, replica_groups=mesh['head'=8,'far'=32,'core'=2] {'head'}, dimensions={0} | all-to-all | bytes 1081344 | tf_op jit(solution)/shard_map/all_to_all | solution.py:252
  17.8 15.2 %all-to-all-start = ((bf16[32,40,128]{2,1,0:T(8,128)(2,1)}), bf16[32,40,128]{2,1,0:T(8,128)(2,1)S(1)}, u32[]{:S(2)}, u32[]{:S(2)}) async-start(bf16[32,40,128]{2,1,0:T(8,128)(2,1)} %get-tuple-element.15), calls=%async_computation | async-start | bytes 655360 | tf_op jit(solution)/shard_map/all_to_all | solution.py:252
  33.0 1.9 %collective-permute-start = (bf16[8,264,128]{2,1,0:T(8,128)(2,1)S(1)}, bf16[8,264,128]{2,1,0:T(8,128)(2,1)S(1)}, u32[]{:S(2)}, u32[]{:S(2)}) collective-permute-start(bf16[8,264,128]{2,1,0:T(8,128)(2,1)S(1)} %all_to_all.25.qa_ref), channel_id=1, source_target_pairs={{0,1},{1,0},{2,3},{3,2},{4,5},{5,4},{6,7},{7,6},{8,9},{9,8},{10,11... | collective-permute-start | bytes 1622024 | tf_op jit(solution)/shard_map/ppermute | solution.py:255
  34.9 10.7 %all-to-all-done.kp_ref = bf16[32,40,128]{2,1,0:T(8,128)(2,1)S(1)} async-done(((bf16[32,40,128]{2,1,0:T(8,128)(2,1)}), bf16[32,40,128]{2,1,0:T(8,128)(2,1)S(1)}, u32[]{:S(2)}, u32[]{:S(2)}) %all-to-all-start) | async-done | bytes 327712 | tf_op jit(solution)/shard_map/all_to_all | solution.py:252
  45.6 0.0 collective-permute-done.qb_ref
  45.6 2.6 %shard_map.86 = (f32[16,32,128]{2,1,0:T(8,128)S(1)}, f32[512,2048]{1,0:T(8,128)S(1)}, f32[512,2048]{1,0:T(8,128)S(1)}, f32[2,2048]{1,0:T(2,128)S(1)}) custom-call(s32[1]{0:T(128)} %bitcast.side_ref, bf16[8,264,128]{2,1,0:T(8,128)(2,1)S(1)} %all_to_all.25.qa_ref, bf16[8,264,128]{2,1,0:T(8,128)(2,1)S(1)} %collective-permute-done.qb_ref, ...), custom_call_target="tpu_custom_call" | custom-call | tf_op jit(solution)/shard_map/pallas_call | solution.py:277
  48.2 11.8 %all_to_all.26.st_ref = f32[16,32,128]{2,1,0:T(8,128)S(1)} all-to-all(f32[16,32,128]{2,1,0:T(8,128)S(1)} %get-tuple-element.17), channel_id=1, replica_groups=mesh['head'=8,'far'=32,'core'=2] {'head','core'}, dimensions={0} | all-to-all | bytes 524288 | tf_op jit(solution)/shard_map/all_to_all | solution.py:252
  59.9 2.1 %shard_map.87 = (bf16[32,32,128]{2,1,0:T(8,128)(2,1)}, bf16[512,2048]{1,0:T(8,128)(2,1)S(1)}) custom-call(s32[1]{0:T(128)} %bitcast.side_ref, bf16[8,264,128]{2,1,0:T(8,128)(2,1)S(1)} %all_to_all.25.qa_ref, bf16[8,264,128]{2,1,0:T(8,128)(2,1)S(1)} %collective-permute-done.qb_ref, f32[16,32,128]{2,1,0:T(8,128)S(1)} %all_to_all.26.st_ref, ...), custom_call_target="tpu_custom_call" | custom-call | tf_op jit(solution)/shard_map/pallas_call | solution.py:284
  62.0 5.1 %all-to-all-start.3 = ((bf16[32,32,128]{2,1,0:T(8,128)(2,1)}), bf16[32,32,128]{2,1,0:T(8,128)(2,1)S(1)}, u32[]{:S(2)}, u32[]{:S(2)}) async-start(bf16[32,32,128]{2,1,0:T(8,128)(2,1)} %get-tuple-element.24), calls=%async_computation.3 | async-start | bytes 524288 | tf_op jit(solution)/shard_map/all_to_all | solution.py:252
  67.1 0.8 shard_map.88
  67.9 2.2 %all-gather = bf16[16,128,128]{2,1,0:T(8,128)(2,1)S(1)} all-gather(bf16[8,128,128]{2,1,0:T(8,128)(2,1)S(1)} %get-tuple-element.23), channel_id=2, replica_groups=mesh['head'=8,'far'=32,'core'=2] {'core'}, dimensions={0}, use_global_device_ids=true | all-gather | bytes 786432 | tf_op jit(solution)/shard_map/all_gather | solution.py:303
  70.1 0.1 fusion
  70.2 8.4 %all-to-all-done.3.gkv_ref = bf16[32,32,128]{2,1,0:T(8,128)(2,1)S(1)} async-done(((bf16[32,32,128]{2,1,0:T(8,128)(2,1)}), bf16[32,32,128]{2,1,0:T(8,128)(2,1)S(1)}, u32[]{:S(2)}, u32[]{:S(2)}) %all-to-all-start.3) | async-done | bytes 262176 | tf_op jit(solution)/shard_map/all_to_all | solution.py:252
  78.6 11.8 %all_to_all.27.gq_ref = bf16[8,128,128]{2,1,0:T(8,128)(2,1)S(1)} all-to-all(bf16[8,128,128]{2,1,0:T(8,128)(2,1)S(1)} %fusion), channel_id=1, replica_groups=mesh['head'=8,'far'=32,'core'=2] {'head'}, dimensions={0} | all-to-all | bytes 524288 | tf_op jit(solution)/shard_map/all_to_all | solution.py:252
  90.3 0.7 shard_map.89
Async XLA Ops:
  17.8 27.8 %all-to-all-start = ((bf16[32,40,128]{2,1,0:T(8,128)(2,1)}), bf16[32,40,128]{2,1,0:T(8,128)(2,1)S(1)}, u32[]{:S(2)}, u32[]{:S(2)}) async-start(bf16[32,40,128]{2,1,0:T(8,128)(2,1)} %get-tuple-element.15), calls=%async_computation | async-start | bytes 655360 | tf_op jit(solution)/shard_map/all_to_all | solution.py:252
  33.0 12.6 %collective-permute-start = (bf16[8,264,128]{2,1,0:T(8,128)(2,1)S(1)}, bf16[8,264,128]{2,1,0:T(8,128)(2,1)S(1)}, u32[]{:S(2)}, u32[]{:S(2)}) collective-permute-start(bf16[8,264,128]{2,1,0:T(8,128)(2,1)S(1)} %all_to_all.25.qa_ref), channel_id=1, source_target_pairs={{0,1},{1,0},{2,3},{3,2},{4,5},{5,4},{6,7},{7,6},{8,9},{9,8},{10,11... | collective-permute-start | bytes 1622024 | tf_op jit(solution)/shard_map/ppermute | solution.py:255
  62.0 16.5 %all-to-all-start.3 = ((bf16[32,32,128]{2,1,0:T(8,128)(2,1)}), bf16[32,32,128]{2,1,0:T(8,128)(2,1)S(1)}, u32[]{:S(2)}, u32[]{:S(2)}) async-start(bf16[32,32,128]{2,1,0:T(8,128)(2,1)} %get-tuple-element.24), calls=%async_computation.3 | async-start | bytes 524288 | tf_op jit(solution)/shard_map/all_to_all | solution.py:252

commit v8 on v7

--- a/solution.py
+++ b/solution.py
@@ -79,9 +79,9 @@
     out.wait()
 
 
-def key_codes(kp_ref, run):
-    n_k, _, hd = kp_ref.shape
-    meta = kp_ref[:, 2 * run : 2 * run + META, :].astype(jnp.float32).reshape(n_k * META, hd)
+def key_codes(kp, run):
+    n_k, _, hd = kp.shape
+    meta = kp[:, 2 * run : 2 * run + META, :].astype(jnp.float32).reshape(n_k * META, hd)
     src = lax.broadcasted_iota(jnp.int32, (hd, 2 * hd), 0)
     dst = lax.broadcasted_iota(jnp.int32, (hd, 2 * hd), 1)
     half = hd // 2
@@ -105,34 +105,30 @@
     return base, base + meta[1:2] * (run * 16.0) + meta[2:3] * float(run) + tok
 
 
-def blocks(qa_ref, qb_ref, side):
-    n_q = qa_ref.shape[0]
-    for d in range(0, 2 * n_q, 2):
-        ref, at = (qa_ref, d) if d < n_q else (qb_ref, d - n_q)
-        yield ref, at, d, (side if d < n_q else 1 - side) * n_q + at
-
-
-def stats_kernel(side_ref, qa_ref, qb_ref, kp_ref, out_ref, e_ref, dp_ref, top_ref, code_ref):
-    n_q, block, hd = qa_ref.shape
-    n_k = kp_ref.shape[0]
+def stats_kernel(side_ref, qp_ref, kp_ref, out_ref, e_ref, dp_ref, top_ref, code_ref):
+    n_q, block, hd = qp_ref.shape
+    _, n_k, kp_rows, _ = kp_ref.shape
     rows = (block - META) // 2
-    run = (kp_ref.shape[1] - META) // 2
+    run = (kp_rows - META) // 2
     scale = 1.0 / math.sqrt(hd)
-    code_ref[...] = key_codes(kp_ref, run)
+    half = n_k * run
     per = CHUNK // run
-    n_c = n_k // per
-    for qp_ref, at, d, home in blocks(qa_ref, qb_ref, side_ref[0]):
-        q = qp_ref[at : at + 2, 0:rows, :].reshape(2 * rows, hd)
-        g = qp_ref[at : at + 2, rows : 2 * rows, :].reshape(2 * rows, hd)
-        pairs = [query_codes(qp_ref, at + i, run) for i in range(2)]
+    cores = (side_ref[0], 1 - side_ref[0])
+    for i, core in enumerate(cores):
+        code_ref[i * half : (i + 1) * half, :] = key_codes(kp_ref.at[core], run)
+    for d in range(0, n_q, 2):
+        q = qp_ref[d : d + 2, 0:rows, :].reshape(2 * rows, hd)
+        g = qp_ref[d : d + 2, rows : 2 * rows, :].reshape(2 * rows, hd)
+        pairs = [query_codes(qp_ref, d + i, run) for i in range(2)]
         base = jnp.concatenate([p[0] for p in pairs], axis=1)
         top = jnp.concatenate([p[1] for p in pairs], axis=1)
         cols = slice(d * rows, (d + 2) * rows)
         sums = []
-        for c in range(n_c):
-            at_k, at_c = slice(c * per, (c + 1) * per), slice(c * CHUNK, (c + 1) * CHUNK)
-            k = kp_ref[at_k, 0:run, :].reshape(CHUNK, hd)
-            v = kp_ref[at_k, run : 2 * run, :].reshape(CHUNK, hd)
+        for c in range(2 * half // CHUNK):
+            core, at = cores[c * CHUNK // half], (c * CHUNK % half) // run
+            at_c = slice(c * CHUNK, (c + 1) * CHUNK)
+            k = kp_ref[core, at : at + per, 0:run, :].reshape(CHUNK, hd)
+            v = kp_ref[core, at : at + per, run : 2 * run, :].reshape(CHUNK, hd)
             code = jnp.concatenate([code_ref[at_c, :]] * (2 * rows // hd), axis=1)
             seen = (code <= top) & (code >= base)
             s = jnp.where(seen, dot_rows(k, q) * scale, LOW)
@@ -153,63 +149,54 @@
         row_dot = jnp.where(some, cross / safe, 0.0)
         for i in range(2):
             lo, hi = i * rows, (i + 1) * rows
-            for to in range(out_ref.shape[0]):
-                out_ref[to, pl.ds(home + i, 1), :] = log_total[:, lo:hi]
-                out_ref[to, pl.ds(2 * n_q + home + i, 1), :] = row_dot[:, lo:hi]
-
-
-def keys_kernel(side_ref, qa_ref, qb_ref, st_ref, e_ref, dp_ref, top_ref, gkv_hbm, ds_ref, log_ref, dot_ref, gkv_ref, sems):
-    n_q, block, hd = qa_ref.shape
-    n_k, twice, _ = gkv_ref.shape
+            for to in range(n_q):
+                out_ref[to, d + i : d + i + 1, :] = log_total[:, lo:hi]
+                out_ref[to, n_q + d + i : n_q + d + i + 1, :] = row_dot[:, lo:hi]
+
+
+def grads_kernel(
+    side_ref, qp_ref, kp_ref, st_ref, e_ref, dp_ref, top_ref, gq_hbm, keep_ref, give_ref, log_ref, dot_ref, ds_ref, gq_ref, sem
+):
+    n_q, block, hd = qp_ref.shape
+    n_k, twice, _ = keep_ref.shape
     run = twice // 2
     rows = (block - META) // 2
     scale = 1.0 / math.sqrt(hd)
-    logs = st_ref[:, 0 : 2 * n_q, :]
+    half = n_k * run
+    cores = (side_ref[0], 1 - side_ref[0])
+    logs = st_ref[:, 0:n_q, :]
     high = jnp.max(logs, axis=0)
     log_total = high + jnp.log(jnp.sum(jnp.exp(logs - high[None]), axis=0))
     log_ref[...] = log_total
-    dot_ref[...] = jnp.sum(jnp.exp(logs - log_total[None]) * st_ref[:, 2 * n_q :, :], axis=0)
-
-    def send(rows_at, i):
-        copy = pltpu.make_async_copy(gkv_ref.at[:, rows_at, :], gkv_hbm.at[:, rows_at, :], sems.at[i])
-        copy.start()
-        return copy
-
-    gv = jnp.zeros((n_k * run, hd), jnp.float32)
-    for qp_ref, at, d, home in blocks(qa_ref, qb_ref, side_ref[0]):
-        g = qp_ref[at : at + 2, rows : 2 * rows, :].reshape(2 * rows, hd)
-        log_row = jnp.concatenate([log_ref[pl.ds(home + i, 1), :] for i in range(2)], axis=1)
-        dot_row = jnp.concatenate([dot_ref[pl.ds(home + i, 1), :] for i in range(2)], axis=1)
+    dot_ref[...] = jnp.sum(jnp.exp(logs - log_total[None]) * st_ref[:, n_q:, :], axis=0)
+    gv = [jnp.zeros((half, hd), jnp.float32) for _ in cores]
+    for d in range(0, n_q, 2):
+        g = qp_ref[d : d + 2, rows : 2 * rows, :].reshape(2 * rows, hd)
+        log_row = jnp.concatenate([log_ref[d + i : d + i + 1, :] for i in range(2)], axis=1)
+        dot_row = jnp.concatenate([dot_ref[d + i : d + i + 1, :] for i in range(2)], axis=1)
         cols = slice(d * rows, (d + 2) * rows)
-        parts = []
-        for c in range(n_k * run // CHUNK):
-            at_c = slice(c * CHUNK, (c + 1) * CHUNK)
-            w = e_ref[at_c, cols] * jnp.exp(top_ref[c : c + 1, cols] - log_row)
-            ds_ref[at_c, cols] = (w * (dp_ref[at_c, cols] - dot_row)).astype(jnp.bfloat16)
-            parts.append(w.astype(jnp.bfloat16))
-        gv = gv + dot_plain(jnp.concatenate(parts, axis=0), g)
-    gkv_ref[:, run:, :] = gv.reshape(n_k, run, hd).astype(gkv_ref.dtype)
-    values = send(slice(run, 2 * run), 0)
-    gk = jnp.zeros((n_k * run, hd), jnp.float32)
-    for qp_ref, at, d, home in blocks(qa_ref, qb_ref, side_ref[0]):
-        q = qp_ref[at : at + 2, 0:rows, :].reshape(2 * rows, hd)
-        gk = gk + dot_plain(ds_ref[:, d * rows : (d + 2) * rows], q)
-    gkv_ref[:, 0:run, :] = (gk * scale).reshape(n_k, run, hd).astype(gkv_ref.dtype)
-    keys = send(slice(0, run), 1)
-    values.wait()
-    keys.wait()
-
-
-def queries_kernel(kp_ref, ds_ref, own_ref, oth_ref):
-    n_q, rows, hd = own_ref.shape
-    n_k = kp_ref.shape[0]
-    run = (kp_ref.shape[1] - META) // 2
-    scale = 1.0 / math.sqrt(hd)
-    k = kp_ref[:, 0:run, :].reshape(n_k * run, hd)
-    for d in list(range(n_q, 2 * n_q, 2)) + list(range(0, n_q, 2)):
-        ref, at = (own_ref, d) if d < n_q else (oth_ref, d - n_q)
-        gq = dot_cols(ds_ref[:, d * rows : (d + 2) * rows], k) * scale
-        ref[at : at + 2] = gq.reshape(2, rows, hd).astype(ref.dtype)
+        gq = jnp.zeros((2 * rows, hd), jnp.float32)
+        for i, core in enumerate(cores):
+            parts = []
+            for c in range(i * half // CHUNK, (i + 1) * half // CHUNK):
+                at_c = slice(c * CHUNK, (c + 1) * CHUNK)
+                w = e_ref[at_c, cols] * jnp.exp(top_ref[c : c + 1, cols] - log_row)
+                ds_ref[at_c, cols] = (w * (dp_ref[at_c, cols] - dot_row)).astype(jnp.bfloat16)
+                parts.append(w.astype(jnp.bfloat16))
+            gv[i] = gv[i] + dot_plain(jnp.concatenate(parts, axis=0), g)
+            k = kp_ref[core, :, 0:run, :].reshape(half, hd)
+            gq = gq + dot_cols(ds_ref[i * half : (i + 1) * half, cols], k)
+        gq_ref[d : d + 2] = (gq * scale).reshape(2, rows, hd).astype(gq_ref.dtype)
+    out = pltpu.make_async_copy(gq_ref, gq_hbm, sem.at[0])
+    out.start()
+    for i, ref in enumerate((keep_ref, give_ref)):
+        gk = jnp.zeros((half, hd), jnp.float32)
+        for d in range(0, n_q, 2):
+            q = qp_ref[d : d + 2, 0:rows, :].reshape(2 * rows, hd)
+            gk = gk + dot_plain(ds_ref[i * half : (i + 1) * half, d * rows : (d + 2) * rows], q)
+        ref[:, 0:run, :] = (gk * scale).reshape(n_k, run, hd).astype(ref.dtype)
+        ref[:, run:, :] = gv[i].reshape(n_k, run, hd).astype(ref.dtype)
+    out.wait()
 
 
 def finish_kernel(gq_ref, gkv_ref, oq_ref, ok_ref, ov_ref):
@@ -240,7 +227,7 @@
 
 
 def on_device(queries, key_vecs, value_vecs, out_grad, positions, documents):
-    n_q, n_k, sides = lax.axis_size("head"), lax.axis_size("far"), lax.axis_size("core")
+    n_q, n_k = lax.axis_size("head"), lax.axis_size("far")
     run, hd = key_vecs.shape
     heads = queries.shape[1] // hd
     rows = run * heads
@@ -250,9 +237,6 @@
 
     def swap(x, axis):
         return lax.all_to_all(x, axis, split_axis=0, concat_axis=0, tiled=True)
-
-    def other(x):
-        return lax.ppermute(x, "core", [(0, 1), (1, 0)])
 
     side = lax.axis_index("core").astype(jnp.int32).reshape(1)
     args = (positions, documents, queries, out_grad, key_vecs, value_vecs)
@@ -268,43 +252,31 @@
         ],
         out_specs=[VMEM, HBM],
     )(*(pltpu.with_memory_space_constraint(a, pltpu.HBM) for a in args))
-    qa = swap(qp, "head")
-    qb = other(qa)
     kp = swap(kp, "far")
-    full = struct((keys, sides * n_q * rows), f32)
-    line = struct((sides * n_q, rows), f32)
-    tops = struct((keys // CHUNK, full.shape[1]), f32)
+    qp, kp = lax.optimization_barrier((qp, kp))
+    qp = swap(qp, "head")
+    kp = lax.all_gather(kp, "core", axis=0, tiled=False)
+    full = struct((2 * keys, n_q * rows), f32)
+    line = pltpu.VMEM((n_q, rows), f32)
     st, e, dp, top = call(
         stats_kernel,
-        [SMEM] + [VMEM] * 3,
-        [struct((sides * n_q, 2 * sides * n_q, rows), f32), full, full, tops],
-        [pltpu.VMEM((keys, hd), f32)],
-    )(side, qa, qb, kp)
-    st = swap(st, ("head", "core"))
-    gkv, ds = call(
-        keys_kernel,
+        [SMEM] + [VMEM] * 2,
+        [struct((n_q, 2 * n_q, rows), f32), full, full, struct((2 * keys // CHUNK, n_q * rows), f32)],
+        [pltpu.VMEM((2 * keys, hd), f32)],
+    )(side, qp, kp)
+    st = swap(st, "head")
+    gq, keep, give = call(
+        grads_kernel,
         [SMEM] + [VMEM] * 6,
-        [pltpu.HBM((n_k, 2 * run, hd), bf), struct(full.shape, bf)],
-        [
-            pltpu.VMEM(line.shape, f32),
-            pltpu.VMEM(line.shape, f32),
-            pltpu.VMEM((n_k, 2 * run, hd), bf),
-            pltpu.SemaphoreType.DMA((2,)),
-        ],
-        out_specs=[HBM, VMEM],
-    )(side, qa, qb, st, e, dp, top)
-    own, oth = call(
-        queries_kernel,
-        [VMEM] * 2,
-        [struct((n_q, rows, hd), f32), struct((n_q, rows, hd), bf)],
-        cost=2 * keys * sides * n_q * rows * hd,
-    )(kp, ds)
+        [pltpu.HBM((n_q, rows, hd), bf), struct((n_k, 2 * run, hd), f32), struct((n_k, 2 * run, hd), bf)],
+        [line, line, pltpu.VMEM(full.shape, bf), pltpu.VMEM((n_q, rows, hd), bf), pltpu.SemaphoreType.DMA((1,))],
+        out_specs=[HBM, VMEM, VMEM],
+    )(side, qp, kp, st, e, dp, top)
+    gq = swap(gq, "head")
+    both = lax.all_gather(give, "core", axis=0, tiled=False)
+    gkv = (keep + jnp.where(side[0] == 0, both[1], both[0]).astype(f32)).astype(bf)
+    gkv, gq = lax.optimization_barrier((gkv, gq))
     gkv = swap(gkv, "far")
-    both = lax.all_gather(oth, "core", axis=0, tiled=False)
-    oth = jnp.where(side == 0, both[1], both[0])
-    gq = (own + oth.astype(f32)).astype(bf)
-    gq, gkv = lax.optimization_barrier((gq, gkv))
-    gq = swap(gq, "head")
     return tuple(
         call(
             finish_kernel,

time: 91.5 us -> 91.7 us (level)
  the two profiles are of different devices: /device:TPU:16 before, /device:TPU:2 now
where the time goes in v8:
time: 91.7 us; the launch traced here: 91.1 us
  blocking collectives  65 us (71%)
  starting transfers between devices  9.62 us (10%)
  Pallas kernels  7.88 us (9%)
  waiting for transfers between devices  7.88 us (9%)
    all_to_all x3, blocking collectives, swap(): return lax.all_to_all(x, axis, split_axis=0, concat_axis=0, tiled=True)  60.6 us
    all_to_all x2, starting transfers between devices, swap(): return lax.all_to_all(x, axis, split_axis=0, concat_axis=0, tiled=True)  9.62 us
    all_to_all x2, waiting for transfers between devices, swap(): return lax.all_to_all(x, axis, split_axis=0, concat_axis=0, tiled=True)  7.88 us
    pallas_call x1, Pallas kernels, on_device(): call(stats_kernel, [SMEM] + [VMEM] * 2, [struct((n_q, 2 * n_q, rows), f32...  2.44 us
    pallas_call x1, Pallas kernels, on_device(): call(grads_kernel, [SMEM] + [VMEM] * 6, [pltpu.HBM((n_q, rows, hd), bf),...  2.39 us
    pallas_call x1, Pallas kernels, on_device(): call(pack_kernel, [HBM] * 6, [struct((n_q, 2 * rows + META, hd), bf), plt...  2.37 us
    all_gather x1, blocking collectives, on_device(): kp = lax.all_gather(kp, 'core', axis=0, tiled=False)  2.26 us
    all_gather x1, blocking collectives, on_device(): both = lax.all_gather(give, 'core', axis=0, tiled=False)  2.17 us
  transfers between devices with their start and end apart: 2, of which 2 were waited for; matrix products, arithmetic and copies ran while one was open for 0% of the time, Pallas kernels for 0%

profile of v8, /device:TPU:2, one launch (start us, length us, event | category | flops | bytes accessed | tf_op | source)
XLA Modules:
  0.0 91.1 jit_solution(15251828072428389628)
XLA Ops:
  0.6 2.4 %shard_map.85 = (bf16[8,264,128]{2,1,0:T(8,128)(2,1)}, bf16[32,40,128]{2,1,0:T(8,128)(2,1)}) custom-call(s32[16]{0:T(128)} %pos_any.1, s32[16]{0:T(128)} %doc_any.1, bf16[16,1024]{1,0:T(8,128)(2,1)} %q_any.1, bf16[16,1024]{1,0:T(8,128)(2,1)} %g_any.1, bf16[16,128]{1,0:T(8,128)(2,1)} %k_any.1, bf16[16,128]{1,0:T(8,128)(2,1)} %v_any.1), custom_call_target="tpu_custom_call" | custom-call | tf_op jit(solution)/shard_map/pallas_call | solution.py:243
  3.0 31.5 %all_to_all.25 = bf16[32,40,128]{2,1,0:T(8,128)(2,1)S(1)} all-to-all(bf16[32,40,128]{2,1,0:T(8,128)(2,1)} %get-tuple-element.17), channel_id=1, replica_groups=mesh['head'=8,'far'=32,'core'=2] {'far'}, dimensions={0} | all-to-all | bytes 655360 | tf_op jit(solution)/shard_map/all_to_all | solution.py:239
  34.5 4.8 %all-to-all-start.1 = ((bf16[8,264,128]{2,1,0:T(8,128)(2,1)}), bf16[8,264,128]{2,1,0:T(8,128)(2,1)S(1)}, u32[]{:S(2)}, u32[]{:S(2)}) async-start(bf16[8,264,128]{2,1,0:T(8,128)(2,1)} %get-tuple-element.18), calls=%async_computation.1 | async-start | bytes 1081344 | tf_op jit(solution)/shard_map/all_to_all | solution.py:239
  39.3 2.3 %all-gather = bf16[64,40,128]{2,1,0:T(8,128)(2,1)S(1)} all-gather(bf16[32,40,128]{2,1,0:T(8,128)(2,1)S(1)} %all_to_all.25), channel_id=2, replica_groups=mesh['head'=8,'far'=32,'core'=2] {'core'}, dimensions={0}, use_global_device_ids=true | all-gather | bytes 983040 | tf_op jit(solution)/shard_map/all_gather | solution.py:258
  41.6 4.6 %all-to-all-done.1.qp_ref = bf16[8,264,128]{2,1,0:T(8,128)(2,1)S(1)} async-done(((bf16[8,264,128]{2,1,0:T(8,128)(2,1)}), bf16[8,264,128]{2,1,0:T(8,128)(2,1)S(1)}, u32[]{:S(2)}, u32[]{:S(2)}) %all-to-all-start.1) | async-done | bytes 540704 | tf_op jit(solution)/shard_map/all_to_all | solution.py:239
  46.2 2.4 %shard_map.86 = (f32[8,16,128]{2,1,0:T(8,128)S(1)}, f32[1024,1024]{1,0:T(8,128)S(1)}, f32[1024,1024]{1,0:T(8,128)S(1)}, f32[4,1024]{1,0:T(4,128)S(1)}) custom-call(s32[1]{0:T(128)} %bitcast.side_ref, bf16[8,264,128]{2,1,0:T(8,128)(2,1)S(1)} %all-to-all-done.1.qp_ref, bf16[2,32,40,128]{3,2,1,0:T(8,128)(2,1)S(1)} %bitcast.2), custom_call_target="tpu_custom_call" | custom-call | tf_op jit(solution)/shard_map/pallas_call | solution.py:261
  48.6 9.3 %all_to_all.26.st_ref = f32[8,16,128]{2,1,0:T(8,128)S(1)} all-to-all(f32[8,16,128]{2,1,0:T(8,128)S(1)} %get-tuple-element.20), channel_id=1, replica_groups=mesh['head'=8,'far'=32,'core'=2] {'head'}, dimensions={0} | all-to-all | bytes 131072 | tf_op jit(solution)/shard_map/all_to_all | solution.py:239
  58.0 2.4 %shard_map.87 = (bf16[8,128,128]{2,1,0:T(8,128)(2,1)}, f32[32,32,128]{2,1,0:T(8,128)S(1)}, bf16[32,32,128]{2,1,0:T(8,128)(2,1)S(1)}) custom-call(s32[1]{0:T(128)} %bitcast.side_ref, bf16[8,264,128]{2,1,0:T(8,128)(2,1)S(1)} %all-to-all-done.1.qp_ref, bf16[2,32,40,128]{3,2,1,0:T(8,128)(2,1)S(1)} %bitcast.3, f32[8,16,128]{2,1,0:T(8,128)S(1)} %all_to_all.26.st_ref, ...), custom_call_target="tpu_custom_call" | custom-call | tf_op jit(solution)/shard_map/pallas_call | solution.py:268
  60.4 4.8 %all-to-all-start.3 = ((bf16[8,128,128]{2,1,0:T(8,128)(2,1)}), bf16[8,128,128]{2,1,0:T(8,128)(2,1)S(1)}, u32[]{:S(2)}, u32[]{:S(2)}) async-start(bf16[8,128,128]{2,1,0:T(8,128)(2,1)} %get-tuple-element.26), calls=%async_computation.3 | async-start | bytes 524288 | tf_op jit(solution)/shard_map/all_to_all | solution.py:239
  65.1 2.2 %all-gather.1 = bf16[64,32,128]{2,1,0:T(8,128)(2,1)S(1)} all-gather(bf16[32,32,128]{2,1,0:T(8,128)(2,1)S(1)} %get-tuple-element.25), channel_id=3, replica_groups=mesh['head'=8,'far'=32,'core'=2] {'core'}, dimensions={0}, use_global_device_ids=true | all-gather | bytes 786432 | tf_op jit(solution)/shard_map/all_gather | solution.py:276
  67.3 0.1 fusion
  67.4 3.3 %all-to-all-done.3.gq_ref = bf16[8,128,128]{2,1,0:T(8,128)(2,1)S(1)} async-done(((bf16[8,128,128]{2,1,0:T(8,128)(2,1)}), bf16[8,128,128]{2,1,0:T(8,128)(2,1)S(1)}, u32[]{:S(2)}, u32[]{:S(2)}) %all-to-all-start.3) | async-done | bytes 262176 | tf_op jit(solution)/shard_map/all_to_all | solution.py:239
  70.7 19.8 %all_to_all.27.gkv_ref = bf16[32,32,128]{2,1,0:T(8,128)(2,1)S(1)} all-to-all(bf16[32,32,128]{2,1,0:T(8,128)(2,1)S(1)} %fusion), channel_id=1, replica_groups=mesh['head'=8,'far'=32,'core'=2] {'far'}, dimensions={0} | all-to-all | bytes 524288 | tf_op jit(solution)/shard_map/all_to_all | solution.py:239
  90.5 0.7 shard_map.88
Async XLA Ops:
  34.5 11.7 %all-to-all-start.1 = ((bf16[8,264,128]{2,1,0:T(8,128)(2,1)}), bf16[8,264,128]{2,1,0:T(8,128)(2,1)S(1)}, u32[]{:S(2)}, u32[]{:S(2)}) async-start(bf16[8,264,128]{2,1,0:T(8,128)(2,1)} %get-tuple-element.18), calls=%async_computation.1 | async-start | bytes 1081344 | tf_op jit(solution)/shard_map/all_to_all | solution.py:239
  60.4 10.3 %all-to-all-start.3 = ((bf16[8,128,128]{2,1,0:T(8,128)(2,1)}), bf16[8,128,128]{2,1,0:T(8,128)(2,1)S(1)}, u32[]{:S(2)}, u32[]{:S(2)}) async-start(bf16[8,128,128]{2,1,0:T(8,128)(2,1)} %get-tuple-element.26), calls=%async_computation.3 | async-start | bytes 524288 | tf_op jit(solution)/shard_map/all_to_all | solution.py:239

commit v9 on v8

--- a/solution.py
+++ b/solution.py
@@ -28,54 +28,58 @@
     return lax.dot_general(a, b, (((0,), (0,)), ((), ())), preferred_element_type=jnp.float32)
 
 
-def pack_kernel(pos_any, doc_any, q_any, g_any, k_any, v_any, qp_ref, kp_hbm, *scratch):
-    bufs, sems, kp_ref, out_sem = scratch[:6], scratch[6], scratch[7], scratch[8]
-    hbm = (pos_any, doc_any, q_any, g_any, k_any, v_any)
+def fetch(hbm, bufs, sems):
     copies = [pltpu.make_async_copy(src, dst, sems.at[i]) for i, (src, dst) in enumerate(zip(hbm, bufs))]
     for copy in copies:
         copy.start()
-    for copy in copies[:2] + copies[4:]:
+    for copy in copies:
         copy.wait()
-    pos_ref, doc_ref, q_ref, g_ref, k_ref, v_ref = bufs
+
+
+def meta_rows(pos_ref, doc_ref, run, tok, item):
+    first = pos_ref[0] // run
+    docs = jnp.zeros(tok.shape, jnp.int32)
+    for t in range(run):
+        docs = jnp.where(tok == t, doc_ref[t], docs)
+    meta = jnp.where(item == 0, docs, jnp.where(item == 1, first // 16, jnp.where(item == 2, first % 16, 0)))
+    return meta.astype(jnp.float32).astype(jnp.bfloat16)
+
+
+def pack_keys_kernel(pos_any, doc_any, k_any, v_any, kp_hbm, pos_ref, doc_ref, k_ref, v_ref, sems, kp_ref, out_sem):
+    fetch((pos_any, doc_any, k_any, v_any), (pos_ref, doc_ref, k_ref, v_ref), sems)
     run, hd = k_ref.shape
-    heads = q_ref.shape[1] // hd
-    n_q, n_k = qp_ref.shape[0], kp_ref.shape[0]
-    rows = run * heads
-    first = pos_ref[0] // run
-    high, low = first // 16, first % 16
     row = lax.broadcasted_iota(jnp.int32, (META, hd), 0)
     lane = lax.broadcasted_iota(jnp.int32, (META, hd), 1)
-    tok = lane % run
-    docs = jnp.zeros((META, hd), jnp.int32)
-    for t in range(run):
-        docs = jnp.where(tok == t, doc_ref[t], docs)
-    q_meta = jnp.where(row == 0, docs, jnp.where(row == 1, high, jnp.where(row == 2, low, 0)))
     half = hd // 2
-    tok_here = jnp.where(lane >= half, row + META, row)
-    docs = jnp.zeros((META, hd), jnp.int32)
-    for t in range(run):
-        docs = jnp.where(tok_here == t, doc_ref[t], docs)
-    item = lane % half
-    k_meta = jnp.where(item == 0, docs, jnp.where(item == 1, high, jnp.where(item == 2, low, 0)))
-    q_meta = q_meta.astype(jnp.float32).astype(jnp.bfloat16)
-    k_meta = k_meta.astype(jnp.float32).astype(jnp.bfloat16)
+    meta = meta_rows(pos_ref, doc_ref, run, jnp.where(lane >= half, row + META, row), lane % half)
     k, v = k_ref[...], v_ref[...]
-    for d in range(n_k):
+    for d in range(kp_ref.shape[0]):
         kp_ref[d, 0:run, :] = k
         kp_ref[d, run : 2 * run, :] = v
-        kp_ref[d, 2 * run : 2 * run + META, :] = k_meta
+        kp_ref[d, 2 * run : 2 * run + META, :] = meta
     out = pltpu.make_async_copy(kp_ref, kp_hbm, out_sem.at[0])
     out.start()
-    for copy in copies[2:4]:
-        copy.wait()
-    for h in range(heads):
+    out.wait()
+
+
+def pack_queries_kernel(pos_any, doc_any, q_any, g_any, qp_hbm, pos_ref, doc_ref, q_ref, g_ref, sems, qp_ref, out_sem):
+    fetch((pos_any, doc_any, q_any, g_any), (pos_ref, doc_ref, q_ref, g_ref), sems)
+    n_q, block, hd = qp_ref.shape
+    rows = (block - META) // 2
+    run = q_ref.shape[0]
+    row = lax.broadcasted_iota(jnp.int32, (META, hd), 0)
+    lane = lax.broadcasted_iota(jnp.int32, (META, hd), 1)
+    meta = meta_rows(pos_ref, doc_ref, run, lane % run, row)
+    for h in range(rows // run):
         q_h = q_ref[:, h * hd : (h + 1) * hd]
         g_h = g_ref[:, h * hd : (h + 1) * hd]
         for d in range(n_q):
             qp_ref[d, h * run : (h + 1) * run, :] = q_h
             qp_ref[d, rows + h * run : rows + (h + 1) * run, :] = g_h
     for d in range(n_q):
-        qp_ref[d, 2 * rows : 2 * rows + META, :] = q_meta
+        qp_ref[d, 2 * rows : 2 * rows + META, :] = meta
+    out = pltpu.make_async_copy(qp_ref, qp_hbm, out_sem.at[0])
+    out.start()
     out.wait()
 
 
@@ -239,19 +243,21 @@
         return lax.all_to_all(x, axis, split_axis=0, concat_axis=0, tiled=True)
 
     side = lax.axis_index("core").astype(jnp.int32).reshape(1)
-    args = (positions, documents, queries, out_grad, key_vecs, value_vecs)
-    qp, kp = call(
-        pack_kernel,
-        [HBM] * 6,
-        [struct((n_q, 2 * rows + META, hd), bf), pltpu.HBM((n_k, 2 * run + META, hd), bf)],
-        [(pltpu.SMEM if a.ndim == 1 else pltpu.VMEM)(a.shape, a.dtype) for a in args]
-        + [
-            pltpu.SemaphoreType.DMA((6,)),
-            pltpu.VMEM((n_k, 2 * run + META, hd), bf),
-            pltpu.SemaphoreType.DMA((1,)),
-        ],
-        out_specs=[VMEM, HBM],
-    )(*(pltpu.with_memory_space_constraint(a, pltpu.HBM) for a in args))
+    def pack(kernel, shape, *args, cost=0):
+        (packed,) = call(
+            kernel,
+            [HBM] * len(args),
+            [pltpu.HBM(shape, bf)],
+            [(pltpu.SMEM if a.ndim == 1 else pltpu.VMEM)(a.shape, a.dtype) for a in args]
+            + [pltpu.SemaphoreType.DMA((len(args),)), pltpu.VMEM(shape, bf), pltpu.SemaphoreType.DMA((1,))],
+            out_specs=[HBM],
+            cost=cost,
+        )(*(pltpu.with_memory_space_constraint(a, pltpu.HBM) for a in args))
+        return packed
+
+    kp = pack(pack_keys_kernel, (n_k, 2 * run + META, hd), positions, documents, key_vecs, value_vecs)
+    q_shape = (n_q, 2 * rows + META, hd)
+    qp = pack(pack_queries_kernel, q_shape, positions, documents, queries, out_grad, cost=10**9)
     kp = swap(kp, "far")
     qp, kp = lax.optimization_barrier((qp, kp))
     qp = swap(qp, "head")

time: 91.7 us -> 90.8 us (level)
  the two profiles are of different devices: /device:TPU:2 before, /device:TPU:8 now
where the time goes in v9:
time: 90.8 us; the launch traced here: 90.3 us
  blocking collectives  32.4 us (36%)
  starting transfers between devices  26 us (29%)
  waiting for transfers between devices  22.3 us (25%)
  Pallas kernels  8.73 us (10%)
    all_to_all x2, blocking collectives, swap(): return lax.all_to_all(x, axis, split_axis=0, concat_axis=0, tiled=True)  28 us
    all_to_all x3, starting transfers between devices, swap(): return lax.all_to_all(x, axis, split_axis=0, concat_axis=0, tiled=True)  26 us
    all_to_all x3, waiting for transfers between devices, swap(): return lax.all_to_all(x, axis, split_axis=0, concat_axis=0, tiled=True)  22.3 us
    pallas_call x2, Pallas kernels, pack(): call(kernel, [HBM] * len(args), [pltpu.HBM(shape, bf)], [(pltpu.SMEM if a...  3.22 us
    pallas_call x1, Pallas kernels, on_device(): call(stats_kernel, [SMEM] + [VMEM] * 2, [struct((n_q, 2 * n_q, rows), f32...  2.43 us
    pallas_call x1, Pallas kernels, on_device(): call(grads_kernel, [SMEM] + [VMEM] * 6, [pltpu.HBM((n_q, rows, hd), bf),...  2.39 us
    all_gather x1, blocking collectives, on_device(): kp = lax.all_gather(kp, 'core', axis=0, tiled=False)  2.26 us
    all_gather x1, blocking collectives, on_device(): both = lax.all_gather(give, 'core', axis=0, tiled=False)  2.17 us
  transfers between devices with their start and end apart: 3, of which 3 were waited for; matrix products, arithmetic and copies ran while one was open for 0% of the time, Pallas kernels for 2%

profile of v9, /device:TPU:8, one launch (start us, length us, event | category | flops | bytes accessed | tf_op | source)
XLA Modules:
  0.0 90.3 jit_solution(7139586957555507672)
XLA Ops:
  0.6 1.5 %shard_map.86 = bf16[32,40,128]{2,1,0:T(8,128)(2,1)} custom-call(s32[16]{0:T(128)} %pos_any.3, s32[16]{0:T(128)} %doc_any.3, bf16[16,128]{1,0:T(8,128)(2,1)} %k_any.1, bf16[16,128]{1,0:T(8,128)(2,1)} %v_any.1), custom_call_target="tpu_custom_call" | custom-call | tf_op jit(solution)/shard_map/pallas_call | solution.py:247
  2.2 15.1 %all-to-all-start = ((bf16[32,40,128]{2,1,0:T(8,128)(2,1)}), bf16[32,40,128]{2,1,0:T(8,128)(2,1)S(1)}, u32[]{:S(2)}, u32[]{:S(2)}) async-start(bf16[32,40,128]{2,1,0:T(8,128)(2,1)} %shard_map.86), calls=%async_computation | async-start | bytes 655360 | tf_op jit(solution)/shard_map/all_to_all | solution.py:243
  17.2 1.7 %shard_map.85 = bf16[8,264,128]{2,1,0:T(8,128)(2,1)} custom-call(s32[16]{0:T(128)} %pos_any.3, s32[16]{0:T(128)} %doc_any.3, bf16[16,1024]{1,0:T(8,128)(2,1)} %q_any.1, bf16[16,1024]{1,0:T(8,128)(2,1)} %g_any.1), custom_call_target="tpu_custom_call" | custom-call | flops 1000000000 | tf_op jit(solution)/shard_map/pallas_call | solution.py:247
  19.0 13.1 %all-to-all-done = bf16[32,40,128]{2,1,0:T(8,128)(2,1)S(1)} async-done(((bf16[32,40,128]{2,1,0:T(8,128)(2,1)}), bf16[32,40,128]{2,1,0:T(8,128)(2,1)S(1)}, u32[]{:S(2)}, u32[]{:S(2)}) %all-to-all-start) | async-done | bytes 327712 | tf_op jit(solution)/shard_map/all_to_all | solution.py:243
  32.0 6.4 %all-to-all-start.1 = ((bf16[8,264,128]{2,1,0:T(8,128)(2,1)}), bf16[8,264,128]{2,1,0:T(8,128)(2,1)S(1)}, u32[]{:S(2)}, u32[]{:S(2)}) async-start(bf16[8,264,128]{2,1,0:T(8,128)(2,1)} %shard_map.85), calls=%async_computation.1 | async-start | bytes 1081344 | tf_op jit(solution)/shard_map/all_to_all | solution.py:243
  38.4 2.3 %all-gather = bf16[64,40,128]{2,1,0:T(8,128)(2,1)S(1)} all-gather(bf16[32,40,128]{2,1,0:T(8,128)(2,1)S(1)} %all-to-all-done), channel_id=2, replica_groups=mesh['head'=8,'far'=32,'core'=2] {'core'}, dimensions={0}, use_global_device_ids=true | all-gather | bytes 983040 | tf_op jit(solution)/shard_map/all_gather | solution.py:264
  40.6 5.3 %all-to-all-done.1.qp_ref = bf16[8,264,128]{2,1,0:T(8,128)(2,1)S(1)} async-done(((bf16[8,264,128]{2,1,0:T(8,128)(2,1)}), bf16[8,264,128]{2,1,0:T(8,128)(2,1)S(1)}, u32[]{:S(2)}, u32[]{:S(2)}) %all-to-all-start.1) | async-done | bytes 540704 | tf_op jit(solution)/shard_map/all_to_all | solution.py:243
  46.0 2.4 %shard_map.87 = (f32[8,16,128]{2,1,0:T(8,128)S(1)}, f32[1024,1024]{1,0:T(8,128)S(1)}, f32[1024,1024]{1,0:T(8,128)S(1)}, f32[4,1024]{1,0:T(4,128)S(1)}) custom-call(s32[1]{0:T(128)} %bitcast.side_ref, bf16[8,264,128]{2,1,0:T(8,128)(2,1)S(1)} %all-to-all-done.1.qp_ref, bf16[2,32,40,128]{3,2,1,0:T(8,128)(2,1)S(1)} %bitcast.2), custom_call_target="tpu_custom_call" | custom-call | tf_op jit(solution)/shard_map/pallas_call | solution.py:267
  48.4 8.8 %all_to_all.25.st_ref = f32[8,16,128]{2,1,0:T(8,128)S(1)} all-to-all(f32[8,16,128]{2,1,0:T(8,128)S(1)} %get-tuple-element.16), channel_id=1, replica_groups=mesh['head'=8,'far'=32,'core'=2] {'head'}, dimensions={0} | all-to-all | bytes 131072 | tf_op jit(solution)/shard_map/all_to_all | solution.py:243
  57.2 2.4 %shard_map.88 = (bf16[8,128,128]{2,1,0:T(8,128)(2,1)}, f32[32,32,128]{2,1,0:T(8,128)S(1)}, bf16[32,32,128]{2,1,0:T(8,128)(2,1)S(1)}) custom-call(s32[1]{0:T(128)} %bitcast.side_ref, bf16[8,264,128]{2,1,0:T(8,128)(2,1)S(1)} %all-to-all-done.1.qp_ref, bf16[2,32,40,128]{3,2,1,0:T(8,128)(2,1)S(1)} %bitcast.3, f32[8,16,128]{2,1,0:T(8,128)S(1)} %all_to_all.25.st_ref, ...), custom_call_target="tpu_custom_call" | custom-call | tf_op jit(solution)/shard_map/pallas_call | solution.py:274
  59.6 4.6 %all-to-all-start.3 = ((bf16[8,128,128]{2,1,0:T(8,128)(2,1)}), bf16[8,128,128]{2,1,0:T(8,128)(2,1)S(1)}, u32[]{:S(2)}, u32[]{:S(2)}) async-start(bf16[8,128,128]{2,1,0:T(8,128)(2,1)} %get-tuple-element.22), calls=%async_computation.3 | async-start | bytes 524288 | tf_op jit(solution)/shard_map/all_to_all | solution.py:243
  64.2 2.2 %all-gather.1 = bf16[64,32,128]{2,1,0:T(8,128)(2,1)S(1)} all-gather(bf16[32,32,128]{2,1,0:T(8,128)(2,1)S(1)} %get-tuple-element.21), channel_id=3, replica_groups=mesh['head'=8,'far'=32,'core'=2] {'core'}, dimensions={0}, use_global_device_ids=true | all-gather | bytes 786432 | tf_op jit(solution)/shard_map/all_gather | solution.py:282
  66.4 0.1 fusion
  66.5 3.9 %all-to-all-done.3.gq_ref = bf16[8,128,128]{2,1,0:T(8,128)(2,1)S(1)} async-done(((bf16[8,128,128]{2,1,0:T(8,128)(2,1)}), bf16[8,128,128]{2,1,0:T(8,128)(2,1)S(1)}, u32[]{:S(2)}, u32[]{:S(2)}) %all-to-all-start.3) | async-done | bytes 262176 | tf_op jit(solution)/shard_map/all_to_all | solution.py:243
  70.4 19.2 %all_to_all.26.gkv_ref = bf16[32,32,128]{2,1,0:T(8,128)(2,1)S(1)} all-to-all(bf16[32,32,128]{2,1,0:T(8,128)(2,1)S(1)} %fusion), channel_id=1, replica_groups=mesh['head'=8,'far'=32,'core'=2] {'far'}, dimensions={0} | all-to-all | bytes 524288 | tf_op jit(solution)/shard_map/all_to_all | solution.py:243
  89.6 0.7 shard_map.89
Async XLA Ops:
  2.2 29.9 %all-to-all-start = ((bf16[32,40,128]{2,1,0:T(8,128)(2,1)}), bf16[32,40,128]{2,1,0:T(8,128)(2,1)S(1)}, u32[]{:S(2)}, u32[]{:S(2)}) async-start(bf16[32,40,128]{2,1,0:T(8,128)(2,1)} %shard_map.86), calls=%async_computation | async-start | bytes 655360 | tf_op jit(solution)/shard_map/all_to_all | solution.py:243
  32.0 14.0 %all-to-all-start.1 = ((bf16[8,264,128]{2,1,0:T(8,128)(2,1)}), bf16[8,264,128]{2,1,0:T(8,128)(2,1)S(1)}, u32[]{:S(2)}, u32[]{:S(2)}) async-start(bf16[8,264,128]{2,1,0:T(8,128)(2,1)} %shard_map.85), calls=%async_computation.1 | async-start | bytes 1081344 | tf_op jit(solution)/shard_map/all_to_all | solution.py:243
  59.6 10.8 %all-to-all-start.3 = ((bf16[8,128,128]{2,1,0:T(8,128)(2,1)}), bf16[8,128,128]{2,1,0:T(8,128)(2,1)S(1)}, u32[]{:S(2)}, u32[]{:S(2)}) async-start(bf16[8,128,128]{2,1,0:T(8,128)(2,1)} %get-tuple-element.22), calls=%async_computation.3 | async-start | bytes 524288 | tf_op jit(solution)/shard_map/all_to_all | solution.py:243

commit v10 on v9

--- a/solution.py
+++ b/solution.py
@@ -231,7 +231,7 @@
 
 
 def on_device(queries, key_vecs, value_vecs, out_grad, positions, documents):
-    n_q, n_k = lax.axis_size("head"), lax.axis_size("far")
+    n_q, n_k = lax.axis_size("x") * 2, lax.axis_size("far")
     run, hd = key_vecs.shape
     heads = queries.shape[1] // hd
     rows = run * heads
@@ -256,11 +256,13 @@
         return packed
 
     kp = pack(pack_keys_kernel, (n_k, 2 * run + META, hd), positions, documents, key_vecs, value_vecs)
-    q_shape = (n_q, 2 * rows + META, hd)
+    q_shape = (1, 2 * rows + META, hd)
     qp = pack(pack_queries_kernel, q_shape, positions, documents, queries, out_grad, cost=10**9)
     kp = swap(kp, "far")
+    qp = lax.all_gather(qp, "near", axis=0, tiled=True)
+    qp = jnp.broadcast_to(qp[None], (n_q // 2, *qp.shape))
     qp, kp = lax.optimization_barrier((qp, kp))
-    qp = swap(qp, "head")
+    qp = swap(qp, "x").reshape(n_q, 2 * rows + META, hd)
     kp = lax.all_gather(kp, "core", axis=0, tiled=False)
     full = struct((2 * keys, n_q * rows), f32)
     line = pltpu.VMEM((n_q, rows), f32)
@@ -270,7 +272,7 @@
         [struct((n_q, 2 * n_q, rows), f32), full, full, struct((2 * keys // CHUNK, n_q * rows), f32)],
         [pltpu.VMEM((2 * keys, hd), f32)],
     )(side, qp, kp)
-    st = swap(st, "head")
+    st = swap(st, ("x", "near"))
     gq, keep, give = call(
         grads_kernel,
         [SMEM] + [VMEM] * 6,
@@ -278,7 +280,7 @@
         [line, line, pltpu.VMEM(full.shape, bf), pltpu.VMEM((n_q, rows, hd), bf), pltpu.SemaphoreType.DMA((1,))],
         out_specs=[HBM, VMEM, VMEM],
     )(side, qp, kp, st, e, dp, top)
-    gq = swap(gq, "head")
+    gq = swap(gq, ("x", "near"))
     both = lax.all_gather(give, "core", axis=0, tiled=False)
     gkv = (keep + jnp.where(side[0] == 0, both[1], both[0]).astype(f32)).astype(bf)
     gkv, gq = lax.optimization_barrier((gkv, gq))
@@ -294,9 +296,9 @@
 
 def solution(mesh):
     n_head, n_ctx = mesh.devices.shape
-    fine = Mesh(mesh.devices.reshape(n_head, n_ctx // 2, 2), ("head", "far", "core"))
-    tok = P(("head", "far", "core"))
-    two = P(("head", "far", "core"), None)
+    every = ("x", "near", "far", "core")
+    fine = Mesh(mesh.devices.reshape(n_head // 2, 2, n_ctx // 2, 2), every)
+    tok, two = P(every), P(every, None)
     return jax.shard_map(
         on_device,
         mesh=fine,

time: 90.8 us -> 91.2 us (level)
  blocking collectives: 32.4 us -> 40.7 us
  waiting for transfers between devices: 22.3 us -> 15.9 us
  starting transfers between devices: 26 us -> 24 us
    all_gather x0 -> x1, blocking collectives: none -> 8.22 us  [on_device(): qp = lax.all_gather(qp, 'near', axis=0, tiled=True)]
    all_to_all x3, waiting for transfers between devices: 22.3 us -> 15.9 us  [swap(): return lax.all_to_all(x, axis, split_axis=0, concat_axis=0, tiled=True)]
    all_to_all x3, starting transfers between devices: 26 us -> 24 us  [swap(): return lax.all_to_all(x, axis, split_axis=0, concat_axis=0, tiled=True)]
where the time goes in v10:
time: 91.2 us; the launch traced here: 90.7 us
  blocking collectives  40.7 us (45%)
  starting transfers between devices  24 us (26%)
  waiting for transfers between devices  15.9 us (17%)
  Pallas kernels  8.5 us (9%)
    all_to_all x2, blocking collectives, swap(): return lax.all_to_all(x, axis, split_axis=0, concat_axis=0, tiled=True)  28 us
    all_to_all x3, starting transfers between devices, swap(): return lax.all_to_all(x, axis, split_axis=0, concat_axis=0, tiled=True)  24 us
    all_to_all x3, waiting for transfers between devices, swap(): return lax.all_to_all(x, axis, split_axis=0, concat_axis=0, tiled=True)  15.9 us
    all_gather x1, blocking collectives, on_device(): qp = lax.all_gather(qp, 'near', axis=0, tiled=True)  8.22 us
    pallas_call x2, Pallas kernels, pack(): call(kernel, [HBM] * len(args), [pltpu.HBM(shape, bf)], [(pltpu.SMEM if a...  2.99 us
    pallas_call x1, Pallas kernels, on_device(): call(stats_kernel, [SMEM] + [VMEM] * 2, [struct((n_q, 2 * n_q, rows), f32...  2.43 us
    pallas_call x1, Pallas kernels, on_device(): call(grads_kernel, [SMEM] + [VMEM] * 6, [pltpu.HBM((n_q, rows, hd), bf),...  2.39 us
    all_gather x1, blocking collectives, on_device(): kp = lax.all_gather(kp, 'core', axis=0, tiled=False)  2.26 us
  transfers between devices with their start and end apart: 3, of which 3 were waited for; matrix products, arithmetic and copies ran while one was open for 0% of the time, Pallas kernels for 2%

profile of v10, /device:TPU:8, one launch (start us, length us, event | category | flops | bytes accessed | tf_op | source)
XLA Modules:
  0.0 90.7 jit_solution(4818688846630657153)
XLA Ops:
  0.6 1.5 %shard_map.86 = bf16[32,40,128]{2,1,0:T(8,128)(2,1)} custom-call(s32[16]{0:T(128)} %pos_any.3, s32[16]{0:T(128)} %doc_any.3, bf16[16,128]{1,0:T(8,128)(2,1)} %k_any.1, bf16[16,128]{1,0:T(8,128)(2,1)} %v_any.1), custom_call_target="tpu_custom_call" | custom-call | tf_op jit(solution)/shard_map/pallas_call | solution.py:247
  2.2 15.1 %all-to-all-start = ((bf16[32,40,128]{2,1,0:T(8,128)(2,1)}), bf16[32,40,128]{2,1,0:T(8,128)(2,1)S(1)}, u32[]{:S(2)}, u32[]{:S(2)}) async-start(bf16[32,40,128]{2,1,0:T(8,128)(2,1)} %shard_map.86), calls=%async_computation | async-start | bytes 655360 | tf_op jit(solution)/shard_map/all_to_all | solution.py:243
  17.2 1.5 %shard_map.85 = bf16[1,264,128]{2,1,0:T(8,128)(2,1)} custom-call(s32[16]{0:T(128)} %pos_any.3, s32[16]{0:T(128)} %doc_any.3, bf16[16,1024]{1,0:T(8,128)(2,1)} %q_any.1, bf16[16,1024]{1,0:T(8,128)(2,1)} %g_any.1), custom_call_target="tpu_custom_call" | custom-call | flops 1000000000 | tf_op jit(solution)/shard_map/pallas_call | solution.py:247
  18.7 8.2 %all_gather.15 = bf16[2,264,128]{2,1,0:T(8,128)(2,1)S(1)} all-gather(bf16[1,264,128]{2,1,0:T(8,128)(2,1)} %shard_map.85), channel_id=1, replica_groups=mesh['x'=4,'near'=2,'far'=32,'core'=2] {'near'}, dimensions={0}, use_global_device_ids=true | all-gather | bytes 202752 | tf_op jit(solution)/shard_map/all_gather | solution.py:262
  26.9 6.1 %all-to-all-done = bf16[32,40,128]{2,1,0:T(8,128)(2,1)S(1)} async-done(((bf16[32,40,128]{2,1,0:T(8,128)(2,1)}), bf16[32,40,128]{2,1,0:T(8,128)(2,1)S(1)}, u32[]{:S(2)}, u32[]{:S(2)}) %all-to-all-start) | async-done | bytes 327712 | tf_op jit(solution)/shard_map/all_to_all | solution.py:243
  33.1 0.9 broadcast_in_dim.2
  33.9 4.3 %all-to-all-start.1 = ((bf16[4,2,264,128]{3,2,1,0:T(8,128)(2,1)}), bf16[4,2,264,128]{3,2,1,0:T(8,128)(2,1)S(1)}, u32[]{:S(2)}, u32[]{:S(2)}) async-start(bf16[4,2,264,128]{3,2,1,0:T(8,128)(2,1)} %broadcast_in_dim.2), calls=%async_computation.1 | async-start | bytes 1081344 | tf_op jit(solution)/shard_map/all_to_all | solution.py:243
  38.2 2.3 %all-gather = bf16[64,40,128]{2,1,0:T(8,128)(2,1)S(1)} all-gather(bf16[32,40,128]{2,1,0:T(8,128)(2,1)S(1)} %all-to-all-done), channel_id=2, replica_groups=mesh['x'=4,'near'=2,'far'=32,'core'=2] {'core'}, dimensions={0}, use_global_device_ids=true | all-gather | bytes 983040 | tf_op jit(solution)/shard_map/all_gather | solution.py:266
  40.5 5.9 %all-to-all-done.1 = bf16[4,2,264,128]{3,2,1,0:T(8,128)(2,1)S(1)} async-done(((bf16[4,2,264,128]{3,2,1,0:T(8,128)(2,1)}), bf16[4,2,264,128]{3,2,1,0:T(8,128)(2,1)S(1)}, u32[]{:S(2)}, u32[]{:S(2)}) %all-to-all-start.1) | async-done | bytes 540704 | tf_op jit(solution)/shard_map/all_to_all | solution.py:243
  46.4 2.4 %shard_map.87 = (f32[8,16,128]{2,1,0:T(8,128)S(1)}, f32[1024,1024]{1,0:T(8,128)S(1)}, f32[1024,1024]{1,0:T(8,128)S(1)}, f32[4,1024]{1,0:T(4,128)S(1)}) custom-call(s32[1]{0:T(128)} %bitcast.side_ref, bf16[8,264,128]{2,1,0:T(8,128)(2,1)S(1)} %bitcast.5, bf16[2,32,40,128]{3,2,1,0:T(8,128)(2,1)S(1)} %bitcast.3), custom_call_target="tpu_custom_call" | custom-call | tf_op jit(solution)/shard_map/pallas_call | solution.py:269
  48.8 9.0 %all_to_all.25.st_ref = f32[8,16,128]{2,1,0:T(8,128)S(1)} all-to-all(f32[8,16,128]{2,1,0:T(8,128)S(1)} %get-tuple-element.16), channel_id=1, replica_groups=mesh['x'=4,'near'=2,'far'=32,'core'=2] {'x','near'}, dimensions={0} | all-to-all | bytes 131072 | tf_op jit(solution)/shard_map/all_to_all | solution.py:243
  57.9 2.4 %shard_map.88 = (bf16[8,128,128]{2,1,0:T(8,128)(2,1)}, f32[32,32,128]{2,1,0:T(8,128)S(1)}, bf16[32,32,128]{2,1,0:T(8,128)(2,1)S(1)}) custom-call(s32[1]{0:T(128)} %bitcast.side_ref, bf16[8,264,128]{2,1,0:T(8,128)(2,1)S(1)} %bitcast.6, bf16[2,32,40,128]{3,2,1,0:T(8,128)(2,1)S(1)} %bitcast.4, f32[8,16,128]{2,1,0:T(8,128)S(1)} %all_to_all.25.st_ref, ...), custom_call_target="tpu_custom_call" | custom-call | tf_op jit(solution)/shard_map/pallas_call | solution.py:276
  60.2 4.6 %all-to-all-start.3 = ((bf16[8,128,128]{2,1,0:T(8,128)(2,1)}), bf16[8,128,128]{2,1,0:T(8,128)(2,1)S(1)}, u32[]{:S(2)}, u32[]{:S(2)}) async-start(bf16[8,128,128]{2,1,0:T(8,128)(2,1)} %get-tuple-element.22), calls=%async_computation.3 | async-start | bytes 524288 | tf_op jit(solution)/shard_map/all_to_all | solution.py:243
  64.9 2.2 %all-gather.1 = bf16[64,32,128]{2,1,0:T(8,128)(2,1)S(1)} all-gather(bf16[32,32,128]{2,1,0:T(8,128)(2,1)S(1)} %get-tuple-element.21), channel_id=3, replica_groups=mesh['x'=4,'near'=2,'far'=32,'core'=2] {'core'}, dimensions={0}, use_global_device_ids=true | all-gather | bytes 786432 | tf_op jit(solution)/shard_map/all_gather | solution.py:284
  67.0 0.1 fusion
  67.1 3.9 %all-to-all-done.3.gq_ref = bf16[8,128,128]{2,1,0:T(8,128)(2,1)S(1)} async-done(((bf16[8,128,128]{2,1,0:T(8,128)(2,1)}), bf16[8,128,128]{2,1,0:T(8,128)(2,1)S(1)}, u32[]{:S(2)}, u32[]{:S(2)}) %all-to-all-start.3) | async-done | bytes 262176 | tf_op jit(solution)/shard_map/all_to_all | solution.py:243
  71.0 19.0 %all_to_all.26.gkv_ref = bf16[32,32,128]{2,1,0:T(8,128)(2,1)S(1)} all-to-all(bf16[32,32,128]{2,1,0:T(8,128)(2,1)S(1)} %fusion), channel_id=1, replica_groups=mesh['x'=4,'near'=2,'far'=32,'core'=2] {'far'}, dimensions={0} | all-to-all | bytes 524288 | tf_op jit(solution)/shard_map/all_to_all | solution.py:243
  90.0 0.7 shard_map.89
Async XLA Ops:
  2.2 30.9 %all-to-all-start = ((bf16[32,40,128]{2,1,0:T(8,128)(2,1)}), bf16[32,40,128]{2,1,0:T(8,128)(2,1)S(1)}, u32[]{:S(2)}, u32[]{:S(2)}) async-start(bf16[32,40,128]{2,1,0:T(8,128)(2,1)} %shard_map.86), calls=%async_computation | async-start | bytes 655360 | tf_op jit(solution)/shard_map/all_to_all | solution.py:243
  33.9 12.5 %all-to-all-start.1 = ((bf16[4,2,264,128]{3,2,1,0:T(8,128)(2,1)}), bf16[4,2,264,128]{3,2,1,0:T(8,128)(2,1)S(1)}, u32[]{:S(2)}, u32[]{:S(2)}) async-start(bf16[4,2,264,128]{3,2,1,0:T(8,128)(2,1)} %broadcast_in_dim.2), calls=%async_computation.1 | async-start | bytes 1081344 | tf_op jit(solution)/shard_map/all_to_all | solution.py:243
  60.2 10.8 %all-to-all-start.3 = ((bf16[8,128,128]{2,1,0:T(8,128)(2,1)}), bf16[8,128,128]{2,1,0:T(8,128)(2,1)S(1)}, u32[]{:S(2)}, u32[]{:S(2)}) async-start(bf16[8,128,128]{2,1,0:T(8,128)(2,1)} %get-tuple-element.22), calls=%async_computation.3 | async-start | bytes 524288 | tf_op jit(solution)/shard_map/all_to_all | solution.py:243

commit v11 on v9

--- a/solution.py
+++ b/solution.py
@@ -109,7 +109,14 @@
     return base, base + meta[1:2] * (run * 16.0) + meta[2:3] * float(run) + tok
 
 
-def stats_kernel(side_ref, qp_ref, kp_ref, out_ref, e_ref, dp_ref, top_ref, code_ref):
+def codes_kernel(side_ref, kp_ref, code_ref):
+    run = (kp_ref.shape[2] - META) // 2
+    half = kp_ref.shape[1] * run
+    for i, core in enumerate((side_ref[0], 1 - side_ref[0])):
+        code_ref[i * half : (i + 1) * half, :] = key_codes(kp_ref.at[core], run)
+
+
+def stats_kernel(side_ref, qp_ref, kp_ref, code_ref, out_ref, e_ref, dp_ref, top_ref):
     n_q, block, hd = qp_ref.shape
     _, n_k, kp_rows, _ = kp_ref.shape
     rows = (block - META) // 2
@@ -118,8 +125,6 @@
     half = n_k * run
     per = CHUNK // run
     cores = (side_ref[0], 1 - side_ref[0])
-    for i, core in enumerate(cores):
-        code_ref[i * half : (i + 1) * half, :] = key_codes(kp_ref.at[core], run)
     for d in range(0, n_q, 2):
         q = qp_ref[d : d + 2, 0:rows, :].reshape(2 * rows, hd)
         g = qp_ref[d : d + 2, rows : 2 * rows, :].reshape(2 * rows, hd)
@@ -262,14 +267,14 @@
     qp, kp = lax.optimization_barrier((qp, kp))
     qp = swap(qp, "head")
     kp = lax.all_gather(kp, "core", axis=0, tiled=False)
+    (code,) = call(codes_kernel, [SMEM, VMEM], [struct((2 * keys, hd), f32)])(side, kp)
     full = struct((2 * keys, n_q * rows), f32)
     line = pltpu.VMEM((n_q, rows), f32)
     st, e, dp, top = call(
         stats_kernel,
-        [SMEM] + [VMEM] * 2,
+        [SMEM] + [VMEM] * 3,
         [struct((n_q, 2 * n_q, rows), f32), full, full, struct((2 * keys // CHUNK, n_q * rows), f32)],
-        [pltpu.VMEM((2 * keys, hd), f32)],
-    )(side, qp, kp)
+    )(side, qp, kp, code)
     st = swap(st, "head")
     gq, keep, give = call(
         grads_kernel,

time: 90.8 us -> 90.8 us (level)
  the two profiles are of different devices: /device:TPU:8 before, /device:TPU:2 now
where the time goes in v11:
time: 90.8 us; the launch traced here: 90.2 us
  blocking collectives  33.5 us (37%)
  starting transfers between devices  25.6 us (28%)
  waiting for transfers between devices  21.5 us (24%)
  Pallas kernels  8.83 us (10%)
    all_to_all x2, blocking collectives, swap(): return lax.all_to_all(x, axis, split_axis=0, concat_axis=0, tiled=True)  29.1 us
    all_to_all x3, starting transfers between devices, swap(): return lax.all_to_all(x, axis, split_axis=0, concat_axis=0, tiled=True)  25.6 us
    all_to_all x3, waiting for transfers between devices, swap(): return lax.all_to_all(x, axis, split_axis=0, concat_axis=0, tiled=True)  21.5 us
    pallas_call x2, Pallas kernels, pack(): call(kernel, [HBM] * len(args), [pltpu.HBM(shape, bf)], [(pltpu.SMEM if a...  3.22 us
    pallas_call x1, Pallas kernels, on_device(): call(grads_kernel, [SMEM] + [VMEM] * 6, [pltpu.HBM((n_q, rows, hd), bf),...  2.39 us
    pallas_call x1, Pallas kernels, on_device(): call(stats_kernel, [SMEM] + [VMEM] * 3, [struct((n_q, 2 * n_q, rows), f32...  2.33 us
    all_gather x1, blocking collectives, on_device(): kp = lax.all_gather(kp, 'core', axis=0, tiled=False)  2.26 us
    all_gather x1, blocking collectives, on_device(): both = lax.all_gather(give, 'core', axis=0, tiled=False)  2.17 us
  transfers between devices with their start and end apart: 3, of which 3 were waited for; matrix products, arithmetic and copies ran while one was open for 0% of the time, Pallas kernels for 2%

profile of v11, /device:TPU:2, one launch (start us, length us, event | category | flops | bytes accessed | tf_op | source)
XLA Modules:
  0.0 90.2 jit_solution(15755484871417518883)
XLA Ops:
  0.6 1.5 %shard_map.86 = bf16[32,40,128]{2,1,0:T(8,128)(2,1)} custom-call(s32[16]{0:T(128)} %pos_any.3, s32[16]{0:T(128)} %doc_any.3, bf16[16,128]{1,0:T(8,128)(2,1)} %k_any.1, bf16[16,128]{1,0:T(8,128)(2,1)} %v_any.1), custom_call_target="tpu_custom_call" | custom-call | tf_op jit(solution)/shard_map/pallas_call | solution.py:252
  2.2 16.0 %all-to-all-start = ((bf16[32,40,128]{2,1,0:T(8,128)(2,1)}), bf16[32,40,128]{2,1,0:T(8,128)(2,1)S(1)}, u32[]{:S(2)}, u32[]{:S(2)}) async-start(bf16[32,40,128]{2,1,0:T(8,128)(2,1)} %shard_map.86), calls=%async_computation | async-start | bytes 655360 | tf_op jit(solution)/shard_map/all_to_all | solution.py:248
  18.1 1.7 %shard_map.85 = bf16[8,264,128]{2,1,0:T(8,128)(2,1)} custom-call(s32[16]{0:T(128)} %pos_any.3, s32[16]{0:T(128)} %doc_any.3, bf16[16,1024]{1,0:T(8,128)(2,1)} %q_any.1, bf16[16,1024]{1,0:T(8,128)(2,1)} %g_any.1), custom_call_target="tpu_custom_call" | custom-call | flops 1000000000 | tf_op jit(solution)/shard_map/pallas_call | solution.py:252
  19.9 13.8 %all-to-all-done = bf16[32,40,128]{2,1,0:T(8,128)(2,1)S(1)} async-done(((bf16[32,40,128]{2,1,0:T(8,128)(2,1)}), bf16[32,40,128]{2,1,0:T(8,128)(2,1)S(1)}, u32[]{:S(2)}, u32[]{:S(2)}) %all-to-all-start) | async-done | bytes 327712 | tf_op jit(solution)/shard_map/all_to_all | solution.py:248
  33.6 4.8 %all-to-all-start.1 = ((bf16[8,264,128]{2,1,0:T(8,128)(2,1)}), bf16[8,264,128]{2,1,0:T(8,128)(2,1)S(1)}, u32[]{:S(2)}, u32[]{:S(2)}) async-start(bf16[8,264,128]{2,1,0:T(8,128)(2,1)} %shard_map.85), calls=%async_computation.1 | async-start | bytes 1081344 | tf_op jit(solution)/shard_map/all_to_all | solution.py:248
  38.5 2.3 %all-gather = bf16[64,40,128]{2,1,0:T(8,128)(2,1)S(1)} all-gather(bf16[32,40,128]{2,1,0:T(8,128)(2,1)S(1)} %all-to-all-done), channel_id=2, replica_groups=mesh['head'=8,'far'=32,'core'=2] {'core'}, dimensions={0}, use_global_device_ids=true | all-gather | bytes 983040 | tf_op jit(solution)/shard_map/all_gather | solution.py:269
  40.7 0.2 shard_map.87.code_ref
  40.9 4.4 %all-to-all-done.1.qp_ref = bf16[8,264,128]{2,1,0:T(8,128)(2,1)S(1)} async-done(((bf16[8,264,128]{2,1,0:T(8,128)(2,1)}), bf16[8,264,128]{2,1,0:T(8,128)(2,1)S(1)}, u32[]{:S(2)}, u32[]{:S(2)}) %all-to-all-start.1) | async-done | bytes 540704 | tf_op jit(solution)/shard_map/all_to_all | solution.py:248
  45.4 2.3 %shard_map.88 = (f32[8,16,128]{2,1,0:T(8,128)S(1)}, f32[1024,1024]{1,0:T(8,128)S(1)}, f32[1024,1024]{1,0:T(8,128)S(1)}, f32[4,1024]{1,0:T(4,128)S(1)}) custom-call(s32[1]{0:T(128)} %bitcast.side_ref, bf16[8,264,128]{2,1,0:T(8,128)(2,1)S(1)} %all-to-all-done.1.qp_ref, bf16[2,32,40,128]{3,2,1,0:T(8,128)(2,1)S(1)} %bitcast.3, f32[1024,128]{1,0:T(8,128)S(1)} %shard_map.87.code_ref), custom_call_target="tpu_custom_call" | custom-call | tf_op jit(solution)/shard_map/pallas_call | solution.py:273
  47.7 9.3 %all_to_all.25.st_ref = f32[8,16,128]{2,1,0:T(8,128)S(1)} all-to-all(f32[8,16,128]{2,1,0:T(8,128)S(1)} %get-tuple-element.16), channel_id=1, replica_groups=mesh['head'=8,'far'=32,'core'=2] {'head'}, dimensions={0} | all-to-all | bytes 131072 | tf_op jit(solution)/shard_map/all_to_all | solution.py:248
  57.0 2.4 %shard_map.89 = (bf16[8,128,128]{2,1,0:T(8,128)(2,1)}, f32[32,32,128]{2,1,0:T(8,128)S(1)}, bf16[32,32,128]{2,1,0:T(8,128)(2,1)S(1)}) custom-call(s32[1]{0:T(128)} %bitcast.side_ref, bf16[8,264,128]{2,1,0:T(8,128)(2,1)S(1)} %all-to-all-done.1.qp_ref, bf16[2,32,40,128]{3,2,1,0:T(8,128)(2,1)S(1)} %bitcast.4, f32[8,16,128]{2,1,0:T(8,128)S(1)} %all_to_all.25.st_ref, ...), custom_call_target="tpu_custom_call" | custom-call | tf_op jit(solution)/shard_map/pallas_call | solution.py:279
  59.4 4.8 %all-to-all-start.3 = ((bf16[8,128,128]{2,1,0:T(8,128)(2,1)}), bf16[8,128,128]{2,1,0:T(8,128)(2,1)S(1)}, u32[]{:S(2)}, u32[]{:S(2)}) async-start(bf16[8,128,128]{2,1,0:T(8,128)(2,1)} %get-tuple-element.22), calls=%async_computation.3 | async-start | bytes 524288 | tf_op jit(solution)/shard_map/all_to_all | solution.py:248
  64.2 2.2 %all-gather.1 = bf16[64,32,128]{2,1,0:T(8,128)(2,1)S(1)} all-gather(bf16[32,32,128]{2,1,0:T(8,128)(2,1)S(1)} %get-tuple-element.21), channel_id=3, replica_groups=mesh['head'=8,'far'=32,'core'=2] {'core'}, dimensions={0}, use_global_device_ids=true | all-gather | bytes 786432 | tf_op jit(solution)/shard_map/all_gather | solution.py:287
  66.4 0.1 fusion
  66.5 3.3 %all-to-all-done.3.gq_ref = bf16[8,128,128]{2,1,0:T(8,128)(2,1)S(1)} async-done(((bf16[8,128,128]{2,1,0:T(8,128)(2,1)}), bf16[8,128,128]{2,1,0:T(8,128)(2,1)S(1)}, u32[]{:S(2)}, u32[]{:S(2)}) %all-to-all-start.3) | async-done | bytes 262176 | tf_op jit(solution)/shard_map/all_to_all | solution.py:248
  69.7 19.8 %all_to_all.26.gkv_ref = bf16[32,32,128]{2,1,0:T(8,128)(2,1)S(1)} all-to-all(bf16[32,32,128]{2,1,0:T(8,128)(2,1)S(1)} %fusion), channel_id=1, replica_groups=mesh['head'=8,'far'=32,'core'=2] {'far'}, dimensions={0} | all-to-all | bytes 524288 | tf_op jit(solution)/shard_map/all_to_all | solution.py:248
  89.5 0.7 shard_map.90
Async XLA Ops:
  2.2 31.5 %all-to-all-start = ((bf16[32,40,128]{2,1,0:T(8,128)(2,1)}), bf16[32,40,128]{2,1,0:T(8,128)(2,1)S(1)}, u32[]{:S(2)}, u32[]{:S(2)}) async-start(bf16[32,40,128]{2,1,0:T(8,128)(2,1)} %shard_map.86), calls=%async_computation | async-start | bytes 655360 | tf_op jit(solution)/shard_map/all_to_all | solution.py:248
  33.6 11.7 %all-to-all-start.1 = ((bf16[8,264,128]{2,1,0:T(8,128)(2,1)}), bf16[8,264,128]{2,1,0:T(8,128)(2,1)S(1)}, u32[]{:S(2)}, u32[]{:S(2)}) async-start(bf16[8,264,128]{2,1,0:T(8,128)(2,1)} %shard_map.85), calls=%async_computation.1 | async-start | bytes 1081344 | tf_op jit(solution)/shard_map/all_to_all | solution.py:248
  59.4 10.3 %all-to-all-start.3 = ((bf16[8,128,128]{2,1,0:T(8,128)(2,1)}), bf16[8,128,128]{2,1,0:T(8,128)(2,1)S(1)}, u32[]{:S(2)}, u32[]{:S(2)}) async-start(bf16[8,128,128]{2,1,0:T(8,128)(2,1)} %get-tuple-element.22), calls=%async_computation.3 | async-start | bytes 524288 | tf_op jit(solution)/shard_map/all_to_all | solution.py:248

commit v12 on v9

--- a/solution.py
+++ b/solution.py
@@ -203,11 +203,16 @@
     out.wait()
 
 
-def finish_kernel(gq_ref, gkv_ref, oq_ref, ok_ref, ov_ref):
-    run, hd = ok_ref.shape
+def finish_queries_kernel(gq_ref, oq_ref):
+    run = gq_ref.shape[1] * gq_ref.shape[2] // oq_ref.shape[1]
+    hd = gq_ref.shape[2]
     gq = jnp.sum(gq_ref[...].astype(jnp.float32), axis=0)
     for h in range(oq_ref.shape[1] // hd):
         oq_ref[:, h * hd : (h + 1) * hd] = gq[h * run : (h + 1) * run, :]
+
+
+def finish_keys_kernel(gkv_ref, ok_ref, ov_ref):
+    run = ok_ref.shape[0]
     gkv = jnp.sum(gkv_ref[...].astype(jnp.float32), axis=0)
     ok_ref[...] = gkv[:run]
     ov_ref[...] = gkv[run:]
@@ -283,13 +288,9 @@
     gkv = (keep + jnp.where(side[0] == 0, both[1], both[0]).astype(f32)).astype(bf)
     gkv, gq = lax.optimization_barrier((gkv, gq))
     gkv = swap(gkv, "far")
-    return tuple(
-        call(
-            finish_kernel,
-            [VMEM] * 2,
-            [struct((run, heads * hd), f32), struct((run, hd), f32), struct((run, hd), f32)],
-        )(gq, gkv)
-    )
+    (oq,) = call(finish_queries_kernel, [VMEM], [struct((run, heads * hd), f32)], cost=10**9)(gq)
+    ok, ov = call(finish_keys_kernel, [VMEM], [struct((run, hd), f32)] * 2)(gkv)
+    return oq, ok, ov
 
 
 def solution(mesh):

time: 90.8 us -> 91.1 us (level)
  the two profiles are of different devices: /device:TPU:8 before, /device:TPU:2 now
where the time goes in v12:
time: 91.1 us; the launch traced here: 90.5 us
  waiting for transfers between devices  34 us (37%)
  starting transfers between devices  31.9 us (35%)
  blocking collectives  13.7 us (15%)
  Pallas kernels  9.37 us (10%)
    all_to_all x4, waiting for transfers between devices, swap(): return lax.all_to_all(x, axis, split_axis=0, concat_axis=0, tiled=True)  34 us
    all_to_all x4, starting transfers between devices, swap(): return lax.all_to_all(x, axis, split_axis=0, concat_axis=0, tiled=True)  31.9 us
    all_to_all x1, blocking collectives, swap(): return lax.all_to_all(x, axis, split_axis=0, concat_axis=0, tiled=True)  9.31 us
    pallas_call x2, Pallas kernels, pack(): call(kernel, [HBM] * len(args), [pltpu.HBM(shape, bf)], [(pltpu.SMEM if a...  3.22 us
    pallas_call x1, Pallas kernels, on_device(): call(stats_kernel, [SMEM] + [VMEM] * 2, [struct((n_q, 2 * n_q, rows), f32...  2.43 us
    pallas_call x1, Pallas kernels, on_device(): call(grads_kernel, [SMEM] + [VMEM] * 6, [pltpu.HBM((n_q, rows, hd), bf),...  2.4 us
    all_gather x1, blocking collectives, on_device(): kp = lax.all_gather(kp, 'core', axis=0, tiled=False)  2.26 us
    all_gather x1, blocking collectives, on_device(): both = lax.all_gather(give, 'core', axis=0, tiled=False)  2.17 us
  transfers between devices with their start and end apart: 4, of which 4 were waited for; matrix products, arithmetic and copies ran while one was open for 1% of the time, Pallas kernels for 3%

profile of v12, /device:TPU:2, one launch (start us, length us, event | category | flops | bytes accessed | tf_op | source)
XLA Modules:
  0.0 90.5 jit_solution(832729375033489813)
XLA Ops:
  0.6 1.5 %shard_map.86 = bf16[32,40,128]{2,1,0:T(8,128)(2,1)} custom-call(s32[16]{0:T(128)} %pos_any.3, s32[16]{0:T(128)} %doc_any.3, bf16[16,128]{1,0:T(8,128)(2,1)} %k_any.1, bf16[16,128]{1,0:T(8,128)(2,1)} %v_any.1), custom_call_target="tpu_custom_call" | custom-call | tf_op jit(solution)/shard_map/pallas_call | solution.py:252
  2.2 16.0 %all-to-all-start = ((bf16[32,40,128]{2,1,0:T(8,128)(2,1)}), bf16[32,40,128]{2,1,0:T(8,128)(2,1)S(1)}, u32[]{:S(2)}, u32[]{:S(2)}) async-start(bf16[32,40,128]{2,1,0:T(8,128)(2,1)} %shard_map.86), calls=%async_computation | async-start | bytes 655360 | tf_op jit(solution)/shard_map/all_to_all | solution.py:248
  18.2 1.7 %shard_map.85 = bf16[8,264,128]{2,1,0:T(8,128)(2,1)} custom-call(s32[16]{0:T(128)} %pos_any.3, s32[16]{0:T(128)} %doc_any.3, bf16[16,1024]{1,0:T(8,128)(2,1)} %q_any.1, bf16[16,1024]{1,0:T(8,128)(2,1)} %g_any.1), custom_call_target="tpu_custom_call" | custom-call | flops 1000000000 | tf_op jit(solution)/shard_map/pallas_call | solution.py:252
  19.8 13.8 %all-to-all-done = bf16[32,40,128]{2,1,0:T(8,128)(2,1)S(1)} async-done(((bf16[32,40,128]{2,1,0:T(8,128)(2,1)}), bf16[32,40,128]{2,1,0:T(8,128)(2,1)S(1)}, u32[]{:S(2)}, u32[]{:S(2)}) %all-to-all-start) | async-done | bytes 327712 | tf_op jit(solution)/shard_map/all_to_all | solution.py:248
  33.7 4.8 %all-to-all-start.1 = ((bf16[8,264,128]{2,1,0:T(8,128)(2,1)}), bf16[8,264,128]{2,1,0:T(8,128)(2,1)S(1)}, u32[]{:S(2)}, u32[]{:S(2)}) async-start(bf16[8,264,128]{2,1,0:T(8,128)(2,1)} %shard_map.85), calls=%async_computation.1 | async-start | bytes 1081344 | tf_op jit(solution)/shard_map/all_to_all | solution.py:248
  38.5 2.3 %all-gather = bf16[64,40,128]{2,1,0:T(8,128)(2,1)S(1)} all-gather(bf16[32,40,128]{2,1,0:T(8,128)(2,1)S(1)} %all-to-all-done), channel_id=2, replica_groups=mesh['head'=8,'far'=32,'core'=2] {'core'}, dimensions={0}, use_global_device_ids=true | all-gather | bytes 983040 | tf_op jit(solution)/shard_map/all_gather | solution.py:269
  40.7 4.6 %all-to-all-done.1.qp_ref = bf16[8,264,128]{2,1,0:T(8,128)(2,1)S(1)} async-done(((bf16[8,264,128]{2,1,0:T(8,128)(2,1)}), bf16[8,264,128]{2,1,0:T(8,128)(2,1)S(1)}, u32[]{:S(2)}, u32[]{:S(2)}) %all-to-all-start.1) | async-done | bytes 540704 | tf_op jit(solution)/shard_map/all_to_all | solution.py:248
  45.4 2.4 %shard_map.87 = (f32[8,16,128]{2,1,0:T(8,128)S(1)}, f32[1024,1024]{1,0:T(8,128)S(1)}, f32[1024,1024]{1,0:T(8,128)S(1)}, f32[4,1024]{1,0:T(4,128)S(1)}) custom-call(s32[1]{0:T(128)} %bitcast.side_ref, bf16[8,264,128]{2,1,0:T(8,128)(2,1)S(1)} %all-to-all-done.1.qp_ref, bf16[2,32,40,128]{3,2,1,0:T(8,128)(2,1)S(1)} %bitcast.2), custom_call_target="tpu_custom_call" | custom-call | tf_op jit(solution)/shard_map/pallas_call | solution.py:272
  47.8 9.3 %all_to_all.25.st_ref = f32[8,16,128]{2,1,0:T(8,128)S(1)} all-to-all(f32[8,16,128]{2,1,0:T(8,128)S(1)} %get-tuple-element.18), channel_id=1, replica_groups=mesh['head'=8,'far'=32,'core'=2] {'head'}, dimensions={0} | all-to-all | bytes 131072 | tf_op jit(solution)/shard_map/all_to_all | solution.py:248
  57.1 2.4 %shard_map.88 = (bf16[8,128,128]{2,1,0:T(8,128)(2,1)}, f32[32,32,128]{2,1,0:T(8,128)S(1)}, bf16[32,32,128]{2,1,0:T(8,128)(2,1)S(1)}) custom-call(s32[1]{0:T(128)} %bitcast.side_ref, bf16[8,264,128]{2,1,0:T(8,128)(2,1)S(1)} %all-to-all-done.1.qp_ref, bf16[2,32,40,128]{3,2,1,0:T(8,128)(2,1)S(1)} %bitcast.3, f32[8,16,128]{2,1,0:T(8,128)S(1)} %all_to_all.25.st_ref, ...), custom_call_target="tpu_custom_call" | custom-call | tf_op jit(solution)/shard_map/pallas_call | solution.py:279
  59.5 4.8 %all-to-all-start.3 = ((bf16[8,128,128]{2,1,0:T(8,128)(2,1)}), bf16[8,128,128]{2,1,0:T(8,128)(2,1)S(1)}, u32[]{:S(2)}, u32[]{:S(2)}) async-start(bf16[8,128,128]{2,1,0:T(8,128)(2,1)} %get-tuple-element.24), calls=%async_computation.3 | async-start | bytes 524288 | tf_op jit(solution)/shard_map/all_to_all | solution.py:248
  64.3 2.2 %all-gather.1 = bf16[64,32,128]{2,1,0:T(8,128)(2,1)S(1)} all-gather(bf16[32,32,128]{2,1,0:T(8,128)(2,1)S(1)} %get-tuple-element.23), channel_id=3, replica_groups=mesh['head'=8,'far'=32,'core'=2] {'core'}, dimensions={0}, use_global_device_ids=true | all-gather | bytes 786432 | tf_op jit(solution)/shard_map/all_gather | solution.py:287
  66.5 0.8 fusion
  67.3 2.6 %all-to-all-done.3.gq_ref = bf16[8,128,128]{2,1,0:T(8,128)(2,1)S(1)} async-done(((bf16[8,128,128]{2,1,0:T(8,128)(2,1)}), bf16[8,128,128]{2,1,0:T(8,128)(2,1)S(1)}, u32[]{:S(2)}, u32[]{:S(2)}) %all-to-all-start.3) | async-done | bytes 262176 | tf_op jit(solution)/shard_map/all_to_all | solution.py:248
  69.9 6.3 %all-to-all-start.4 = ((bf16[32,32,128]{2,1,0:T(8,128)(2,1)}), bf16[32,32,128]{2,1,0:T(8,128)(2,1)S(1)}, u32[]{:S(2)}, u32[]{:S(2)}) async-start(bf16[32,32,128]{2,1,0:T(8,128)(2,1)} %fusion), calls=%async_computation.4 | async-start | bytes 524288 | tf_op jit(solution)/shard_map/all_to_all | solution.py:248
  76.2 0.7 shard_map.89
  76.9 13.0 %all-to-all-done.4.gkv_ref = bf16[32,32,128]{2,1,0:T(8,128)(2,1)S(1)} async-done(((bf16[32,32,128]{2,1,0:T(8,128)(2,1)}), bf16[32,32,128]{2,1,0:T(8,128)(2,1)S(1)}, u32[]{:S(2)}, u32[]{:S(2)}) %all-to-all-start.4) | async-done | bytes 262176 | tf_op jit(solution)/shard_map/all_to_all | solution.py:248
  89.9 0.7 shard_map.90
Async XLA Ops:
  2.2 31.5 %all-to-all-start = ((bf16[32,40,128]{2,1,0:T(8,128)(2,1)}), bf16[32,40,128]{2,1,0:T(8,128)(2,1)S(1)}, u32[]{:S(2)}, u32[]{:S(2)}) async-start(bf16[32,40,128]{2,1,0:T(8,128)(2,1)} %shard_map.86), calls=%async_computation | async-start | bytes 655360 | tf_op jit(solution)/shard_map/all_to_all | solution.py:248
  33.7 11.7 %all-to-all-start.1 = ((bf16[8,264,128]{2,1,0:T(8,128)(2,1)}), bf16[8,264,128]{2,1,0:T(8,128)(2,1)S(1)}, u32[]{:S(2)}, u32[]{:S(2)}) async-start(bf16[8,264,128]{2,1,0:T(8,128)(2,1)} %shard_map.85), calls=%async_computation.1 | async-start | bytes 1081344 | tf_op jit(solution)/shard_map/all_to_all | solution.py:248
  59.5 10.3 %all-to-all-start.3 = ((bf16[8,128,128]{2,1,0:T(8,128)(2,1)}), bf16[8,128,128]{2,1,0:T(8,128)(2,1)S(1)}, u32[]{:S(2)}, u32[]{:S(2)}) async-start(bf16[8,128,128]{2,1,0:T(8,128)(2,1)} %get-tuple-element.24), calls=%async_computation.3 | async-start | bytes 524288 | tf_op jit(solution)/shard_map/all_to_all | solution.py:248
  69.9 20.0 %all-to-all-start.4 = ((bf16[32,32,128]{2,1,0:T(8,128)(2,1)}), bf16[32,32,128]{2,1,0:T(8,128)(2,1)S(1)}, u32[]{:S(2)}, u32[]{:S(2)}) async-start(bf16[32,32,128]{2,1,0:T(8,128)(2,1)} %fusion), calls=%async_computation.4 | async-start | bytes 524288 | tf_op jit(solution)/shard_map/all_to_all | solution.py:248

commit v13 on v9

--- a/solution.py
+++ b/solution.py
@@ -13,7 +13,7 @@
 FLOOR = -1e29
 DOC_STEP = 8192.0
 META = 8
-CHUNK = 256
+CHUNK = 128
 
 
 def dot_rows(a, b):

time: 90.8 us -> 91 us (level)
  no operation moved by 1% of the time
where the time goes in v13:
time: 91 us; the launch traced here: 90.5 us
  blocking collectives  32.4 us (36%)
  starting transfers between devices  26 us (29%)
  waiting for transfers between devices  22.3 us (25%)
  Pallas kernels  8.91 us (10%)
    all_to_all x2, blocking collectives, swap(): return lax.all_to_all(x, axis, split_axis=0, concat_axis=0, tiled=True)  28 us
    all_to_all x3, starting transfers between devices, swap(): return lax.all_to_all(x, axis, split_axis=0, concat_axis=0, tiled=True)  26 us
    all_to_all x3, waiting for transfers between devices, swap(): return lax.all_to_all(x, axis, split_axis=0, concat_axis=0, tiled=True)  22.3 us
    pallas_call x2, Pallas kernels, pack(): call(kernel, [HBM] * len(args), [pltpu.HBM(shape, bf)], [(pltpu.SMEM if a...  3.22 us
    pallas_call x1, Pallas kernels, on_device(): call(stats_kernel, [SMEM] + [VMEM] * 2, [struct((n_q, 2 * n_q, rows), f32...  2.61 us
    pallas_call x1, Pallas kernels, on_device(): call(grads_kernel, [SMEM] + [VMEM] * 6, [pltpu.HBM((n_q, rows, hd), bf),...  2.39 us
    all_gather x1, blocking collectives, on_device(): kp = lax.all_gather(kp, 'core', axis=0, tiled=False)  2.26 us
    all_gather x1, blocking collectives, on_device(): both = lax.all_gather(give, 'core', axis=0, tiled=False)  2.17 us
  transfers between devices with their start and end apart: 3, of which 3 were waited for; matrix products, arithmetic and copies ran while one was open for 0% of the time, Pallas kernels for 2%

profile of v13, /device:TPU:8, one launch (start us, length us, event | category | flops | bytes accessed | tf_op | source)
XLA Modules:
  0.0 90.5 jit_solution(4076189252729038449)
XLA Ops:
  0.6 1.5 %shard_map.86 = bf16[32,40,128]{2,1,0:T(8,128)(2,1)} custom-call(s32[16]{0:T(128)} %pos_any.3, s32[16]{0:T(128)} %doc_any.3, bf16[16,128]{1,0:T(8,128)(2,1)} %k_any.1, bf16[16,128]{1,0:T(8,128)(2,1)} %v_any.1), custom_call_target="tpu_custom_call" | custom-call | tf_op jit(solution)/shard_map/pallas_call | solution.py:247
  2.2 15.1 %all-to-all-start = ((bf16[32,40,128]{2,1,0:T(8,128)(2,1)}), bf16[32,40,128]{2,1,0:T(8,128)(2,1)S(1)}, u32[]{:S(2)}, u32[]{:S(2)}) async-start(bf16[32,40,128]{2,1,0:T(8,128)(2,1)} %shard_map.86), calls=%async_computation | async-start | bytes 655360 | tf_op jit(solution)/shard_map/all_to_all | solution.py:243
  17.2 1.7 %shard_map.85 = bf16[8,264,128]{2,1,0:T(8,128)(2,1)} custom-call(s32[16]{0:T(128)} %pos_any.3, s32[16]{0:T(128)} %doc_any.3, bf16[16,1024]{1,0:T(8,128)(2,1)} %q_any.1, bf16[16,1024]{1,0:T(8,128)(2,1)} %g_any.1), custom_call_target="tpu_custom_call" | custom-call | flops 1000000000 | tf_op jit(solution)/shard_map/pallas_call | solution.py:247
  19.0 13.1 %all-to-all-done = bf16[32,40,128]{2,1,0:T(8,128)(2,1)S(1)} async-done(((bf16[32,40,128]{2,1,0:T(8,128)(2,1)}), bf16[32,40,128]{2,1,0:T(8,128)(2,1)S(1)}, u32[]{:S(2)}, u32[]{:S(2)}) %all-to-all-start) | async-done | bytes 327712 | tf_op jit(solution)/shard_map/all_to_all | solution.py:243
  32.0 6.4 %all-to-all-start.1 = ((bf16[8,264,128]{2,1,0:T(8,128)(2,1)}), bf16[8,264,128]{2,1,0:T(8,128)(2,1)S(1)}, u32[]{:S(2)}, u32[]{:S(2)}) async-start(bf16[8,264,128]{2,1,0:T(8,128)(2,1)} %shard_map.85), calls=%async_computation.1 | async-start | bytes 1081344 | tf_op jit(solution)/shard_map/all_to_all | solution.py:243
  38.4 2.3 %all-gather = bf16[64,40,128]{2,1,0:T(8,128)(2,1)S(1)} all-gather(bf16[32,40,128]{2,1,0:T(8,128)(2,1)S(1)} %all-to-all-done), channel_id=2, replica_groups=mesh['head'=8,'far'=32,'core'=2] {'core'}, dimensions={0}, use_global_device_ids=true | all-gather | bytes 983040 | tf_op jit(solution)/shard_map/all_gather | solution.py:264
  40.6 5.3 %all-to-all-done.1.qp_ref = bf16[8,264,128]{2,1,0:T(8,128)(2,1)S(1)} async-done(((bf16[8,264,128]{2,1,0:T(8,128)(2,1)}), bf16[8,264,128]{2,1,0:T(8,128)(2,1)S(1)}, u32[]{:S(2)}, u32[]{:S(2)}) %all-to-all-start.1) | async-done | bytes 540704 | tf_op jit(solution)/shard_map/all_to_all | solution.py:243
  46.0 2.6 %shard_map.87 = (f32[8,16,128]{2,1,0:T(8,128)S(1)}, f32[1024,1024]{1,0:T(8,128)S(1)}, f32[1024,1024]{1,0:T(8,128)S(1)}, f32[8,1024]{1,0:T(8,128)S(1)}) custom-call(s32[1]{0:T(128)} %bitcast.side_ref, bf16[8,264,128]{2,1,0:T(8,128)(2,1)S(1)} %all-to-all-done.1.qp_ref, bf16[2,32,40,128]{3,2,1,0:T(8,128)(2,1)S(1)} %bitcast.2), custom_call_target="tpu_custom_call" | custom-call | tf_op jit(solution)/shard_map/pallas_call | solution.py:267
  48.6 8.8 %all_to_all.25.st_ref = f32[8,16,128]{2,1,0:T(8,128)S(1)} all-to-all(f32[8,16,128]{2,1,0:T(8,128)S(1)} %get-tuple-element.16), channel_id=1, replica_groups=mesh['head'=8,'far'=32,'core'=2] {'head'}, dimensions={0} | all-to-all | bytes 131072 | tf_op jit(solution)/shard_map/all_to_all | solution.py:243
  57.4 2.4 %shard_map.88 = (bf16[8,128,128]{2,1,0:T(8,128)(2,1)}, f32[32,32,128]{2,1,0:T(8,128)S(1)}, bf16[32,32,128]{2,1,0:T(8,128)(2,1)S(1)}) custom-call(s32[1]{0:T(128)} %bitcast.side_ref, bf16[8,264,128]{2,1,0:T(8,128)(2,1)S(1)} %all-to-all-done.1.qp_ref, bf16[2,32,40,128]{3,2,1,0:T(8,128)(2,1)S(1)} %bitcast.3, f32[8,16,128]{2,1,0:T(8,128)S(1)} %all_to_all.25.st_ref, ...), custom_call_target="tpu_custom_call" | custom-call | tf_op jit(solution)/shard_map/pallas_call | solution.py:274
  59.8 4.6 %all-to-all-start.3 = ((bf16[8,128,128]{2,1,0:T(8,128)(2,1)}), bf16[8,128,128]{2,1,0:T(8,128)(2,1)S(1)}, u32[]{:S(2)}, u32[]{:S(2)}) async-start(bf16[8,128,128]{2,1,0:T(8,128)(2,1)} %get-tuple-element.22), calls=%async_computation.3 | async-start | bytes 524288 | tf_op jit(solution)/shard_map/all_to_all | solution.py:243
  64.4 2.2 %all-gather.1 = bf16[64,32,128]{2,1,0:T(8,128)(2,1)S(1)} all-gather(bf16[32,32,128]{2,1,0:T(8,128)(2,1)S(1)} %get-tuple-element.21), channel_id=3, replica_groups=mesh['head'=8,'far'=32,'core'=2] {'core'}, dimensions={0}, use_global_device_ids=true | all-gather | bytes 786432 | tf_op jit(solution)/shard_map/all_gather | solution.py:282
  66.6 0.1 fusion
  66.7 3.9 %all-to-all-done.3.gq_ref = bf16[8,128,128]{2,1,0:T(8,128)(2,1)S(1)} async-done(((bf16[8,128,128]{2,1,0:T(8,128)(2,1)}), bf16[8,128,128]{2,1,0:T(8,128)(2,1)S(1)}, u32[]{:S(2)}, u32[]{:S(2)}) %all-to-all-start.3) | async-done | bytes 262176 | tf_op jit(solution)/shard_map/all_to_all | solution.py:243
  70.5 19.2 %all_to_all.26.gkv_ref = bf16[32,32,128]{2,1,0:T(8,128)(2,1)S(1)} all-to-all(bf16[32,32,128]{2,1,0:T(8,128)(2,1)S(1)} %fusion), channel_id=1, replica_groups=mesh['head'=8,'far'=32,'core'=2] {'far'}, dimensions={0} | all-to-all | bytes 524288 | tf_op jit(solution)/shard_map/all_to_all | solution.py:243
  89.8 0.7 shard_map.89
Async XLA Ops:
  2.2 29.9 %all-to-all-start = ((bf16[32,40,128]{2,1,0:T(8,128)(2,1)}), bf16[32,40,128]{2,1,0:T(8,128)(2,1)S(1)}, u32[]{:S(2)}, u32[]{:S(2)}) async-start(bf16[32,40,128]{2,1,0:T(8,128)(2,1)} %shard_map.86), calls=%async_computation | async-start | bytes 655360 | tf_op jit(solution)/shard_map/all_to_all | solution.py:243
  32.0 14.0 %all-to-all-start.1 = ((bf16[8,264,128]{2,1,0:T(8,128)(2,1)}), bf16[8,264,128]{2,1,0:T(8,128)(2,1)S(1)}, u32[]{:S(2)}, u32[]{:S(2)}) async-start(bf16[8,264,128]{2,1,0:T(8,128)(2,1)} %shard_map.85), calls=%async_computation.1 | async-start | bytes 1081344 | tf_op jit(solution)/shard_map/all_to_all | solution.py:243
  59.8 10.8 %all-to-all-start.3 = ((bf16[8,128,128]{2,1,0:T(8,128)(2,1)}), bf16[8,128,128]{2,1,0:T(8,128)(2,1)S(1)}, u32[]{:S(2)}, u32[]{:S(2)}) async-start(bf16[8,128,128]{2,1,0:T(8,128)(2,1)} %get-tuple-element.22), calls=%async_computation.3 | async-start | bytes 524288 | tf_op jit(solution)/shard_map/all_to_all | solution.py:243
